TPU v7x, 32 devices: a whole 2x2x4 slice. The times are simulated.
32 devices in a mesh: shard: 2 (over y), row: 16 (over z, x, core).
Axes of the slice: x: 2, y: 2, z: 4, core: 2. Of those that a mesh axis runs over, the one named last changes fastest.
Arguments:
- documents: bfloat16 [32768, 4096], P(('shard', 'row')), parts along dimension 0, may hold values from -60 to 60
- queries: bfloat16 [128, 4096], P('row'), may hold values from -6 to 6
- precond: bfloat16 [4, 1024, 1024], P(None, 'row'), may hold values from -1 to 3, as said below
Outputs:
- scores: float32 [32768, 128], P(('shard', 'row')), parts along dimension 0
There are 2 independent parts, one for each index of `shard`. A program takes and returns all parts, laid end to end along the dimension named above; an argument that names none is the same for every part. Nothing has to cross between parts.
Inputs may be any that keep to these rules, and one draw needn't show every extreme that they name: Each block precond[b] is symmetric with a positive diagonal.
All inputs are finite; a program needn't handle non-finite values.
Results may differ from a plain program's by a relative error of at most 0.0029.
Values may be sent and summed in bfloat16 or wider, within the bound.
No kernel may reach another device: no remote copies, remote signals or barrier semaphores. Data moves between devices by JAX's collectives and lax.ppermute only.
A program may use at most 64 MiB of HBM per device.

v0:
```python
import jax
import jax.numpy as jnp
from jax import lax
from jax.sharding import PartitionSpec as P


def shards(documents, queries, precond):
    doc_count, width = documents.shape
    panels = precond.shape[0]
    panel_width = precond.shape[2]
    own_count = queries.shape[0]
    own_panels = queries.reshape(own_count, panels, panel_width)
    own_ready = jnp.einsum(
        "qbk,brk->qbr",
        own_panels,
        lax.all_gather(precond, "row", axis=1, tiled=True),
        preferred_element_type=jnp.float32,
    )
    own_ready = own_ready.astype(jnp.bfloat16).reshape(own_count, width)
    raw = jnp.dot(
        documents,
        lax.all_gather(own_ready, "row", axis=0, tiled=True).T,
        preferred_element_type=jnp.float32,
    )
    dense = documents.astype(jnp.float32)
    spread = jnp.sqrt(jnp.mean(dense * dense, axis=1) + 1e-06)
    return raw / (spread[:, None] * jnp.sqrt(jnp.float32(width)))


def solution(mesh):
    placed = (P(("shard", "row"), None), P("row", None), P(None, "row", None))
    return jax.shard_map(
        shards, mesh=mesh, in_specs=placed, out_specs=P(("shard", "row"), None), check_vma=False
    )
```

profile of v0, /device:TPU:0, one launch (start us, length us, event | category | flops | bytes accessed | tf_op | source)
XLA Modules:
  0.0 144.3 jit_solution(13086589602824941877)
XLA Ops:
  6.5 0.0 copy-start
  6.5 0.0 all-gather.3.cloned.1.call-start
  6.5 0.7 all-gather.3.cloned.1.call-update
  7.3 0.0 all-gather.5.cloned.1.call-start
  7.3 79.9 %all-gather.3.cloned.1.call-done = bf16[4,1024,1024]{2,1,0:T(8,128)(2,1)} async-done(((bf16[4,64,1024]{2,1,0:T(8,128)(2,1)}), bf16[4,1024,1024]{2,1,0:T(8,128)(2,1)}) %all-gather.3.cloned.1.call-update) | async-done | bytes 8388624 | tf_op jit(solution)/shard_map/all_gather | solution.py:16
  87.2 0.0 copy-done
  87.2 6.3 %convolution_convert_fusion = bf16[4,1024,8]{1,2,0:T(8,128)(2,1)} fusion(bf16[4,1024,1024]{2,1,0:T(8,128)(2,1)} %all-gather.3.cloned.1.call-done, bf16[8,4,1024]{2,0,1:T(8,128)(2,1)S(1)} %bitcast.10), kind=kOutput, calls=%fused_computation.3 | convolution fusion | flops 67141632 | bytes 8519680 | tf_op jit(solution)/shard_map/qbk,brk->qbr/dot_general | solution.py:13
  93.5 0.0 all-gather.5.cloned.1.call-update
  93.5 5.1 %multiply_reduce_fusion = f32[1024]{0:T(1024)S(1)} fusion(bf16[1024,4096]{1,0:T(8,128)(2,1)} %param.3), kind=kLoop, calls=%fused_computation | loop fusion | flops 12581888 | bytes 8392704 | tf_op jit(solution)/shard_map/reduce_sum | solution.py:26
  98.6 31.3 %all-gather.5.cloned.1.call-done = bf16[128,4096]{1,0:T(8,128)(2,1)} async-done(((bf16[8,4096]{1,0:T(8,128)(2,1)}), bf16[128,4096]{1,0:T(8,128)(2,1)}) %all-gather.5.cloned.1.call-update) | async-done | bytes 1048592 | tf_op jit(solution)/shard_map/all_gather | solution.py:22
  129.8 6.6 %fusion = f32[1024,128]{0,1:T(8,128)S(1)} fusion(bf16[128,4096]{1,0:T(8,128)(2,1)} %all-gather.5.cloned.1.call-done, bf16[1024,4096]{1,0:T(8,128)(2,1)} %param.3, f32[1024]{0:T(1024)S(1)} %sqrt_multiply_fusion), kind=kOutput, calls=%fused_computation.2 | convolution fusion | flops 1073872896 | bytes 9965568 | tf_op jit(solution)/shard_map/dot_general | solution.py:20
  136.5 1.0 copy.4
  (1 shorter events, 0.0 us)
Async XLA Ops:
  6.5 80.7 %copy-start = (bf16[8,4096]{1,0:T(8,128)(2,1)S(1)}, bf16[8,4096]{1,0:T(8,128)(2,1)}, u32[]{:S(2)}) copy-start(bf16[8,4096]{1,0:T(8,128)(2,1)} %param.4) | copy-start | bytes 196612
  6.5 80.7 %all-gather.3.cloned.1.call-start = ((), (), s32[]{:S(2)}) async-start(), calls=%async_computation | async-start | bytes 8912896 | tf_op jit(solution)/shard_map/all_gather | solution.py:16
  7.3 122.6 %all-gather.5.cloned.1.call-start = ((), (), s32[]{:S(2)}) async-start(), calls=%async_computation.1 | async-start | bytes 1114112 | tf_op jit(solution)/shard_map/all_gather | solution.py:22
Sparse Core Ops, SparseCore 0:
  9.5 77.6 all-gather.2
  93.6 36.1 all-gather.4
where the time goes:
time: 145 us; the launch traced here: 144 us
  waiting for transfers between devices  112 us (77%)
  between operations  13.4 us (9%)
  matrix products  12.9 us (9%)
  other arithmetic  5.08 us (4%)
    all_gather x1, waiting for transfers between devices, shards(): lax.all_gather(precond, 'row', axis=1, tiled=True)  79.9 us
    all_gather x1, waiting for transfers between devices, shards(): lax.all_gather(own_ready, 'row', axis=0, tiled=True)  31.3 us
    dot_general x1, matrix products, shards(): jnp.dot(documents, lax.all_gather(own_ready, 'row', axis=0, tiled=True).T...  6.62 us
    dot_general x1, matrix products, shards(): jnp.einsum('qbk,brk->qbr', own_panels, lax.all_gather(precond, 'row', axi...  6.29 us
    reduce_sum x1, other arithmetic, shards(): spread = jnp.sqrt(jnp.mean(dense * dense, axis=1) + 1e-06)  5.07 us
  transfers between devices with their start and end apart: 2, of which 2 were waited for; matrix products, arithmetic and copies ran while one was open for 4% of the time, Pallas kernels for 0%

commit v1 on v0

v1 whole, which is shorter than its diff:
```python
import functools

import jax
import jax.numpy as jnp
from jax import lax
from jax.experimental import pallas as pl
from jax.experimental.pallas import tpu as pltpu
from jax.sharding import PartitionSpec as P

AXES = ("shard", "row")
F32, BF16 = jnp.float32, jnp.bfloat16
VMEM_BYTES = 48 * 1024 * 1024


def place():
    row = lax.axis_index("row")
    return lax.axis_index("shard"), row // 4, (row // 2) % 2, row % 2


def swap(array, dy=0, dz=0, dx=0, dc=0, shear=False, only=None):
    pairs = []
    for y in range(2):
        for z in range(4):
            for x in range(2):
                for c in range(2):
                    sx = x ^ dx ^ (y if shear else 0)
                    source = (y ^ dy) * 16 + (z ^ dz) * 4 + sx * 2 + (c ^ dc)
                    pairs.append((source, y * 16 + z * 4 + x * 2 + c))
    return lax.ppermute(array, AXES, pairs)


def condition_kernel(q0, q1, q2, q3, own, other, out, acc):
    _, z, _, c = place()
    panels, rows, width = own.shape
    for b in range(panels):
        at = slice(b * width, (b + 1) * width)
        asked = jnp.concatenate([q[:, at].astype(F32) for q in (q0, q1, q2, q3)], axis=0)
        block = jnp.concatenate([own[b], other[b]], axis=0)
        got = lax.dot_general(
            asked.astype(BF16), block, (((1,), (1,)), ((), ())), preferred_element_type=F32
        )
        got = pltpu.roll(got, c * rows, axis=1)
        for k in range(4):
            acc[pl.ds(pl.multiple_of((z ^ k) * 8, 8), 8), b * 128 : (b + 1) * 128] = got[
                k * 8 : (k + 1) * 8
            ]
    out[...] = acc[...].astype(BF16)


def score_kernel(order, docs, *refs):
    pieces, (out, held, ready) = refs[: len(order)], refs[len(order) :]
    y, z, x, c = place()
    width = docs.shape[1]

    @pl.when(pl.program_id(0) == 0)
    def _():
        for (dy, dx, dc), piece in zip(order, pieces, strict=True):
            px = x ^ dx
            slot = (px ^ y ^ dy) * 2 + (c ^ dc)
            rows = pl.ds(pl.multiple_of(slot * 32, 32), 32)
            for k in range(4):
                for b in range(4):
                    start = b * (width // 4) + (z ^ k) * 256 + px * 128
                    held[rows, pl.ds(pl.multiple_of(start, 128), 128)] = piece[
                        k, :, b * 128 : (b + 1) * 128
                    ]
        step = 512
        for at in range(0, width, step):
            part = held[:, at : at + step].astype(F32).reshape(4, 4, 8, step)
            part = jnp.concatenate(
                [part[s, k] for k in range(4) for s in range(4)], axis=0
            )
            ready[:, at : at + step] = part.astype(BF16)

    block = docs[...]
    raw = lax.dot_general(
        block, ready[...], (((1,), (1,)), ((), ())), preferred_element_type=F32
    )
    dense = block.astype(F32)
    mean = jnp.sum(dense * dense, axis=1, keepdims=True) * (1.0 / width)
    out[...] = raw * (lax.rsqrt(mean + 1e-06) * (1.0 / width**0.5))


def grouped(documents, queries, precond):
    doc_count, width = documents.shape
    q3 = swap(queries, dz=3, shear=True)
    q2 = swap(queries, dz=2, shear=True)
    q1 = swap(queries, dz=1, shear=True)
    q0 = swap(queries, dz=0, shear=True)
    other = swap(precond, dc=1)
    vmem = pl.BlockSpec(memory_space=pltpu.VMEM)
    piece = pl.pallas_call(
        condition_kernel,
        out_shape=jax.ShapeDtypeStruct((32, 512), BF16),
        in_specs=[vmem] * 6,
        out_specs=vmem,
        scratch_shapes=[pltpu.VMEM((32, 512), F32)],
        compiler_params=pltpu.CompilerParams(vmem_limit_bytes=VMEM_BYTES),
    )(q0, q1, q2, q3, precond, other)
    line = jnp.stack([piece] + [swap(piece, dz=k) for k in (1, 2, 3)])
    order, pieces = [], []
    for dy, dx in ((0, 0), (1, 1), (0, 1), (1, 0)):
        got = swap(line, dy=dy, dx=dx) if dy or dx else line
        order += [(dy, dx, 0), (dy, dx, 1)]
        pieces += [got, swap(got, dc=1)]
    rows = 128
    return pl.pallas_call(
        functools.partial(score_kernel, order),
        grid=(doc_count // rows,),
        out_shape=jax.ShapeDtypeStruct((doc_count, 128), F32),
        in_specs=[pl.BlockSpec((rows, width), lambda i: (i, 0))] + [vmem] * 8,
        out_specs=pl.BlockSpec((rows, 128), lambda i: (i, 0)),
        scratch_shapes=[pltpu.VMEM((128, width), BF16), pltpu.VMEM((128, width), BF16)],
        compiler_params=pltpu.CompilerParams(vmem_limit_bytes=VMEM_BYTES),
    )(documents, *pieces)


def general(documents, queries, precond):
    panels, _, panel_width = precond.shape
    width = documents.shape[1]
    asked = lax.all_gather(queries, "row", axis=0, tiled=True)
    asked = asked.reshape(asked.shape[0], panels, panel_width)
    own = jnp.einsum("qbk,brk->bqr", asked, precond, preferred_element_type=F32).astype(BF16)
    ready = lax.all_gather(own, "row", axis=0)
    ready = ready.transpose(2, 1, 0, 3).reshape(-1, width)
    raw = jnp.dot(documents, ready.T, preferred_element_type=F32)
    dense = documents.astype(F32)
    spread = jnp.sqrt(jnp.mean(dense * dense, axis=1) + 1e-06)
    return raw / (spread[:, None] * jnp.sqrt(F32(width)))


def solution(mesh):
    fits = mesh.shape["shard"] == 2 and mesh.shape["row"] == 16
    placed = (P(AXES, None), P("row", None), P(None, "row", None))
    return jax.shard_map(
        grouped if fits else general,
        mesh=mesh,
        in_specs=placed,
        out_specs=P(AXES, None),
        check_vma=False,
    )
```

time: 145 us -> 45.1 us (0.31)
  waiting for transfers between devices: 112 us -> 17.2 us
  starting transfers between devices: 0.04 us -> 17.3 us
  between operations: 13.4 us -> 0.04 us
  matrix products: 12.9 us -> 0 us
  Pallas kernels: 0 us -> 9.22 us
  other arithmetic: 5.08 us -> 0.02 us
    all_gather x2 -> x0, waiting for transfers between devices: 111 us -> none  [the longest x1 79.9 us: shards(): lax.all_gather(precond, 'row', axis=1, tiled=True)]
    ppermute x0 -> x15, starting transfers between devices: none -> 17.3 us  [swap(): return lax.ppermute(array, AXES, pairs)]
    ppermute x0 -> x15, waiting for transfers between devices: none -> 17.2 us  [swap(): return lax.ppermute(array, AXES, pairs)]
    dot_general x2 -> x0, matrix products: 12.9 us -> none  [the longest x1 6.62 us: shards(): jnp.dot(documents, lax.all_gather(own_ready, 'row', axis=0, tiled=True).T...]
    pallas_call x0 -> x2, Pallas kernels: none -> 9.22 us  [the longest x1 8.69 us: grouped(): pl.pallas_call(functools.partial(score_kernel, order), grid=(doc_count //...]
    reduce_sum x1 -> x0, other arithmetic: 5.07 us -> none  [shards(): spread = jnp.sqrt(jnp.mean(dense * dense, axis=1) + 1e-06)]
  transfers between devices with their start and end apart: 2 -> 15, of which waited for: 2 -> 8; matrix products, arithmetic and copies ran while one was open for 4% -> 0% of each run, Pallas kernels for 0% -> 0%
where the time goes in v1:
time: 45.1 us; the launch traced here: 44.8 us
  starting transfers between devices  17.3 us (38%)
  waiting for transfers between devices  17.2 us (38%)
  Pallas kernels  9.22 us (20%)
  local copies, waits for them, and re-layouts  1.04 us (2%)
    ppermute x15, starting transfers between devices, swap(): return lax.ppermute(array, AXES, pairs)  17.3 us
    ppermute x15, waiting for transfers between devices, swap(): return lax.ppermute(array, AXES, pairs)  17.2 us
    pallas_call x1, Pallas kernels, grouped(): pl.pallas_call(functools.partial(score_kernel, order), grid=(doc_count //...  8.69 us
    unnamed x2, local copies, waits for them, and re-layouts  1.04 us
  transfers between devices with their start and end apart: 15, of which 8 were waited for; matrix products, arithmetic and copies ran while one was open for 0% of the time, Pallas kernels for 0%

profile of v1, /device:TPU:0, one launch (start us, length us, event | category | flops | bytes accessed | tf_op | source)
XLA Modules:
  0.0 44.8 jit_solution(14914167393496717426)
XLA Ops:
  0.0 0.5 %collective-permute-start.4 = (bf16[4,64,1024]{2,1,0:T(8,128)(2,1)}, bf16[4,64,1024]{2,1,0:T(8,128)(2,1)S(1)}, u32[]{:S(2)}, u32[]{:S(2)}) collective-permute-start(bf16[4,64,1024]{2,1,0:T(8,128)(2,1)} %own.1), channel_id=1, source_target_pairs={{1,0},{0,1},{3,2},{2,3},{5,4},{4,5},{7,6},{6,7},{9,8},{8,9},{11,10... | collective-permute-start | bytes 1572872 | tf_op jit(solution)/shard_map/ppermute | solution.py:29
  0.5 2.6 %collective-permute-start.1 = (bf16[8,4096]{1,0:T(8,128)(2,1)}, bf16[8,4096]{1,0:T(8,128)(2,1)S(1)}, u32[]{:S(2)}, u32[]{:S(2)}) collective-permute-start(bf16[8,4096]{1,0:T(8,128)(2,1)} %param.4), channel_id=1, source_target_pairs={{4,0},{5,1},{6,2},{7,3},{0,4},{1,5},{2,6},{3,7},{12,8},{13,9},{14,... | collective-permute-start | bytes 196616 | tf_op jit(solution)/shard_map/ppermute | solution.py:29
  3.0 1.5 %collective-permute-start = (bf16[8,4096]{1,0:T(8,128)(2,1)}, bf16[8,4096]{1,0:T(8,128)(2,1)S(1)}, u32[]{:S(2)}, u32[]{:S(2)}) collective-permute-start(bf16[8,4096]{1,0:T(8,128)(2,1)} %param.4), channel_id=1, source_target_pairs={{0,0},{1,1},{2,2},{3,3},{4,4},{5,5},{6,6},{7,7},{8,8},{9,9},{10,10... | collective-permute-start | bytes 196616 | tf_op jit(solution)/shard_map/ppermute | solution.py:29
  4.5 2.5 %collective-permute-start.3 = (bf16[8,4096]{1,0:T(8,128)(2,1)}, bf16[8,4096]{1,0:T(8,128)(2,1)S(1)}, u32[]{:S(2)}, u32[]{:S(2)}) collective-permute-start(bf16[8,4096]{1,0:T(8,128)(2,1)} %param.4), channel_id=1, source_target_pairs={{12,0},{13,1},{14,2},{15,3},{8,4},{9,5},{10,6},{11,7},{4,8},{5,9},... | collective-permute-start | bytes 196616 | tf_op jit(solution)/shard_map/ppermute | solution.py:29
  7.0 0.1 collective-permute-start.2
  7.1 0.0 collective-permute-done.1.q1
  7.1 0.0 collective-permute-done.q0
  7.1 3.8 %collective-permute-done.3.q3 = bf16[8,4096]{1,0:T(8,128)(2,1)S(1)} collective-permute-done((bf16[8,4096]{1,0:T(8,128)(2,1)}, bf16[8,4096]{1,0:T(8,128)(2,1)S(1)}, u32[]{:S(2)}, u32[]{:S(2)}) %collective-permute-start.3) | collective-permute-done | bytes 65568 | tf_op jit(solution)/shard_map/ppermute | solution.py:29
  10.9 3.1 %collective-permute-done.2.q2 = bf16[8,4096]{1,0:T(8,128)(2,1)S(1)} collective-permute-done((bf16[8,4096]{1,0:T(8,128)(2,1)}, bf16[8,4096]{1,0:T(8,128)(2,1)S(1)}, u32[]{:S(2)}, u32[]{:S(2)}) %collective-permute-start.2) | collective-permute-done | bytes 65568 | tf_op jit(solution)/shard_map/ppermute | solution.py:29
  14.0 0.0 collective-permute-done.4.other
  14.0 0.0 copy-start
  14.0 1.0 %copy-done = bf16[4,64,1024]{2,1,0:T(8,128)(2,1)S(1)} copy-done((bf16[4,64,1024]{2,1,0:T(8,128)(2,1)S(1)}, bf16[4,64,1024]{2,1,0:T(8,128)(2,1)}, u32[]{:S(2)}) %copy-start) | copy-done | bytes 524312
  15.1 0.5 %shard_map.37 = bf16[32,512]{1,0:T(8,128)(2,1)S(1)} custom-call(bf16[8,4096]{1,0:T(8,128)(2,1)S(1)} %collective-permute-done.q0, bf16[8,4096]{1,0:T(8,128)(2,1)S(1)} %collective-permute-done.1.q1, bf16[8,4096]{1,0:T(8,128)(2,1)S(1)} %collective-permute-done.2.q2, bf16[8,4096]{1,0:T(8,128)(2,1)S(1)} %collective-permute-done.3.q3, ...), custom_call_target="tpu_custom_call" | custom-call | tf_op jit(solution)/shard_map/pallas_call | solution.py:92
  15.6 2.7 %collective-permute-start.7 = (bf16[32,512]{1,0:T(8,128)(2,1)S(1)}, bf16[32,512]{1,0:T(8,128)(2,1)S(1)}, u32[]{:S(2)}, u32[]{:S(2)}) collective-permute-start(bf16[32,512]{1,0:T(8,128)(2,1)S(1)} %shard_map.37), channel_id=1, source_target_pairs={{12,0},{13,1},{14,2},{15,3},{8,4},{9,5},{10,6},{11,7},{4,8},{5,9},... | collective-permute-start | bytes 98312 | tf_op jit(solution)/shard_map/ppermute | solution.py:29
  18.3 0.0 collective-permute-start.6
  18.3 1.7 %collective-permute-start.5 = (bf16[32,512]{1,0:T(8,128)(2,1)S(1)}, bf16[32,512]{1,0:T(8,128)(2,1)S(1)}, u32[]{:S(2)}, u32[]{:S(2)}) collective-permute-start(bf16[32,512]{1,0:T(8,128)(2,1)S(1)} %shard_map.37), channel_id=1, source_target_pairs={{4,0},{5,1},{6,2},{7,3},{0,4},{1,5},{2,6},{3,7},{12,8},{13,9},{14,... | collective-permute-start | bytes 98312 | tf_op jit(solution)/shard_map/ppermute | solution.py:29
  20.0 1.4 %collective-permute-done.7 = bf16[32,512]{1,0:T(8,128)(2,1)S(1)} collective-permute-done((bf16[32,512]{1,0:T(8,128)(2,1)S(1)}, bf16[32,512]{1,0:T(8,128)(2,1)S(1)}, u32[]{:S(2)}, u32[]{:S(2)}) %collective-permute-start.7) | collective-permute-done | bytes 32800 | tf_op jit(solution)/shard_map/ppermute | solution.py:29
  21.4 1.8 %collective-permute-done.6 = bf16[32,512]{1,0:T(8,128)(2,1)S(1)} collective-permute-done((bf16[32,512]{1,0:T(8,128)(2,1)S(1)}, bf16[32,512]{1,0:T(8,128)(2,1)S(1)}, u32[]{:S(2)}, u32[]{:S(2)}) %collective-permute-start.6) | collective-permute-done | bytes 32800 | tf_op jit(solution)/shard_map/ppermute | solution.py:29
  23.2 0.0 collective-permute-done.5
  23.2 4.2 %collective-permute-start.13 = (bf16[4,32,512]{2,1,0:T(8,128)(2,1)S(1)}, bf16[4,32,512]{2,1,0:T(8,128)(2,1)S(1)}, u32[]{:S(2)}, u32[]{:S(2)}) collective-permute-start(bf16[4,32,512]{2,1,0:T(8,128)(2,1)S(1)} %pad_maximum_fusion.refs_0_), channel_id=1, source_target_pairs={{16,0},{17,1},{18,2},{19,3},{20,4},{21,5},{22,6},{23,7},{24,8},{25... | collective-permute-start | bytes 393224 | tf_op jit(solution)/shard_map/ppermute | solution.py:29
  27.4 1.5 %collective-permute-start.11 = (bf16[4,32,512]{2,1,0:T(8,128)(2,1)S(1)}, bf16[4,32,512]{2,1,0:T(8,128)(2,1)S(1)}, u32[]{:S(2)}, u32[]{:S(2)}) collective-permute-start(bf16[4,32,512]{2,1,0:T(8,128)(2,1)S(1)} %pad_maximum_fusion.refs_0_), channel_id=1, source_target_pairs={{2,0},{3,1},{0,2},{1,3},{6,4},{7,5},{4,6},{5,7},{10,8},{11,9},{8,1... | collective-permute-start | bytes 393224 | tf_op jit(solution)/shard_map/ppermute | solution.py:29
  28.9 0.1 collective-permute-start.9
  28.9 0.0 collective-permute-start.8
  28.9 2.3 %collective-permute-done.13.refs_6_ = bf16[4,32,512]{2,1,0:T(8,128)(2,1)S(1)} collective-permute-done((bf16[4,32,512]{2,1,0:T(8,128)(2,1)S(1)}, bf16[4,32,512]{2,1,0:T(8,128)(2,1)S(1)}, u32[]{:S(2)}, u32[]{:S(2)}) %collective-permute-start.13) | collective-permute-done | bytes 131104 | tf_op jit(solution)/shard_map/ppermute | solution.py:29
  31.2 0.0 collective-permute-start.14
  31.3 1.1 %collective-permute-done.11.refs_4_ = bf16[4,32,512]{2,1,0:T(8,128)(2,1)S(1)} collective-permute-done((bf16[4,32,512]{2,1,0:T(8,128)(2,1)S(1)}, bf16[4,32,512]{2,1,0:T(8,128)(2,1)S(1)}, u32[]{:S(2)}, u32[]{:S(2)}) %collective-permute-start.11) | collective-permute-done | bytes 131104 | tf_op jit(solution)/shard_map/ppermute | solution.py:29
  32.3 0.0 collective-permute-start.12
  32.3 2.4 %collective-permute-done.9.refs_2_ = bf16[4,32,512]{2,1,0:T(8,128)(2,1)S(1)} collective-permute-done((bf16[4,32,512]{2,1,0:T(8,128)(2,1)S(1)}, bf16[4,32,512]{2,1,0:T(8,128)(2,1)S(1)}, u32[]{:S(2)}, u32[]{:S(2)}) %collective-permute-start.9) | collective-permute-done | bytes 131104 | tf_op jit(solution)/shard_map/ppermute | solution.py:29
  34.7 0.0 collective-permute-start.10
  34.7 0.0 collective-permute-done.8.refs_1_
  34.7 0.0 collective-permute-done.14.refs_7_
  34.7 0.0 collective-permute-done.12.refs_5_
  34.8 1.3 %collective-permute-done.10.refs_3_ = bf16[4,32,512]{2,1,0:T(8,128)(2,1)S(1)} collective-permute-done((bf16[4,32,512]{2,1,0:T(8,128)(2,1)S(1)}, bf16[4,32,512]{2,1,0:T(8,128)(2,1)S(1)}, u32[]{:S(2)}, u32[]{:S(2)}) %collective-permute-start.10) | collective-permute-done | bytes 131104 | tf_op jit(solution)/shard_map/ppermute | solution.py:29
  36.1 8.7 %shard_map.38 = f32[1024,128]{1,0:T(8,128)} custom-call(bf16[1024,4096]{1,0:T(8,128)(2,1)} %docs.1, bf16[4,32,512]{2,1,0:T(8,128)(2,1)S(1)} %pad_maximum_fusion.refs_0_, bf16[4,32,512]{2,1,0:T(8,128)(2,1)S(1)} %collective-permute-done.8.refs_1_, bf16[4,32,512]{2,1,0:T(8,128)(2,1)S(1)} %collective-permute-done.9.refs_2_, ...), custom_call_target="tpu_custom_call" | custom-call | tf_op jit(solution)/shard_map/pallas_call | solution.py:107
  (1 shorter events, 0.0 us)
Async XLA Ops:
  0.0 14.0 %collective-permute-start.4 = (bf16[4,64,1024]{2,1,0:T(8,128)(2,1)}, bf16[4,64,1024]{2,1,0:T(8,128)(2,1)S(1)}, u32[]{:S(2)}, u32[]{:S(2)}) collective-permute-start(bf16[4,64,1024]{2,1,0:T(8,128)(2,1)} %own.1), channel_id=1, source_target_pairs={{1,0},{0,1},{3,2},{2,3},{5,4},{4,5},{7,6},{6,7},{9,8},{8,9},{11,10... | collective-permute-start | bytes 1572872 | tf_op jit(solution)/shard_map/ppermute | solution.py:29
  0.5 6.7 %collective-permute-start.1 = (bf16[8,4096]{1,0:T(8,128)(2,1)}, bf16[8,4096]{1,0:T(8,128)(2,1)S(1)}, u32[]{:S(2)}, u32[]{:S(2)}) collective-permute-start(bf16[8,4096]{1,0:T(8,128)(2,1)} %param.4), channel_id=1, source_target_pairs={{4,0},{5,1},{6,2},{7,3},{0,4},{1,5},{2,6},{3,7},{12,8},{13,9},{14,... | collective-permute-start | bytes 196616 | tf_op jit(solution)/shard_map/ppermute | solution.py:29
  3.0 4.1 %collective-permute-start = (bf16[8,4096]{1,0:T(8,128)(2,1)}, bf16[8,4096]{1,0:T(8,128)(2,1)S(1)}, u32[]{:S(2)}, u32[]{:S(2)}) collective-permute-start(bf16[8,4096]{1,0:T(8,128)(2,1)} %param.4), channel_id=1, source_target_pairs={{0,0},{1,1},{2,2},{3,3},{4,4},{5,5},{6,6},{7,7},{8,8},{9,9},{10,10... | collective-permute-start | bytes 196616 | tf_op jit(solution)/shard_map/ppermute | solution.py:29
  4.5 6.4 %collective-permute-start.3 = (bf16[8,4096]{1,0:T(8,128)(2,1)}, bf16[8,4096]{1,0:T(8,128)(2,1)S(1)}, u32[]{:S(2)}, u32[]{:S(2)}) collective-permute-start(bf16[8,4096]{1,0:T(8,128)(2,1)} %param.4), channel_id=1, source_target_pairs={{12,0},{13,1},{14,2},{15,3},{8,4},{9,5},{10,6},{11,7},{4,8},{5,9},... | collective-permute-start | bytes 196616 | tf_op jit(solution)/shard_map/ppermute | solution.py:29
  7.0 7.0 %collective-permute-start.2 = (bf16[8,4096]{1,0:T(8,128)(2,1)}, bf16[8,4096]{1,0:T(8,128)(2,1)S(1)}, u32[]{:S(2)}, u32[]{:S(2)}) collective-permute-start(bf16[8,4096]{1,0:T(8,128)(2,1)} %param.4), channel_id=1, source_target_pairs={{8,0},{9,1},{10,2},{11,3},{12,4},{13,5},{14,6},{15,7},{0,8},{1,9},... | collective-permute-start | bytes 196616 | tf_op jit(solution)/shard_map/ppermute | solution.py:29
  14.0 1.0 %copy-start = (bf16[4,64,1024]{2,1,0:T(8,128)(2,1)S(1)}, bf16[4,64,1024]{2,1,0:T(8,128)(2,1)}, u32[]{:S(2)}) copy-start(bf16[4,64,1024]{2,1,0:T(8,128)(2,1)} %own.1) | copy-start | bytes 1572868
  15.6 5.8 %collective-permute-start.7 = (bf16[32,512]{1,0:T(8,128)(2,1)S(1)}, bf16[32,512]{1,0:T(8,128)(2,1)S(1)}, u32[]{:S(2)}, u32[]{:S(2)}) collective-permute-start(bf16[32,512]{1,0:T(8,128)(2,1)S(1)} %shard_map.37), channel_id=1, source_target_pairs={{12,0},{13,1},{14,2},{15,3},{8,4},{9,5},{10,6},{11,7},{4,8},{5,9},... | collective-permute-start | bytes 98312 | tf_op jit(solution)/shard_map/ppermute | solution.py:29
  18.3 4.8 %collective-permute-start.6 = (bf16[32,512]{1,0:T(8,128)(2,1)S(1)}, bf16[32,512]{1,0:T(8,128)(2,1)S(1)}, u32[]{:S(2)}, u32[]{:S(2)}) collective-permute-start(bf16[32,512]{1,0:T(8,128)(2,1)S(1)} %shard_map.37), channel_id=1, source_target_pairs={{8,0},{9,1},{10,2},{11,3},{12,4},{13,5},{14,6},{15,7},{0,8},{1,9},... | collective-permute-start | bytes 98312 | tf_op jit(solution)/shard_map/ppermute | solution.py:29
  18.3 4.8 %collective-permute-start.5 = (bf16[32,512]{1,0:T(8,128)(2,1)S(1)}, bf16[32,512]{1,0:T(8,128)(2,1)S(1)}, u32[]{:S(2)}, u32[]{:S(2)}) collective-permute-start(bf16[32,512]{1,0:T(8,128)(2,1)S(1)} %shard_map.37), channel_id=1, source_target_pairs={{4,0},{5,1},{6,2},{7,3},{0,4},{1,5},{2,6},{3,7},{12,8},{13,9},{14,... | collective-permute-start | bytes 98312 | tf_op jit(solution)/shard_map/ppermute | solution.py:29
  23.2 8.1 %collective-permute-start.13 = (bf16[4,32,512]{2,1,0:T(8,128)(2,1)S(1)}, bf16[4,32,512]{2,1,0:T(8,128)(2,1)S(1)}, u32[]{:S(2)}, u32[]{:S(2)}) collective-permute-start(bf16[4,32,512]{2,1,0:T(8,128)(2,1)S(1)} %pad_maximum_fusion.refs_0_), channel_id=1, source_target_pairs={{16,0},{17,1},{18,2},{19,3},{20,4},{21,5},{22,6},{23,7},{24,8},{25... | collective-permute-start | bytes 393224 | tf_op jit(solution)/shard_map/ppermute | solution.py:29
  27.4 5.0 %collective-permute-start.11 = (bf16[4,32,512]{2,1,0:T(8,128)(2,1)S(1)}, bf16[4,32,512]{2,1,0:T(8,128)(2,1)S(1)}, u32[]{:S(2)}, u32[]{:S(2)}) collective-permute-start(bf16[4,32,512]{2,1,0:T(8,128)(2,1)S(1)} %pad_maximum_fusion.refs_0_), channel_id=1, source_target_pairs={{2,0},{3,1},{0,2},{1,3},{6,4},{7,5},{4,6},{5,7},{10,8},{11,9},{8,1... | collective-permute-start | bytes 393224 | tf_op jit(solution)/shard_map/ppermute | solution.py:29
  28.9 5.9 %collective-permute-start.9 = (bf16[4,32,512]{2,1,0:T(8,128)(2,1)S(1)}, bf16[4,32,512]{2,1,0:T(8,128)(2,1)S(1)}, u32[]{:S(2)}, u32[]{:S(2)}) collective-permute-start(bf16[4,32,512]{2,1,0:T(8,128)(2,1)S(1)} %pad_maximum_fusion.refs_0_), channel_id=1, source_target_pairs={{18,0},{19,1},{16,2},{17,3},{22,4},{23,5},{20,6},{21,7},{26,8},{27... | collective-permute-start | bytes 393224 | tf_op jit(solution)/shard_map/ppermute | solution.py:29
  28.9 5.8 %collective-permute-start.8 = (bf16[4,32,512]{2,1,0:T(8,128)(2,1)S(1)}, bf16[4,32,512]{2,1,0:T(8,128)(2,1)S(1)}, u32[]{:S(2)}, u32[]{:S(2)}) collective-permute-start(bf16[4,32,512]{2,1,0:T(8,128)(2,1)S(1)} %pad_maximum_fusion.refs_0_), channel_id=1, source_target_pairs={{1,0},{0,1},{3,2},{2,3},{5,4},{4,5},{7,6},{6,7},{9,8},{8,9},{11,10... | collective-permute-start | bytes 393224 | tf_op jit(solution)/shard_map/ppermute | solution.py:29
  31.2 3.5 %collective-permute-start.14 = (bf16[4,32,512]{2,1,0:T(8,128)(2,1)S(1)}, bf16[4,32,512]{2,1,0:T(8,128)(2,1)S(1)}, u32[]{:S(2)}, u32[]{:S(2)}) collective-permute-start(bf16[4,32,512]{2,1,0:T(8,128)(2,1)S(1)} %collective-permute-done.13.refs_6_), channel_id=1, source_target_pairs={{1,0},{0,1},{3,2},{2,3},{5,4},{4,5},{7,6},{6,7},{9,8},{8,9},{11,10... | collective-permute-start | bytes 393224 | tf_op jit(solution)/shard_map/ppermute | solution.py:29
  32.3 2.4 %collective-permute-start.12 = (bf16[4,32,512]{2,1,0:T(8,128)(2,1)S(1)}, bf16[4,32,512]{2,1,0:T(8,128)(2,1)S(1)}, u32[]{:S(2)}, u32[]{:S(2)}) collective-permute-start(bf16[4,32,512]{2,1,0:T(8,128)(2,1)S(1)} %collective-permute-done.11.refs_4_), channel_id=1, source_target_pairs={{1,0},{0,1},{3,2},{2,3},{5,4},{4,5},{7,6},{6,7},{9,8},{8,9},{11,10... | collective-permute-start | bytes 393224 | tf_op jit(solution)/shard_map/ppermute | solution.py:29
  34.7 1.3 %collective-permute-start.10 = (bf16[4,32,512]{2,1,0:T(8,128)(2,1)S(1)}, bf16[4,32,512]{2,1,0:T(8,128)(2,1)S(1)}, u32[]{:S(2)}, u32[]{:S(2)}) collective-permute-start(bf16[4,32,512]{2,1,0:T(8,128)(2,1)S(1)} %collective-permute-done.9.refs_2_), channel_id=1, source_target_pairs={{1,0},{0,1},{3,2},{2,3},{5,4},{4,5},{7,6},{6,7},{9,8},{8,9},{11,10... | collective-permute-start | bytes 393224 | tf_op jit(solution)/shard_map/ppermute | solution.py:29

commit v2 on v0

v2 whole, which is shorter than its diff:
```python
import jax
import jax.numpy as jnp
from jax import lax
from jax.experimental import pallas as pl
from jax.experimental.pallas import tpu as pltpu
from jax.sharding import PartitionSpec as P

AXES = ("shard", "row")
F32, BF16 = jnp.float32, jnp.bfloat16


def place():
    row = lax.axis_index("row")
    return lax.axis_index("shard"), row // 4, (row // 2) % 2, row % 2


def moved(array, source_of):
    pairs = []
    for index in range(32):
        here = (index // 16, index // 4 % 4, index // 2 % 2, index % 2)
        y, z, x, c = source_of(*here)
        pairs.append((y * 16 + z * 4 + x * 2 + c, index))
    return lax.ppermute(array, AXES, pairs)


def over_core(array):
    return moved(array, lambda y, z, x, c: (y, z, x, c ^ 1))


def condition_kernel(q0, q1, q2, q3, own, other, out, acc):
    _, z, _, c = place()
    panels, rows, width = own.shape
    for b in range(panels):
        at = slice(b * width, (b + 1) * width)
        asked = jnp.concatenate([q[:, at].astype(F32) for q in (q0, q1, q2, q3)], axis=0)
        block = jnp.concatenate([own[b], other[b]], axis=0)
        got = lax.dot_general(
            asked.astype(BF16), block, (((1,), (1,)), ((), ())), preferred_element_type=F32
        )
        got = pltpu.roll(got, c * rows, axis=1)
        for k in range(4):
            acc[pl.ds(pl.multiple_of((z ^ k) * 8, 8), 8), b * 128 : (b + 1) * 128] = got[
                k * 8 : (k + 1) * 8
            ]
    out[...] = acc[...].astype(BF16)


def norm_kernel(docs, own, after, kept, scale, own_kept, sems):
    count, width = docs.shape
    parts = 8
    rows = count // parts
    copies = [
        pltpu.make_async_copy(
            docs.at[pl.ds(i * rows, rows)], kept.at[pl.ds(i * rows, rows)], sems.at[i]
        )
        for i in range(parts)
    ]
    last = pltpu.make_async_copy(own, own_kept, sems.at[parts])
    for copy in copies:
        copy.start()
    last.start()
    for i, copy in enumerate(copies):
        copy.wait()
        total = jnp.zeros((rows, 128), F32)
        for at in range(0, width, 128):
            dense = kept[i * rows : (i + 1) * rows, at : at + 128].astype(F32)
            total += dense * dense
        mean = jnp.sum(total, axis=1, keepdims=True) * (1.0 / width)
        value = lax.rsqrt(mean + 1e-06) * (1.0 / width**0.5)
        scale[i * rows : (i + 1) * rows] = jnp.broadcast_to(value, (rows, 128))
    last.wait()


def assemble(pieces, held, ready, z):
    for slot, piece in pieces:
        rows = pl.ds(pl.multiple_of(slot * 32, 32), 32)
        for k in range(4):
            for b in range(4):
                start = b * 512 + (z ^ k) * 128
                held[rows, pl.ds(pl.multiple_of(start, 128), 128)] = piece[
                    k, :, b * 128 : (b + 1) * 128
                ]
    width = held.shape[1]
    step = 512
    for at in range(0, width, step):
        part = held[:, at : at + step].astype(F32).reshape(4, 4, 8, step)
        part = jnp.concatenate([part[s, k] for k in range(4) for s in range(4)], axis=0)
        ready[:, at : at + step] = part.astype(BF16)


def columns(docs, at, rows, side):
    parts = []
    for block in range(16):
        start = pl.multiple_of(block * 256 + side * 128, 128)
        parts.append(docs[pl.ds(at, rows), pl.ds(start, 128)])
    return jnp.concatenate(parts, axis=1)


def times(left, right):
    return lax.dot_general(left, right, (((1,), (1,)), ((), ())), preferred_element_type=F32)


def near_kernel(docs, line, line_c, first, second, first_c, second_c, out, held, ready):
    y, z, x, c = place()
    s = x ^ y

    def fill(own, across, own_c, across_c):
        assemble(
            [
                (s * 2 + c, own),
                ((1 - s) * 2 + c, across),
                (s * 2 + 1 - c, own_c),
                ((1 - s) * 2 + 1 - c, across_c),
            ],
            held,
            ready,
            z,
        )

    @pl.when(c == 0)
    def _():
        fill(line, second, line_c, first_c)

    @pl.when(c == 1)
    def _():
        fill(line, first, line_c, second_c)

    rows = 256
    for at in range(0, docs.shape[0], rows):
        out[at : at + rows] = times(columns(docs, at, rows, x), ready[...])


def far_kernel(
    docs, scale, near, third, first, second, third_c, first_c, second_c, out, held, ready, made, sems
):
    y, z, x, c = place()
    s = x ^ y

    def fill(diagonal, beside, diagonal_c, beside_c):
        assemble(
            [
                (s * 2 + c, diagonal),
                ((1 - s) * 2 + c, beside),
                (s * 2 + 1 - c, diagonal_c),
                ((1 - s) * 2 + 1 - c, beside_c),
            ],
            held,
            ready,
            z,
        )

    @pl.when(c == 0)
    def _():
        fill(third, first, third_c, second_c)

    @pl.when(c == 1)
    def _():
        fill(third, second, third_c, first_c)

    rows = 256
    copies = []
    for i, at in enumerate(range(0, docs.shape[0], rows)):
        got = times(columns(docs, at, rows, 1 - x), ready[...])
        made[at : at + rows] = (near[at : at + rows] + got) * scale[at : at + rows]
        copies.append(
            pltpu.make_async_copy(
                made.at[pl.ds(at, rows)], out.at[pl.ds(at, rows)], sems.at[i]
            )
        )
        copies[-1].start()
    for copy in copies:
        copy.wait()


def in_hbm(array):
    return pltpu.with_memory_space_constraint(array, pltpu.HBM)


def call(kernel, inputs, specs, outs, out_specs, scratch, flops, moved_bytes, limit):
    return pl.pallas_call(
        kernel,
        out_shape=outs,
        in_specs=specs,
        out_specs=out_specs,
        scratch_shapes=scratch,
        cost_estimate=pl.CostEstimate(flops=flops, bytes_accessed=moved_bytes, transcendentals=0),
        compiler_params=pltpu.CompilerParams(vmem_limit_bytes=limit),
    )(*inputs)


def grouped(documents, queries, precond):
    count, width = documents.shape
    vmem, anywhere = pl.BlockSpec(memory_space=pltpu.VMEM), pl.BlockSpec(memory_space=pltpu.HBM)
    like = jax.ShapeDtypeStruct
    mib = 1024 * 1024

    other = over_core(precond)
    asked = {}
    for k in (3, 2):
        asked[k] = moved(queries, lambda y, z, x, c: (y, z ^ k, x ^ y, c))
    queries, other = lax.optimization_barrier((queries, other))
    for k in (1, 0):
        asked[k] = moved(queries, lambda y, z, x, c: (y, z ^ k, x ^ y, c))
    kept, scale, own = call(
        norm_kernel,
        (in_hbm(documents), in_hbm(precond), other),
        [anywhere, anywhere, pl.BlockSpec(memory_space=pl.ANY)],
        (like((count, width), BF16), like((count, 128), F32), like(precond.shape, BF16)),
        (vmem,) * 3,
        [pltpu.SemaphoreType.DMA((9,))],
        count * width * 2,
        count * width * 2,
        2 * mib,
    )
    piece = call(
        condition_kernel,
        (*[asked[k] for k in range(4)], own, other),
        [vmem] * 6,
        like((32, 512), BF16),
        vmem,
        [pltpu.VMEM((32, 512), F32)],
        2 * 32 * 512 * 1024,
        mib,
        4 * mib,
    )
    line = jnp.stack([piece] + [moved(piece, lambda y, z, x, c: (y, z ^ k, x, c)) for k in (1, 2, 3)])
    first = moved(line, lambda y, z, x, c: (y ^ c, z, x ^ 1 ^ c, c))
    second = moved(line, lambda y, z, x, c: (y ^ 1 ^ c, z, x ^ c, c))
    third = moved(first, lambda y, z, x, c: (y ^ 1 ^ c, z, x ^ c, c))
    line_c, first_c, second_c, third_c = map(over_core, (line, first, second, third))
    half = [pltpu.VMEM((128, width // 2), BF16), pltpu.VMEM((128, width // 2), BF16)]
    near = call(
        near_kernel,
        (kept, line, line_c, first, second, first_c, second_c),
        [vmem] * 7,
        like((count, 128), F32),
        vmem,
        half,
        count * width * 128,
        count * width,
        12 * mib,
    )
    return call(
        far_kernel,
        (kept, scale, near, third, first, second, third_c, first_c, second_c),
        [vmem] * 9,
        like((count, 128), F32),
        anywhere,
        [*half, pltpu.VMEM((count, 128), F32), pltpu.SemaphoreType.DMA((4,))],
        count * width * 128,
        count * width,
        12 * mib,
    )


def general(documents, queries, precond):
    panels, _, panel_width = precond.shape
    width = documents.shape[1]
    asked = lax.all_gather(queries, "row", axis=0, tiled=True)
    asked = asked.reshape(asked.shape[0], panels, panel_width)
    own = jnp.einsum("qbk,brk->bqr", asked, precond, preferred_element_type=F32).astype(BF16)
    ready = lax.all_gather(own, "row", axis=0)
    ready = ready.transpose(2, 1, 0, 3).reshape(-1, width)
    raw = jnp.dot(documents, ready.T, preferred_element_type=F32)
    dense = documents.astype(F32)
    spread = jnp.sqrt(jnp.mean(dense * dense, axis=1) + 1e-06)
    return raw / (spread[:, None] * jnp.sqrt(F32(width)))


def solution(mesh):
    fits = mesh.shape["shard"] == 2 and mesh.shape["row"] == 16
    placed = (P(AXES, None), P("row", None), P(None, "row", None))
    return jax.shard_map(
        grouped if fits else general,
        mesh=mesh,
        in_specs=placed,
        out_specs=P(AXES, None),
        check_vma=False,
    )
```

time: 145 us -> 37.2 us (0.26)
  waiting for transfers between devices: 112 us -> 6.66 us
  starting transfers between devices: 0.04 us -> 22.2 us
  between operations: 13.4 us -> 0.07 us
  matrix products: 12.9 us -> 0 us
  Pallas kernels: 0 us -> 8.06 us
  other arithmetic: 5.08 us -> 0.02 us
    all_gather x2 -> x0, waiting for transfers between devices: 111 us -> none  [the longest x1 79.9 us: shards(): lax.all_gather(precond, 'row', axis=1, tiled=True)]
    ppermute x0 -> x15, starting transfers between devices: none -> 22.2 us  [moved(): return lax.ppermute(array, AXES, pairs)]
    dot_general x2 -> x0, matrix products: 12.9 us -> none  [the longest x1 6.62 us: shards(): jnp.dot(documents, lax.all_gather(own_ready, 'row', axis=0, tiled=True).T...]
    pallas_call x0 -> x4, Pallas kernels: none -> 8.06 us  [call(): pl.pallas_call(kernel, out_shape=outs, in_specs=specs, out_specs=out_spec...]
    ppermute x0 -> x15, waiting for transfers between devices: none -> 6.66 us  [moved(): return lax.ppermute(array, AXES, pairs)]
    reduce_sum x1 -> x0, other arithmetic: 5.07 us -> none  [shards(): spread = jnp.sqrt(jnp.mean(dense * dense, axis=1) + 1e-06)]
  transfers between devices with their start and end apart: 2 -> 15, of which waited for: 2 -> 4; matrix products, arithmetic and copies ran while one was open for 4% -> 0% of each run, Pallas kernels for 0% -> 14%
where the time goes in v2:
time: 37.2 us; the launch traced here: 37 us
  starting transfers between devices  22.2 us (60%)
  Pallas kernels  8.06 us (22%)
  waiting for transfers between devices  6.66 us (18%)
    ppermute x15, starting transfers between devices, moved(): return lax.ppermute(array, AXES, pairs)  22.2 us
    pallas_call x4, Pallas kernels, call(): pl.pallas_call(kernel, out_shape=outs, in_specs=specs, out_specs=out_spec...  8.06 us
    ppermute x15, waiting for transfers between devices, moved(): return lax.ppermute(array, AXES, pairs)  6.66 us
  transfers between devices with their start and end apart: 15, of which 4 were waited for; matrix products, arithmetic and copies ran while one was open for 0% of the time, Pallas kernels for 14%

profile of v2, /device:TPU:0, one launch (start us, length us, event | category | flops | bytes accessed | tf_op | source)
XLA Modules:
  0.0 37.0 jit_solution(12024970864386616259)
XLA Ops:
  0.0 0.5 %collective-permute-start = (bf16[4,64,1024]{2,1,0:T(8,128)(2,1)}, bf16[4,64,1024]{2,1,0:T(8,128)(2,1)S(1)}, u32[]{:S(2)}, u32[]{:S(2)}) collective-permute-start(bf16[4,64,1024]{2,1,0:T(8,128)(2,1)} %own.1), channel_id=1, source_target_pairs={{1,0},{0,1},{3,2},{2,3},{5,4},{4,5},{7,6},{6,7},{9,8},{8,9},{11,10... | collective-permute-start | bytes 1572872 | tf_op jit(solution)/shard_map/ppermute | solution.py:23
  0.5 4.6 %collective-permute-start.4 = (bf16[8,4096]{1,0:T(8,128)(2,1)}, bf16[8,4096]{1,0:T(8,128)(2,1)S(1)}, u32[]{:S(2)}, u32[]{:S(2)}) collective-permute-start(bf16[8,4096]{1,0:T(8,128)(2,1)} %param.4), channel_id=1, source_target_pairs={{12,0},{13,1},{14,2},{15,3},{8,4},{9,5},{10,6},{11,7},{4,8},{5,9},... | collective-permute-start | bytes 196616 | tf_op jit(solution)/shard_map/ppermute | solution.py:23
  5.1 0.0 collective-permute-start.3
  5.1 0.0 collective-permute-done.after.other
  5.1 0.6 %collective-permute-start.2 = (bf16[8,4096]{1,0:T(8,128)(2,1)}, bf16[8,4096]{1,0:T(8,128)(2,1)S(1)}, u32[]{:S(2)}, u32[]{:S(2)}) collective-permute-start(bf16[8,4096]{1,0:T(8,128)(2,1)} %param.4), channel_id=1, source_target_pairs={{4,0},{5,1},{6,2},{7,3},{0,4},{1,5},{2,6},{3,7},{12,8},{13,9},{14,... | collective-permute-start | bytes 196616 | tf_op jit(solution)/shard_map/ppermute | solution.py:23
  5.7 1.5 %collective-permute-start.1 = (bf16[8,4096]{1,0:T(8,128)(2,1)}, bf16[8,4096]{1,0:T(8,128)(2,1)S(1)}, u32[]{:S(2)}, u32[]{:S(2)}) collective-permute-start(bf16[8,4096]{1,0:T(8,128)(2,1)} %param.4), channel_id=1, source_target_pairs={{0,0},{1,1},{2,2},{3,3},{4,4},{5,5},{6,6},{7,7},{8,8},{9,9},{10,10... | collective-permute-start | bytes 196616 | tf_op jit(solution)/shard_map/ppermute | solution.py:23
  7.2 3.8 %shard_map.37 = (bf16[1024,4096]{1,0:T(8,128)(2,1)S(1)}, f32[1024,128]{1,0:T(8,128)S(1)}, bf16[4,64,1024]{2,1,0:T(8,128)(2,1)S(1)}) custom-call(bf16[1024,4096]{1,0:T(8,128)(2,1)} %docs.1, bf16[4,64,1024]{2,1,0:T(8,128)(2,1)} %own.1, bf16[4,64,1024]{2,1,0:T(8,128)(2,1)S(1)} %collective-permute-done.after.other), custom_call_target="tpu_custom_call" | custom-call | flops 8388608 | bytes 8388608 | tf_op jit(solution)/shard_map/pallas_call | solution.py:180
  11.0 0.0 collective-permute-done.4.q3
  11.0 0.4 %collective-permute-done.3.q2 = bf16[8,4096]{1,0:T(8,128)(2,1)S(1)} collective-permute-done((bf16[8,4096]{1,0:T(8,128)(2,1)}, bf16[8,4096]{1,0:T(8,128)(2,1)S(1)}, u32[]{:S(2)}, u32[]{:S(2)}) %collective-permute-start.3) | collective-permute-done | bytes 65568 | tf_op jit(solution)/shard_map/ppermute | solution.py:23
  11.4 0.0 collective-permute-done.2.q1
  11.4 0.0 collective-permute-done.1.q0
  11.4 0.5 %shard_map.38 = bf16[32,512]{1,0:T(8,128)(2,1)S(1)} custom-call(bf16[8,4096]{1,0:T(8,128)(2,1)S(1)} %collective-permute-done.1.q0, bf16[8,4096]{1,0:T(8,128)(2,1)S(1)} %collective-permute-done.2.q1, bf16[8,4096]{1,0:T(8,128)(2,1)S(1)} %collective-permute-done.3.q2, bf16[8,4096]{1,0:T(8,128)(2,1)S(1)} %collective-permute-done.4.q3, ...), custom_call_target="tpu_custom_call" | custom-call | flops 33554432 | bytes 1048576 | tf_op jit(solution)/shard_map/pallas_call | solution.py:180
  11.9 3.4 %collective-permute-start.7 = (bf16[32,512]{1,0:T(8,128)(2,1)S(1)}, bf16[32,512]{1,0:T(8,128)(2,1)S(1)}, u32[]{:S(2)}, u32[]{:S(2)}) collective-permute-start(bf16[32,512]{1,0:T(8,128)(2,1)S(1)} %shard_map.38), channel_id=1, source_target_pairs={{12,0},{13,1},{14,2},{15,3},{8,4},{9,5},{10,6},{11,7},{4,8},{5,9},... | collective-permute-start | bytes 98312 | tf_op jit(solution)/shard_map/ppermute | solution.py:23
  15.4 0.0 collective-permute-start.6
  15.4 1.0 %collective-permute-start.5 = (bf16[32,512]{1,0:T(8,128)(2,1)S(1)}, bf16[32,512]{1,0:T(8,128)(2,1)S(1)}, u32[]{:S(2)}, u32[]{:S(2)}) collective-permute-start(bf16[32,512]{1,0:T(8,128)(2,1)S(1)} %shard_map.38), channel_id=1, source_target_pairs={{4,0},{5,1},{6,2},{7,3},{0,4},{1,5},{2,6},{3,7},{12,8},{13,9},{14,... | collective-permute-start | bytes 98312 | tf_op jit(solution)/shard_map/ppermute | solution.py:23
  16.4 1.5 %collective-permute-done.7 = bf16[32,512]{1,0:T(8,128)(2,1)S(1)} collective-permute-done((bf16[32,512]{1,0:T(8,128)(2,1)S(1)}, bf16[32,512]{1,0:T(8,128)(2,1)S(1)}, u32[]{:S(2)}, u32[]{:S(2)}) %collective-permute-start.7) | collective-permute-done | bytes 32800 | tf_op jit(solution)/shard_map/ppermute | solution.py:23
  17.9 2.3 %collective-permute-done.6 = bf16[32,512]{1,0:T(8,128)(2,1)S(1)} collective-permute-done((bf16[32,512]{1,0:T(8,128)(2,1)S(1)}, bf16[32,512]{1,0:T(8,128)(2,1)S(1)}, u32[]{:S(2)}, u32[]{:S(2)}) %collective-permute-start.6) | collective-permute-done | bytes 32800 | tf_op jit(solution)/shard_map/ppermute | solution.py:23
  20.2 0.0 collective-permute-done.5
  20.2 1.6 %collective-permute-start.9 = (bf16[4,32,512]{2,1,0:T(8,128)(2,1)S(1)}, bf16[4,32,512]{2,1,0:T(8,128)(2,1)S(1)}, u32[]{:S(2)}, u32[]{:S(2)}) collective-permute-start(bf16[4,32,512]{2,1,0:T(8,128)(2,1)S(1)} %pad_maximum_fusion.line), channel_id=1, source_target_pairs={{2,0},{17,1},{0,2},{19,3},{6,4},{21,5},{4,6},{23,7},{10,8},{25,9},... | collective-permute-start | bytes 393224 | tf_op jit(solution)/shard_map/ppermute | solution.py:23
  21.8 4.3 %collective-permute-start.10 = (bf16[4,32,512]{2,1,0:T(8,128)(2,1)S(1)}, bf16[4,32,512]{2,1,0:T(8,128)(2,1)S(1)}, u32[]{:S(2)}, u32[]{:S(2)}) collective-permute-start(bf16[4,32,512]{2,1,0:T(8,128)(2,1)S(1)} %pad_maximum_fusion.line), channel_id=1, source_target_pairs={{16,0},{3,1},{18,2},{1,3},{20,4},{7,5},{22,6},{5,7},{24,8},{11,9},... | collective-permute-start | bytes 393224 | tf_op jit(solution)/shard_map/ppermute | solution.py:23
  26.1 0.0 collective-permute-done.9.first
  26.1 4.2 %collective-permute-start.13 = (bf16[4,32,512]{2,1,0:T(8,128)(2,1)S(1)}, bf16[4,32,512]{2,1,0:T(8,128)(2,1)S(1)}, u32[]{:S(2)}, u32[]{:S(2)}) collective-permute-start(bf16[4,32,512]{2,1,0:T(8,128)(2,1)S(1)} %collective-permute-done.9.first), channel_id=1, source_target_pairs={{16,0},{3,1},{18,2},{1,3},{20,4},{7,5},{22,6},{5,7},{24,8},{11,9},... | collective-permute-start | bytes 393224 | tf_op jit(solution)/shard_map/ppermute | solution.py:23
  30.2 0.0 collective-permute-start.8
  30.2 0.0 collective-permute-done.10.second
  30.2 0.5 %collective-permute-start.12 = (bf16[4,32,512]{2,1,0:T(8,128)(2,1)S(1)}, bf16[4,32,512]{2,1,0:T(8,128)(2,1)S(1)}, u32[]{:S(2)}, u32[]{:S(2)}) collective-permute-start(bf16[4,32,512]{2,1,0:T(8,128)(2,1)S(1)} %collective-permute-done.10.second), channel_id=1, source_target_pairs={{1,0},{0,1},{3,2},{2,3},{5,4},{4,5},{7,6},{6,7},{9,8},{8,9},{11,10... | collective-permute-start | bytes 393224 | tf_op jit(solution)/shard_map/ppermute | solution.py:23
  30.7 0.0 collective-permute-start.11
  30.7 2.4 %collective-permute-done.13.third = bf16[4,32,512]{2,1,0:T(8,128)(2,1)S(1)} collective-permute-done((bf16[4,32,512]{2,1,0:T(8,128)(2,1)S(1)}, bf16[4,32,512]{2,1,0:T(8,128)(2,1)S(1)}, u32[]{:S(2)}, u32[]{:S(2)}) %collective-permute-start.13) | collective-permute-done | bytes 131104 | tf_op jit(solution)/shard_map/ppermute | solution.py:23
  33.2 0.0 collective-permute-start.14
  33.2 0.0 collective-permute-done.8.line_c
  33.2 0.0 collective-permute-done.12.second_c
  33.2 0.0 collective-permute-done.11.first_c
  33.2 1.5 %shard_map.39.near = f32[1024,128]{1,0:T(8,128)S(1)} custom-call(bf16[1024,4096]{1,0:T(8,128)(2,1)S(1)} %get-tuple-element.11.docs, bf16[4,32,512]{2,1,0:T(8,128)(2,1)S(1)} %pad_maximum_fusion.line, bf16[4,32,512]{2,1,0:T(8,128)(2,1)S(1)} %collective-permute-done.8.line_c, bf16[4,32,512]{2,1,0:T(8,128)(2,1)S(1)} %collective-permute-done.9.first, ...), custom_call_target="tpu_custom_call" | custom-call | flops 536870912 | bytes 4194304 | tf_op jit(solution)/shard_map/pallas_call | solution.py:180
  34.7 0.0 collective-permute-done.14.third_c
  34.7 2.3 %shard_map.40 = f32[1024,128]{1,0:T(8,128)} custom-call(bf16[1024,4096]{1,0:T(8,128)(2,1)S(1)} %get-tuple-element.11.docs, f32[1024,128]{1,0:T(8,128)S(1)} %get-tuple-element.12.scale, f32[1024,128]{1,0:T(8,128)S(1)} %shard_map.39.near, bf16[4,32,512]{2,1,0:T(8,128)(2,1)S(1)} %collective-permute-done.13.third, ...), custom_call_target="tpu_custom_call" | custom-call | flops 536870912 | bytes 4194304 | tf_op jit(solution)/shard_map/pallas_call | solution.py:180
  (1 shorter events, 0.0 us)
Async XLA Ops:
  0.0 5.1 %collective-permute-start = (bf16[4,64,1024]{2,1,0:T(8,128)(2,1)}, bf16[4,64,1024]{2,1,0:T(8,128)(2,1)S(1)}, u32[]{:S(2)}, u32[]{:S(2)}) collective-permute-start(bf16[4,64,1024]{2,1,0:T(8,128)(2,1)} %own.1), channel_id=1, source_target_pairs={{1,0},{0,1},{3,2},{2,3},{5,4},{4,5},{7,6},{6,7},{9,8},{8,9},{11,10... | collective-permute-start | bytes 1572872 | tf_op jit(solution)/shard_map/ppermute | solution.py:23
  0.5 10.5 %collective-permute-start.4 = (bf16[8,4096]{1,0:T(8,128)(2,1)}, bf16[8,4096]{1,0:T(8,128)(2,1)S(1)}, u32[]{:S(2)}, u32[]{:S(2)}) collective-permute-start(bf16[8,4096]{1,0:T(8,128)(2,1)} %param.4), channel_id=1, source_target_pairs={{12,0},{13,1},{14,2},{15,3},{8,4},{9,5},{10,6},{11,7},{4,8},{5,9},... | collective-permute-start | bytes 196616 | tf_op jit(solution)/shard_map/ppermute | solution.py:23
  5.1 6.3 %collective-permute-start.3 = (bf16[8,4096]{1,0:T(8,128)(2,1)}, bf16[8,4096]{1,0:T(8,128)(2,1)S(1)}, u32[]{:S(2)}, u32[]{:S(2)}) collective-permute-start(bf16[8,4096]{1,0:T(8,128)(2,1)} %param.4), channel_id=1, source_target_pairs={{8,0},{9,1},{10,2},{11,3},{12,4},{13,5},{14,6},{15,7},{0,8},{1,9},... | collective-permute-start | bytes 196616 | tf_op jit(solution)/shard_map/ppermute | solution.py:23
  5.1 6.3 %collective-permute-start.2 = (bf16[8,4096]{1,0:T(8,128)(2,1)}, bf16[8,4096]{1,0:T(8,128)(2,1)S(1)}, u32[]{:S(2)}, u32[]{:S(2)}) collective-permute-start(bf16[8,4096]{1,0:T(8,128)(2,1)} %param.4), channel_id=1, source_target_pairs={{4,0},{5,1},{6,2},{7,3},{0,4},{1,5},{2,6},{3,7},{12,8},{13,9},{14,... | collective-permute-start | bytes 196616 | tf_op jit(solution)/shard_map/ppermute | solution.py:23
  5.7 5.7 %collective-permute-start.1 = (bf16[8,4096]{1,0:T(8,128)(2,1)}, bf16[8,4096]{1,0:T(8,128)(2,1)S(1)}, u32[]{:S(2)}, u32[]{:S(2)}) collective-permute-start(bf16[8,4096]{1,0:T(8,128)(2,1)} %param.4), channel_id=1, source_target_pairs={{0,0},{1,1},{2,2},{3,3},{4,4},{5,5},{6,6},{7,7},{8,8},{9,9},{10,10... | collective-permute-start | bytes 196616 | tf_op jit(solution)/shard_map/ppermute | solution.py:23
  11.9 5.9 %collective-permute-start.7 = (bf16[32,512]{1,0:T(8,128)(2,1)S(1)}, bf16[32,512]{1,0:T(8,128)(2,1)S(1)}, u32[]{:S(2)}, u32[]{:S(2)}) collective-permute-start(bf16[32,512]{1,0:T(8,128)(2,1)S(1)} %shard_map.38), channel_id=1, source_target_pairs={{12,0},{13,1},{14,2},{15,3},{8,4},{9,5},{10,6},{11,7},{4,8},{5,9},... | collective-permute-start | bytes 98312 | tf_op jit(solution)/shard_map/ppermute | solution.py:23
  15.4 4.8 %collective-permute-start.6 = (bf16[32,512]{1,0:T(8,128)(2,1)S(1)}, bf16[32,512]{1,0:T(8,128)(2,1)S(1)}, u32[]{:S(2)}, u32[]{:S(2)}) collective-permute-start(bf16[32,512]{1,0:T(8,128)(2,1)S(1)} %shard_map.38), channel_id=1, source_target_pairs={{8,0},{9,1},{10,2},{11,3},{12,4},{13,5},{14,6},{15,7},{0,8},{1,9},... | collective-permute-start | bytes 98312 | tf_op jit(solution)/shard_map/ppermute | solution.py:23
  15.4 4.8 %collective-permute-start.5 = (bf16[32,512]{1,0:T(8,128)(2,1)S(1)}, bf16[32,512]{1,0:T(8,128)(2,1)S(1)}, u32[]{:S(2)}, u32[]{:S(2)}) collective-permute-start(bf16[32,512]{1,0:T(8,128)(2,1)S(1)} %shard_map.38), channel_id=1, source_target_pairs={{4,0},{5,1},{6,2},{7,3},{0,4},{1,5},{2,6},{3,7},{12,8},{13,9},{14,... | collective-permute-start | bytes 98312 | tf_op jit(solution)/shard_map/ppermute | solution.py:23
  20.2 5.9 %collective-permute-start.9 = (bf16[4,32,512]{2,1,0:T(8,128)(2,1)S(1)}, bf16[4,32,512]{2,1,0:T(8,128)(2,1)S(1)}, u32[]{:S(2)}, u32[]{:S(2)}) collective-permute-start(bf16[4,32,512]{2,1,0:T(8,128)(2,1)S(1)} %pad_maximum_fusion.line), channel_id=1, source_target_pairs={{2,0},{17,1},{0,2},{19,3},{6,4},{21,5},{4,6},{23,7},{10,8},{25,9},... | collective-permute-start | bytes 393224 | tf_op jit(solution)/shard_map/ppermute | solution.py:23
  21.8 8.5 %collective-permute-start.10 = (bf16[4,32,512]{2,1,0:T(8,128)(2,1)S(1)}, bf16[4,32,512]{2,1,0:T(8,128)(2,1)S(1)}, u32[]{:S(2)}, u32[]{:S(2)}) collective-permute-start(bf16[4,32,512]{2,1,0:T(8,128)(2,1)S(1)} %pad_maximum_fusion.line), channel_id=1, source_target_pairs={{16,0},{3,1},{18,2},{1,3},{20,4},{7,5},{22,6},{5,7},{24,8},{11,9},... | collective-permute-start | bytes 393224 | tf_op jit(solution)/shard_map/ppermute | solution.py:23
  26.1 7.1 %collective-permute-start.13 = (bf16[4,32,512]{2,1,0:T(8,128)(2,1)S(1)}, bf16[4,32,512]{2,1,0:T(8,128)(2,1)S(1)}, u32[]{:S(2)}, u32[]{:S(2)}) collective-permute-start(bf16[4,32,512]{2,1,0:T(8,128)(2,1)S(1)} %collective-permute-done.9.first), channel_id=1, source_target_pairs={{16,0},{3,1},{18,2},{1,3},{20,4},{7,5},{22,6},{5,7},{24,8},{11,9},... | collective-permute-start | bytes 393224 | tf_op jit(solution)/shard_map/ppermute | solution.py:23
  30.2 3.0 %collective-permute-start.8 = (bf16[4,32,512]{2,1,0:T(8,128)(2,1)S(1)}, bf16[4,32,512]{2,1,0:T(8,128)(2,1)S(1)}, u32[]{:S(2)}, u32[]{:S(2)}) collective-permute-start(bf16[4,32,512]{2,1,0:T(8,128)(2,1)S(1)} %pad_maximum_fusion.line), channel_id=1, source_target_pairs={{1,0},{0,1},{3,2},{2,3},{5,4},{4,5},{7,6},{6,7},{9,8},{8,9},{11,10... | collective-permute-start | bytes 393224 | tf_op jit(solution)/shard_map/ppermute | solution.py:23
  30.2 2.9 %collective-permute-start.12 = (bf16[4,32,512]{2,1,0:T(8,128)(2,1)S(1)}, bf16[4,32,512]{2,1,0:T(8,128)(2,1)S(1)}, u32[]{:S(2)}, u32[]{:S(2)}) collective-permute-start(bf16[4,32,512]{2,1,0:T(8,128)(2,1)S(1)} %collective-permute-done.10.second), channel_id=1, source_target_pairs={{1,0},{0,1},{3,2},{2,3},{5,4},{4,5},{7,6},{6,7},{9,8},{8,9},{11,10... | collective-permute-start | bytes 393224 | tf_op jit(solution)/shard_map/ppermute | solution.py:23
  30.7 2.4 %collective-permute-start.11 = (bf16[4,32,512]{2,1,0:T(8,128)(2,1)S(1)}, bf16[4,32,512]{2,1,0:T(8,128)(2,1)S(1)}, u32[]{:S(2)}, u32[]{:S(2)}) collective-permute-start(bf16[4,32,512]{2,1,0:T(8,128)(2,1)S(1)} %collective-permute-done.9.first), channel_id=1, source_target_pairs={{1,0},{0,1},{3,2},{2,3},{5,4},{4,5},{7,6},{6,7},{9,8},{8,9},{11,10... | collective-permute-start | bytes 393224 | tf_op jit(solution)/shard_map/ppermute | solution.py:23
  33.2 1.5 %collective-permute-start.14 = (bf16[4,32,512]{2,1,0:T(8,128)(2,1)S(1)}, bf16[4,32,512]{2,1,0:T(8,128)(2,1)S(1)}, u32[]{:S(2)}, u32[]{:S(2)}) collective-permute-start(bf16[4,32,512]{2,1,0:T(8,128)(2,1)S(1)} %collective-permute-done.13.third), channel_id=1, source_target_pairs={{1,0},{0,1},{3,2},{2,3},{5,4},{4,5},{7,6},{6,7},{9,8},{8,9},{11,10... | collective-permute-start | bytes 393224 | tf_op jit(solution)/shard_map/ppermute | solution.py:23

commit v3 on v2

--- a/solution.py
+++ b/solution.py
@@ -25,6 +25,14 @@
 
 def over_core(array):
     return moved(array, lambda y, z, x, c: (y, z, x, c ^ 1))
+
+
+def parity(z):
+    return z % 2
+
+
+def spot(z):
+    return parity(z) * 2 + z // 2
 
 
 def condition_kernel(q0, q1, q2, q3, own, other, out, acc):
@@ -39,7 +47,7 @@
         )
         got = pltpu.roll(got, c * rows, axis=1)
         for k in range(4):
-            acc[pl.ds(pl.multiple_of((z ^ k) * 8, 8), 8), b * 128 : (b + 1) * 128] = got[
+            acc[pl.ds(pl.multiple_of(spot(z ^ k) * 8, 8), 8), b * 128 : (b + 1) * 128] = got[
                 k * 8 : (k + 1) * 8
             ]
     out[...] = acc[...].astype(BF16)
@@ -72,19 +80,21 @@
 
 
 def assemble(pieces, held, ready, z):
-    for slot, piece in pieces:
-        rows = pl.ds(pl.multiple_of(slot * 32, 32), 32)
+    for tilt, core, piece in pieces:
         for k in range(4):
-            for b in range(4):
-                start = b * 512 + (z ^ k) * 128
-                held[rows, pl.ds(pl.multiple_of(start, 128), 128)] = piece[
-                    k, :, b * 128 : (b + 1) * 128
-                ]
+            for group in range(2):
+                side = tilt ^ parity(z ^ k) ^ group
+                rows = pl.ds(pl.multiple_of((side * 2 + core) * 32 + group * 16, 16), 16)
+                for b in range(4):
+                    start = pl.multiple_of(b * 512 + (z ^ k) * 128, 128)
+                    held[rows, pl.ds(start, 128)] = piece[
+                        k, group * 16 : (group + 1) * 16, b * 128 : (b + 1) * 128
+                    ]
     width = held.shape[1]
     step = 512
     for at in range(0, width, step):
         part = held[:, at : at + step].astype(F32).reshape(4, 4, 8, step)
-        part = jnp.concatenate([part[s, k] for k in range(4) for s in range(4)], axis=0)
+        part = jnp.concatenate([part[s, spot(at_z)] for at_z in range(4) for s in range(4)], axis=0)
         ready[:, at : at + step] = part.astype(BF16)
 
 
@@ -100,63 +110,28 @@
     return lax.dot_general(left, right, (((1,), (1,)), ((), ())), preferred_element_type=F32)
 
 
-def near_kernel(docs, line, line_c, first, second, first_c, second_c, out, held, ready):
+def near_kernel(docs, own, own_c, across, across_c, out, held, ready):
     y, z, x, c = place()
     s = x ^ y
-
-    def fill(own, across, own_c, across_c):
-        assemble(
-            [
-                (s * 2 + c, own),
-                ((1 - s) * 2 + c, across),
-                (s * 2 + 1 - c, own_c),
-                ((1 - s) * 2 + 1 - c, across_c),
-            ],
-            held,
-            ready,
-            z,
-        )
-
-    @pl.when(c == 0)
-    def _():
-        fill(line, second, line_c, first_c)
-
-    @pl.when(c == 1)
-    def _():
-        fill(line, first, line_c, second_c)
-
+    assemble(
+        ((s, c, own), (s, 1 - c, own_c), (1 - s, c, across), (1 - s, 1 - c, across_c)), held, ready, z
+    )
     rows = 256
     for at in range(0, docs.shape[0], rows):
         out[at : at + rows] = times(columns(docs, at, rows, x), ready[...])
 
 
 def far_kernel(
-    docs, scale, near, third, first, second, third_c, first_c, second_c, out, held, ready, made, sems
+    docs, scale, near, diagonal, diagonal_c, beside, beside_c, out, held, ready, made, sems
 ):
     y, z, x, c = place()
     s = x ^ y
-
-    def fill(diagonal, beside, diagonal_c, beside_c):
-        assemble(
-            [
-                (s * 2 + c, diagonal),
-                ((1 - s) * 2 + c, beside),
-                (s * 2 + 1 - c, diagonal_c),
-                ((1 - s) * 2 + 1 - c, beside_c),
-            ],
-            held,
-            ready,
-            z,
-        )
-
-    @pl.when(c == 0)
-    def _():
-        fill(third, first, third_c, second_c)
-
-    @pl.when(c == 1)
-    def _():
-        fill(third, second, third_c, first_c)
-
+    assemble(
+        ((s, c, diagonal), (s, 1 - c, diagonal_c), (1 - s, c, beside), (1 - s, 1 - c, beside_c)),
+        held,
+        ready,
+        z,
+    )
     rows = 256
     copies = []
     for i, at in enumerate(range(0, docs.shape[0], rows)):
@@ -196,11 +171,11 @@
 
     other = over_core(precond)
     asked = {}
-    for k in (3, 2):
-        asked[k] = moved(queries, lambda y, z, x, c: (y, z ^ k, x ^ y, c))
+    for k in (3,2):
+        asked[k] = moved(queries, lambda y, z, x, c: (y, z ^ k, x ^ y ^ parity(k), c))
     queries, other = lax.optimization_barrier((queries, other))
-    for k in (1, 0):
-        asked[k] = moved(queries, lambda y, z, x, c: (y, z ^ k, x ^ y, c))
+    for k in (1,0):
+        asked[k] = moved(queries, lambda y, z, x, c: (y, z ^ k, x ^ y ^ parity(k), c))
     kept, scale, own = call(
         norm_kernel,
         (in_hbm(documents), in_hbm(precond), other),
@@ -224,15 +199,15 @@
         4 * mib,
     )
     line = jnp.stack([piece] + [moved(piece, lambda y, z, x, c: (y, z ^ k, x, c)) for k in (1, 2, 3)])
-    first = moved(line, lambda y, z, x, c: (y ^ c, z, x ^ 1 ^ c, c))
-    second = moved(line, lambda y, z, x, c: (y ^ 1 ^ c, z, x ^ c, c))
-    third = moved(first, lambda y, z, x, c: (y ^ 1 ^ c, z, x ^ c, c))
-    line_c, first_c, second_c, third_c = map(over_core, (line, first, second, third))
+    diagonal = moved(line, lambda y, z, x, c: (y ^ 1, z, x ^ 1, c))
+    beside = moved(line, lambda y, z, x, c: (y, z, x ^ 1, c))
+    across = moved(line, lambda y, z, x, c: (y ^ 1, z, x, c))
+    line_c, across_c, beside_c, diagonal_c = map(over_core, (line, across, beside, diagonal))
     half = [pltpu.VMEM((128, width // 2), BF16), pltpu.VMEM((128, width // 2), BF16)]
     near = call(
         near_kernel,
-        (kept, line, line_c, first, second, first_c, second_c),
-        [vmem] * 7,
+        (kept, line, line_c, across, across_c),
+        [vmem] * 5,
         like((count, 128), F32),
         vmem,
         half,
@@ -242,8 +217,8 @@
     )
     return call(
         far_kernel,
-        (kept, scale, near, third, first, second, third_c, first_c, second_c),
-        [vmem] * 9,
+        (kept, scale, near, diagonal, diagonal_c, beside, beside_c),
+        [vmem] * 7,
         like((count, 128), F32),
         anywhere,
         [*half, pltpu.VMEM((count, 128), F32), pltpu.SemaphoreType.DMA((4,))],

time: 37.2 us -> 35.1 us (0.944)
  starting transfers between devices: 22.2 us -> 16.8 us
  waiting for transfers between devices: 6.66 us -> 9.92 us
    ppermute x15, starting transfers between devices: 22.2 us -> 16.8 us  [moved(): return lax.ppermute(array, AXES, pairs)]
    ppermute x15, waiting for transfers between devices: 6.66 us -> 9.92 us  [moved(): return lax.ppermute(array, AXES, pairs)]
  transfers between devices with their start and end apart: 15 -> 15, of which waited for: 4 -> 7; matrix products, arithmetic and copies ran while one was open for 0% -> 0% of each run, Pallas kernels for 14% -> 15%
where the time goes in v3:
time: 35.1 us; the launch traced here: 34.9 us
  starting transfers between devices  16.8 us (48%)
  waiting for transfers between devices  9.92 us (28%)
  Pallas kernels  8.12 us (23%)
    ppermute x15, starting transfers between devices, moved(): return lax.ppermute(array, AXES, pairs)  16.8 us
    ppermute x15, waiting for transfers between devices, moved(): return lax.ppermute(array, AXES, pairs)  9.92 us
    pallas_call x4, Pallas kernels, call(): pl.pallas_call(kernel, out_shape=outs, in_specs=specs, out_specs=out_spec...  8.12 us
  transfers between devices with their start and end apart: 15, of which 7 were waited for; matrix products, arithmetic and copies ran while one was open for 0% of the time, Pallas kernels for 15%

profile of v3, /device:TPU:0, one launch (start us, length us, event | category | flops | bytes accessed | tf_op | source)
XLA Modules:
  0.0 34.9 jit_solution(17220885850201252778)
XLA Ops:
  0.0 0.5 %collective-permute-start = (bf16[4,64,1024]{2,1,0:T(8,128)(2,1)}, bf16[4,64,1024]{2,1,0:T(8,128)(2,1)S(1)}, u32[]{:S(2)}, u32[]{:S(2)}) collective-permute-start(bf16[4,64,1024]{2,1,0:T(8,128)(2,1)} %own.1), channel_id=1, source_target_pairs={{1,0},{0,1},{3,2},{2,3},{5,4},{4,5},{7,6},{6,7},{9,8},{8,9},{11,10... | collective-permute-start | bytes 1572872 | tf_op jit(solution)/shard_map/ppermute | solution.py:23
  0.5 5.5 %collective-permute-start.4 = (bf16[8,4096]{1,0:T(8,128)(2,1)}, bf16[8,4096]{1,0:T(8,128)(2,1)S(1)}, u32[]{:S(2)}, u32[]{:S(2)}) collective-permute-start(bf16[8,4096]{1,0:T(8,128)(2,1)} %param.4), channel_id=1, source_target_pairs={{14,0},{15,1},{12,2},{13,3},{10,4},{11,5},{8,6},{9,7},{6,8},{7,9},... | collective-permute-start | bytes 196616 | tf_op jit(solution)/shard_map/ppermute | solution.py:23
  6.0 0.0 collective-permute-start.3
  6.0 0.0 collective-permute-done.after.other
  6.0 0.6 %collective-permute-start.2 = (bf16[8,4096]{1,0:T(8,128)(2,1)}, bf16[8,4096]{1,0:T(8,128)(2,1)S(1)}, u32[]{:S(2)}, u32[]{:S(2)}) collective-permute-start(bf16[8,4096]{1,0:T(8,128)(2,1)} %param.4), channel_id=1, source_target_pairs={{6,0},{7,1},{4,2},{5,3},{2,4},{3,5},{0,6},{1,7},{14,8},{15,9},{12,... | collective-permute-start | bytes 196616 | tf_op jit(solution)/shard_map/ppermute | solution.py:23
  6.6 1.5 %collective-permute-start.1 = (bf16[8,4096]{1,0:T(8,128)(2,1)}, bf16[8,4096]{1,0:T(8,128)(2,1)S(1)}, u32[]{:S(2)}, u32[]{:S(2)}) collective-permute-start(bf16[8,4096]{1,0:T(8,128)(2,1)} %param.4), channel_id=1, source_target_pairs={{0,0},{1,1},{2,2},{3,3},{4,4},{5,5},{6,6},{7,7},{8,8},{9,9},{10,10... | collective-permute-start | bytes 196616 | tf_op jit(solution)/shard_map/ppermute | solution.py:23
  8.1 3.8 %shard_map.37 = (bf16[1024,4096]{1,0:T(8,128)(2,1)S(1)}, f32[1024,128]{1,0:T(8,128)S(1)}, bf16[4,64,1024]{2,1,0:T(8,128)(2,1)S(1)}) custom-call(bf16[1024,4096]{1,0:T(8,128)(2,1)} %docs.1, bf16[4,64,1024]{2,1,0:T(8,128)(2,1)} %own.1, bf16[4,64,1024]{2,1,0:T(8,128)(2,1)S(1)} %collective-permute-done.after.other), custom_call_target="tpu_custom_call" | custom-call | flops 8388608 | bytes 8388608 | tf_op jit(solution)/shard_map/pallas_call | solution.py:155
  11.9 0.0 collective-permute-done.4.q3
  11.9 0.4 %collective-permute-done.3.q2 = bf16[8,4096]{1,0:T(8,128)(2,1)S(1)} collective-permute-done((bf16[8,4096]{1,0:T(8,128)(2,1)}, bf16[8,4096]{1,0:T(8,128)(2,1)S(1)}, u32[]{:S(2)}, u32[]{:S(2)}) %collective-permute-start.3) | collective-permute-done | bytes 65568 | tf_op jit(solution)/shard_map/ppermute | solution.py:23
  12.3 0.4 %collective-permute-done.2.q1 = bf16[8,4096]{1,0:T(8,128)(2,1)S(1)} collective-permute-done((bf16[8,4096]{1,0:T(8,128)(2,1)}, bf16[8,4096]{1,0:T(8,128)(2,1)S(1)}, u32[]{:S(2)}, u32[]{:S(2)}) %collective-permute-start.2) | collective-permute-done | bytes 65568 | tf_op jit(solution)/shard_map/ppermute | solution.py:23
  12.7 0.0 collective-permute-done.1.q0
  12.7 0.5 %shard_map.38 = bf16[32,512]{1,0:T(8,128)(2,1)S(1)} custom-call(bf16[8,4096]{1,0:T(8,128)(2,1)S(1)} %collective-permute-done.1.q0, bf16[8,4096]{1,0:T(8,128)(2,1)S(1)} %collective-permute-done.2.q1, bf16[8,4096]{1,0:T(8,128)(2,1)S(1)} %collective-permute-done.3.q2, bf16[8,4096]{1,0:T(8,128)(2,1)S(1)} %collective-permute-done.4.q3, ...), custom_call_target="tpu_custom_call" | custom-call | flops 33554432 | bytes 1048576 | tf_op jit(solution)/shard_map/pallas_call | solution.py:155
  13.3 3.0 %collective-permute-start.7 = (bf16[32,512]{1,0:T(8,128)(2,1)S(1)}, bf16[32,512]{1,0:T(8,128)(2,1)S(1)}, u32[]{:S(2)}, u32[]{:S(2)}) collective-permute-start(bf16[32,512]{1,0:T(8,128)(2,1)S(1)} %shard_map.38), channel_id=1, source_target_pairs={{12,0},{13,1},{14,2},{15,3},{8,4},{9,5},{10,6},{11,7},{4,8},{5,9},... | collective-permute-start | bytes 98312 | tf_op jit(solution)/shard_map/ppermute | solution.py:23
  16.3 0.0 collective-permute-start.6
  16.3 1.5 %collective-permute-start.5 = (bf16[32,512]{1,0:T(8,128)(2,1)S(1)}, bf16[32,512]{1,0:T(8,128)(2,1)S(1)}, u32[]{:S(2)}, u32[]{:S(2)}) collective-permute-start(bf16[32,512]{1,0:T(8,128)(2,1)S(1)} %shard_map.38), channel_id=1, source_target_pairs={{4,0},{5,1},{6,2},{7,3},{0,4},{1,5},{2,6},{3,7},{12,8},{13,9},{14,... | collective-permute-start | bytes 98312 | tf_op jit(solution)/shard_map/ppermute | solution.py:23
  17.7 1.3 %collective-permute-done.7 = bf16[32,512]{1,0:T(8,128)(2,1)S(1)} collective-permute-done((bf16[32,512]{1,0:T(8,128)(2,1)S(1)}, bf16[32,512]{1,0:T(8,128)(2,1)S(1)}, u32[]{:S(2)}, u32[]{:S(2)}) %collective-permute-start.7) | collective-permute-done | bytes 32800 | tf_op jit(solution)/shard_map/ppermute | solution.py:23
  19.0 2.0 %collective-permute-done.6 = bf16[32,512]{1,0:T(8,128)(2,1)S(1)} collective-permute-done((bf16[32,512]{1,0:T(8,128)(2,1)S(1)}, bf16[32,512]{1,0:T(8,128)(2,1)S(1)}, u32[]{:S(2)}, u32[]{:S(2)}) %collective-permute-start.6) | collective-permute-done | bytes 32800 | tf_op jit(solution)/shard_map/ppermute | solution.py:23
  21.1 0.0 collective-permute-done.5
  21.1 2.7 %collective-permute-start.9 = (bf16[4,32,512]{2,1,0:T(8,128)(2,1)S(1)}, bf16[4,32,512]{2,1,0:T(8,128)(2,1)S(1)}, u32[]{:S(2)}, u32[]{:S(2)}) collective-permute-start(bf16[4,32,512]{2,1,0:T(8,128)(2,1)S(1)} %pad_maximum_fusion.own), channel_id=1, source_target_pairs={{16,0},{17,1},{18,2},{19,3},{20,4},{21,5},{22,6},{23,7},{24,8},{25... | collective-permute-start | bytes 393224 | tf_op jit(solution)/shard_map/ppermute | solution.py:23
  23.8 1.4 %collective-permute-start.13 = (bf16[4,32,512]{2,1,0:T(8,128)(2,1)S(1)}, bf16[4,32,512]{2,1,0:T(8,128)(2,1)S(1)}, u32[]{:S(2)}, u32[]{:S(2)}) collective-permute-start(bf16[4,32,512]{2,1,0:T(8,128)(2,1)S(1)} %pad_maximum_fusion.own), channel_id=1, source_target_pairs={{2,0},{3,1},{0,2},{1,3},{6,4},{7,5},{4,6},{5,7},{10,8},{11,9},{8,1... | collective-permute-start | bytes 393224 | tf_op jit(solution)/shard_map/ppermute | solution.py:23
  25.2 0.1 collective-permute-start.11
  25.3 0.0 collective-permute-start.8
  25.3 2.8 %collective-permute-done.9.across = bf16[4,32,512]{2,1,0:T(8,128)(2,1)S(1)} collective-permute-done((bf16[4,32,512]{2,1,0:T(8,128)(2,1)S(1)}, bf16[4,32,512]{2,1,0:T(8,128)(2,1)S(1)}, u32[]{:S(2)}, u32[]{:S(2)}) %collective-permute-start.9) | collective-permute-done | bytes 131104 | tf_op jit(solution)/shard_map/ppermute | solution.py:23
  28.1 0.0 collective-permute-start.10
  28.1 0.6 %collective-permute-done.13.beside = bf16[4,32,512]{2,1,0:T(8,128)(2,1)S(1)} collective-permute-done((bf16[4,32,512]{2,1,0:T(8,128)(2,1)S(1)}, bf16[4,32,512]{2,1,0:T(8,128)(2,1)S(1)}, u32[]{:S(2)}, u32[]{:S(2)}) %collective-permute-start.13) | collective-permute-done | bytes 131104 | tf_op jit(solution)/shard_map/ppermute | solution.py:23
  28.7 0.0 collective-permute-start.14
  28.7 2.3 %collective-permute-done.11.diagonal = bf16[4,32,512]{2,1,0:T(8,128)(2,1)S(1)} collective-permute-done((bf16[4,32,512]{2,1,0:T(8,128)(2,1)S(1)}, bf16[4,32,512]{2,1,0:T(8,128)(2,1)S(1)}, u32[]{:S(2)}, u32[]{:S(2)}) %collective-permute-start.11) | collective-permute-done | bytes 131104 | tf_op jit(solution)/shard_map/ppermute | solution.py:23
  31.0 0.0 collective-permute-start.12
  31.0 0.0 collective-permute-done.8.own_c
  31.0 0.0 collective-permute-done.10.across_c
  31.0 1.5 %shard_map.39.near = f32[1024,128]{1,0:T(8,128)S(1)} custom-call(bf16[1024,4096]{1,0:T(8,128)(2,1)S(1)} %get-tuple-element.11.docs, bf16[4,32,512]{2,1,0:T(8,128)(2,1)S(1)} %pad_maximum_fusion.own, bf16[4,32,512]{2,1,0:T(8,128)(2,1)S(1)} %collective-permute-done.8.own_c, bf16[4,32,512]{2,1,0:T(8,128)(2,1)S(1)} %collective-permute-done.9.across, ...), custom_call_target="tpu_custom_call" | custom-call | flops 536870912 | bytes 4194304 | tf_op jit(solution)/shard_map/pallas_call | solution.py:155
  32.6 0.0 collective-permute-done.14.beside_c
  32.6 0.0 collective-permute-done.12.diagonal_c
  32.6 2.3 %shard_map.40 = f32[1024,128]{1,0:T(8,128)} custom-call(bf16[1024,4096]{1,0:T(8,128)(2,1)S(1)} %get-tuple-element.11.docs, f32[1024,128]{1,0:T(8,128)S(1)} %get-tuple-element.12.scale, f32[1024,128]{1,0:T(8,128)S(1)} %shard_map.39.near, bf16[4,32,512]{2,1,0:T(8,128)(2,1)S(1)} %collective-permute-done.11.diagonal, ...), custom_call_target="tpu_custom_call" | custom-call | flops 536870912 | bytes 4194304 | tf_op jit(solution)/shard_map/pallas_call | solution.py:155
  (1 shorter events, 0.0 us)
Async XLA Ops:
  0.0 6.0 %collective-permute-start = (bf16[4,64,1024]{2,1,0:T(8,128)(2,1)}, bf16[4,64,1024]{2,1,0:T(8,128)(2,1)S(1)}, u32[]{:S(2)}, u32[]{:S(2)}) collective-permute-start(bf16[4,64,1024]{2,1,0:T(8,128)(2,1)} %own.1), channel_id=1, source_target_pairs={{1,0},{0,1},{3,2},{2,3},{5,4},{4,5},{7,6},{6,7},{9,8},{8,9},{11,10... | collective-permute-start | bytes 1572872 | tf_op jit(solution)/shard_map/ppermute | solution.py:23
  0.5 11.4 %collective-permute-start.4 = (bf16[8,4096]{1,0:T(8,128)(2,1)}, bf16[8,4096]{1,0:T(8,128)(2,1)S(1)}, u32[]{:S(2)}, u32[]{:S(2)}) collective-permute-start(bf16[8,4096]{1,0:T(8,128)(2,1)} %param.4), channel_id=1, source_target_pairs={{14,0},{15,1},{12,2},{13,3},{10,4},{11,5},{8,6},{9,7},{6,8},{7,9},... | collective-permute-start | bytes 196616 | tf_op jit(solution)/shard_map/ppermute | solution.py:23
  6.0 6.3 %collective-permute-start.3 = (bf16[8,4096]{1,0:T(8,128)(2,1)}, bf16[8,4096]{1,0:T(8,128)(2,1)S(1)}, u32[]{:S(2)}, u32[]{:S(2)}) collective-permute-start(bf16[8,4096]{1,0:T(8,128)(2,1)} %param.4), channel_id=1, source_target_pairs={{8,0},{9,1},{10,2},{11,3},{12,4},{13,5},{14,6},{15,7},{0,8},{1,9},... | collective-permute-start | bytes 196616 | tf_op jit(solution)/shard_map/ppermute | solution.py:23
  6.0 6.7 %collective-permute-start.2 = (bf16[8,4096]{1,0:T(8,128)(2,1)}, bf16[8,4096]{1,0:T(8,128)(2,1)S(1)}, u32[]{:S(2)}, u32[]{:S(2)}) collective-permute-start(bf16[8,4096]{1,0:T(8,128)(2,1)} %param.4), channel_id=1, source_target_pairs={{6,0},{7,1},{4,2},{5,3},{2,4},{3,5},{0,6},{1,7},{14,8},{15,9},{12,... | collective-permute-start | bytes 196616 | tf_op jit(solution)/shard_map/ppermute | solution.py:23
  6.6 6.1 %collective-permute-start.1 = (bf16[8,4096]{1,0:T(8,128)(2,1)}, bf16[8,4096]{1,0:T(8,128)(2,1)S(1)}, u32[]{:S(2)}, u32[]{:S(2)}) collective-permute-start(bf16[8,4096]{1,0:T(8,128)(2,1)} %param.4), channel_id=1, source_target_pairs={{0,0},{1,1},{2,2},{3,3},{4,4},{5,5},{6,6},{7,7},{8,8},{9,9},{10,10... | collective-permute-start | bytes 196616 | tf_op jit(solution)/shard_map/ppermute | solution.py:23
  13.3 5.8 %collective-permute-start.7 = (bf16[32,512]{1,0:T(8,128)(2,1)S(1)}, bf16[32,512]{1,0:T(8,128)(2,1)S(1)}, u32[]{:S(2)}, u32[]{:S(2)}) collective-permute-start(bf16[32,512]{1,0:T(8,128)(2,1)S(1)} %shard_map.38), channel_id=1, source_target_pairs={{12,0},{13,1},{14,2},{15,3},{8,4},{9,5},{10,6},{11,7},{4,8},{5,9},... | collective-permute-start | bytes 98312 | tf_op jit(solution)/shard_map/ppermute | solution.py:23
  16.3 4.8 %collective-permute-start.6 = (bf16[32,512]{1,0:T(8,128)(2,1)S(1)}, bf16[32,512]{1,0:T(8,128)(2,1)S(1)}, u32[]{:S(2)}, u32[]{:S(2)}) collective-permute-start(bf16[32,512]{1,0:T(8,128)(2,1)S(1)} %shard_map.38), channel_id=1, source_target_pairs={{8,0},{9,1},{10,2},{11,3},{12,4},{13,5},{14,6},{15,7},{0,8},{1,9},... | collective-permute-start | bytes 98312 | tf_op jit(solution)/shard_map/ppermute | solution.py:23
  16.3 4.8 %collective-permute-start.5 = (bf16[32,512]{1,0:T(8,128)(2,1)S(1)}, bf16[32,512]{1,0:T(8,128)(2,1)S(1)}, u32[]{:S(2)}, u32[]{:S(2)}) collective-permute-start(bf16[32,512]{1,0:T(8,128)(2,1)S(1)} %shard_map.38), channel_id=1, source_target_pairs={{4,0},{5,1},{6,2},{7,3},{0,4},{1,5},{2,6},{3,7},{12,8},{13,9},{14,... | collective-permute-start | bytes 98312 | tf_op jit(solution)/shard_map/ppermute | solution.py:23
  21.1 7.0 %collective-permute-start.9 = (bf16[4,32,512]{2,1,0:T(8,128)(2,1)S(1)}, bf16[4,32,512]{2,1,0:T(8,128)(2,1)S(1)}, u32[]{:S(2)}, u32[]{:S(2)}) collective-permute-start(bf16[4,32,512]{2,1,0:T(8,128)(2,1)S(1)} %pad_maximum_fusion.own), channel_id=1, source_target_pairs={{16,0},{17,1},{18,2},{19,3},{20,4},{21,5},{22,6},{23,7},{24,8},{25... | collective-permute-start | bytes 393224 | tf_op jit(solution)/shard_map/ppermute | solution.py:23
  23.8 5.0 %collective-permute-start.13 = (bf16[4,32,512]{2,1,0:T(8,128)(2,1)S(1)}, bf16[4,32,512]{2,1,0:T(8,128)(2,1)S(1)}, u32[]{:S(2)}, u32[]{:S(2)}) collective-permute-start(bf16[4,32,512]{2,1,0:T(8,128)(2,1)S(1)} %pad_maximum_fusion.own), channel_id=1, source_target_pairs={{2,0},{3,1},{0,2},{1,3},{6,4},{7,5},{4,6},{5,7},{10,8},{11,9},{8,1... | collective-permute-start | bytes 393224 | tf_op jit(solution)/shard_map/ppermute | solution.py:23
  25.2 5.9 %collective-permute-start.11 = (bf16[4,32,512]{2,1,0:T(8,128)(2,1)S(1)}, bf16[4,32,512]{2,1,0:T(8,128)(2,1)S(1)}, u32[]{:S(2)}, u32[]{:S(2)}) collective-permute-start(bf16[4,32,512]{2,1,0:T(8,128)(2,1)S(1)} %pad_maximum_fusion.own), channel_id=1, source_target_pairs={{18,0},{19,1},{16,2},{17,3},{22,4},{23,5},{20,6},{21,7},{26,8},{27... | collective-permute-start | bytes 393224 | tf_op jit(solution)/shard_map/ppermute | solution.py:23
  25.3 5.7 %collective-permute-start.8 = (bf16[4,32,512]{2,1,0:T(8,128)(2,1)S(1)}, bf16[4,32,512]{2,1,0:T(8,128)(2,1)S(1)}, u32[]{:S(2)}, u32[]{:S(2)}) collective-permute-start(bf16[4,32,512]{2,1,0:T(8,128)(2,1)S(1)} %pad_maximum_fusion.own), channel_id=1, source_target_pairs={{1,0},{0,1},{3,2},{2,3},{5,4},{4,5},{7,6},{6,7},{9,8},{8,9},{11,10... | collective-permute-start | bytes 393224 | tf_op jit(solution)/shard_map/ppermute | solution.py:23
  28.1 3.0 %collective-permute-start.10 = (bf16[4,32,512]{2,1,0:T(8,128)(2,1)S(1)}, bf16[4,32,512]{2,1,0:T(8,128)(2,1)S(1)}, u32[]{:S(2)}, u32[]{:S(2)}) collective-permute-start(bf16[4,32,512]{2,1,0:T(8,128)(2,1)S(1)} %collective-permute-done.9.across), channel_id=1, source_target_pairs={{1,0},{0,1},{3,2},{2,3},{5,4},{4,5},{7,6},{6,7},{9,8},{8,9},{11,10... | collective-permute-start | bytes 393224 | tf_op jit(solution)/shard_map/ppermute | solution.py:23
  28.7 3.9 %collective-permute-start.14 = (bf16[4,32,512]{2,1,0:T(8,128)(2,1)S(1)}, bf16[4,32,512]{2,1,0:T(8,128)(2,1)S(1)}, u32[]{:S(2)}, u32[]{:S(2)}) collective-permute-start(bf16[4,32,512]{2,1,0:T(8,128)(2,1)S(1)} %collective-permute-done.13.beside), channel_id=1, source_target_pairs={{1,0},{0,1},{3,2},{2,3},{5,4},{4,5},{7,6},{6,7},{9,8},{8,9},{11,10... | collective-permute-start | bytes 393224 | tf_op jit(solution)/shard_map/ppermute | solution.py:23
  31.0 1.6 %collective-permute-start.12 = (bf16[4,32,512]{2,1,0:T(8,128)(2,1)S(1)}, bf16[4,32,512]{2,1,0:T(8,128)(2,1)S(1)}, u32[]{:S(2)}, u32[]{:S(2)}) collective-permute-start(bf16[4,32,512]{2,1,0:T(8,128)(2,1)S(1)} %collective-permute-done.11.diagonal), channel_id=1, source_target_pairs={{1,0},{0,1},{3,2},{2,3},{5,4},{4,5},{7,6},{6,7},{9,8},{8,9},{11,10... | collective-permute-start | bytes 393224 | tf_op jit(solution)/shard_map/ppermute | solution.py:23

commit v4 on v3

v4 whole, which is shorter than its diff:
```python
import jax
import jax.numpy as jnp
from jax import lax
from jax.experimental import pallas as pl
from jax.experimental.pallas import tpu as pltpu
from jax.sharding import PartitionSpec as P

AXES = ("shard", "row")
F32, BF16 = jnp.float32, jnp.bfloat16


def place():
    row = lax.axis_index("row")
    return lax.axis_index("shard"), row // 4, (row // 2) % 2, row % 2


def moved(array, source_of):
    pairs = []
    for index in range(32):
        here = (index // 16, index // 4 % 4, index // 2 % 2, index % 2)
        y, z, x, c = source_of(*here)
        pairs.append((y * 16 + z * 4 + x * 2 + c, index))
    return lax.ppermute(array, AXES, pairs)


def over_core(array):
    return moved(array, lambda y, z, x, c: (y, z, x, c ^ 1))


def asked_of(turn, y, c):
    dz = turn * 3 ^ c * 1
    return dz, y ^ dz % 2


def condition_kernel(asked0, asked1, own, other, out):
    c = place()[3]
    panels, rows, width = own.shape
    for b in range(panels):
        at = slice(b * width, (b + 1) * width)
        asked = jnp.concatenate([asked0[:, at], asked1[:, at]], axis=0)
        block = jnp.concatenate([own[b], other[b]], axis=0)
        got = pltpu.roll(times(asked, block), c * rows, axis=1)
        first = [got[turn * 16 : turn * 16 + 8] for turn in range(2)]
        second = [got[turn * 16 + 8 : turn * 16 + 16] for turn in range(2)]
        mine = [jnp.where(c == 0, f, s) for f, s in zip(first, second, strict=True)]
        theirs = [jnp.where(c == 0, s, f) for f, s in zip(first, second, strict=True)]
        out[:, b * 128 : (b + 1) * 128] = jnp.concatenate(
            [mine[0], theirs[0], mine[1], theirs[1]], axis=0
        ).astype(BF16)


def take(docs, first, kept, scale, sems):
    count, width = kept.shape
    parts = 4
    rows = count // parts
    copies = [
        pltpu.make_async_copy(
            docs.at[pl.ds(first + i * rows, rows)], kept.at[pl.ds(i * rows, rows)], sems.at[i]
        )
        for i in range(parts)
    ]
    for copy in copies:
        copy.start()
    for i, copy in enumerate(copies):
        copy.wait()
        total = jnp.zeros((rows, 128), F32)
        for at in range(0, width, 128):
            dense = kept[i * rows : (i + 1) * rows, at : at + 128].astype(F32)
            total += dense * dense
        mean = jnp.sum(total, axis=1, keepdims=True) * (1.0 / width)
        value = lax.rsqrt(mean + 1e-06) * (1.0 / width**0.5)
        scale[i * rows : (i + 1) * rows] = jnp.broadcast_to(value, (rows, 128))


def upper_kernel(docs, own, after, kept, scale, own_kept, sems):
    last = pltpu.make_async_copy(own, own_kept, sems.at[4])
    last.start()
    take(docs, 0, kept, scale, sems)
    last.wait()


def lower_kernel(docs, after, kept, scale, sems):
    take(docs, kept.shape[0], kept, scale, sems)


def assemble(pieces, ready, z):
    for x, y, core, piece in pieces:
        for k in range(4):
            for turn in range(2):
                dz, dx = asked_of(turn, y, core)
                start = (z ^ k ^ dz) * 32 + (x ^ dx) * 16
                rows = pl.ds(pl.multiple_of(start, 16), 16)
                for b in range(4):
                    start = pl.multiple_of(b * 512 + (z ^ k) * 128, 128)
                    ready[rows, pl.ds(start, 128)] = piece[
                        k, turn * 16 : (turn + 1) * 16, b * 128 : (b + 1) * 128
                    ]


def columns(docs, at, rows, side):
    parts = []
    for block in range(16):
        start = pl.multiple_of(block * 256 + side * 128, 128)
        parts.append(docs[pl.ds(at, rows), pl.ds(start, 128)])
    return jnp.concatenate(parts, axis=1)


def times(left, right):
    return lax.dot_general(left, right, (((1,), (1,)), ((), ())), preferred_element_type=F32)


def near_kernel(upper, lower, own, own_c, across, across_c, out, ready):
    y, z, x, c = place()
    assemble(
        ((x, y, c, own), (x, y, 1 - c, own_c), (x, 1 - y, c, across), (x, 1 - y, 1 - c, across_c)),
        ready,
        z,
    )
    count, rows = upper.shape[0], 256
    for half, docs in enumerate((upper, lower)):
        for at in range(0, count, rows):
            out[half * count + at : half * count + at + rows] = times(
                columns(docs, at, rows, x), ready[...]
            )


def far_kernel(
    upper,
    lower,
    upper_scale,
    lower_scale,
    near,
    diagonal,
    diagonal_c,
    beside,
    beside_c,
    out,
    ready,
    made,
    sems,
):
    y, z, x, c = place()
    assemble(
        (
            (1 - x, 1 - y, c, diagonal),
            (1 - x, 1 - y, 1 - c, diagonal_c),
            (1 - x, y, c, beside),
            (1 - x, y, 1 - c, beside_c),
        ),
        ready,
        z,
    )
    count, rows = upper.shape[0], 256
    copies = []
    for half, (docs, scale) in enumerate(((upper, upper_scale), (lower, lower_scale))):
        for at in range(0, count, rows):
            here = half * count + at
            got = times(columns(docs, at, rows, 1 - x), ready[...])
            made[here : here + rows] = (near[here : here + rows] + got) * scale[at : at + rows]
            copies.append(
                pltpu.make_async_copy(
                    made.at[pl.ds(here, rows)], out.at[pl.ds(here, rows)], sems.at[len(copies)]
                )
            )
            copies[-1].start()
    for copy in copies:
        copy.wait()


def in_hbm(array):
    return pltpu.with_memory_space_constraint(array, pltpu.HBM)


def call(kernel, inputs, specs, outs, out_specs, scratch, flops, moved_bytes, limit):
    return pl.pallas_call(
        kernel,
        out_shape=outs,
        in_specs=specs,
        out_specs=out_specs,
        scratch_shapes=scratch,
        cost_estimate=pl.CostEstimate(flops=flops, bytes_accessed=moved_bytes, transcendentals=0),
        compiler_params=pltpu.CompilerParams(vmem_limit_bytes=limit),
    )(*inputs)


def grouped(documents, queries, precond):
    count, width = documents.shape
    vmem, anywhere = pl.BlockSpec(memory_space=pltpu.VMEM), pl.BlockSpec(memory_space=pltpu.HBM)
    like = jax.ShapeDtypeStruct
    mib = 1024 * 1024

    paired = over_core(queries)
    both = jnp.concatenate([queries, paired], axis=0)
    other = over_core(precond)

    def turned(turn):
        def source(y, z, x, c):
            dz, dx = asked_of(turn, y, c)
            return y, z ^ dz, x ^ dx, c

        return moved(both, source)

    asked = {turn: turned(turn) for turn in (1, 0)}
    half_docs, lanes = like((count // 2, width), BF16), like((count // 2, 128), F32)
    upper, upper_scale, own = call(
        upper_kernel,
        (in_hbm(documents), in_hbm(precond), other),
        [anywhere, anywhere, pl.BlockSpec(memory_space=pl.ANY)],
        (half_docs, lanes, like(precond.shape, BF16)),
        (vmem,) * 3,
        [pltpu.SemaphoreType.DMA((5,))],
        count * width,
        count * width,
        2 * mib,
    )
    piece = call(
        condition_kernel,
        (asked[0], asked[1], own, other),
        [vmem] * 4,
        like((32, 512), BF16),
        vmem,
        [],
        2 * 32 * 512 * 1024,
        mib,
        4 * mib,
    )
    line = jnp.stack([piece] + [moved(piece, lambda y, z, x, c: (y, z ^ k, x, c)) for k in (1, 2, 3)])
    diagonal = moved(line, lambda y, z, x, c: (y ^ 1, z, x ^ 1, c))
    beside = moved(line, lambda y, z, x, c: (y, z, x ^ 1, c))
    across = moved(line, lambda y, z, x, c: (y ^ 1, z, x, c))
    lower, lower_scale = call(
        lower_kernel,
        (in_hbm(documents), line),
        [anywhere, pl.BlockSpec(memory_space=pl.ANY)],
        (half_docs, lanes),
        (vmem,) * 2,
        [pltpu.SemaphoreType.DMA((4,))],
        count * width,
        count * width,
        2 * mib,
    )
    across, lower_scale = lax.optimization_barrier((across, lower_scale))
    line_c, across_c, beside_c, diagonal_c = map(over_core, (line, across, beside, diagonal))
    half = [pltpu.VMEM((128, width // 2), BF16)]
    near = call(
        near_kernel,
        (upper, lower, line, line_c, across, across_c),
        [vmem] * 6,
        like((count, 128), F32),
        vmem,
        half,
        count * width * 128,
        count * width,
        12 * mib,
    )
    return call(
        far_kernel,
        (upper, lower, upper_scale, lower_scale, near, diagonal, diagonal_c, beside, beside_c),
        [vmem] * 9,
        like((count, 128), F32),
        anywhere,
        [*half, pltpu.VMEM((count, 128), F32), pltpu.SemaphoreType.DMA((4,))],
        count * width * 128,
        count * width,
        12 * mib,
    )


def general(documents, queries, precond):
    panels, _, panel_width = precond.shape
    width = documents.shape[1]
    asked = lax.all_gather(queries, "row", axis=0, tiled=True)
    asked = asked.reshape(asked.shape[0], panels, panel_width)
    own = jnp.einsum("qbk,brk->bqr", asked, precond, preferred_element_type=F32).astype(BF16)
    ready = lax.all_gather(own, "row", axis=0)
    ready = ready.transpose(2, 1, 0, 3).reshape(-1, width)
    raw = jnp.dot(documents, ready.T, preferred_element_type=F32)
    dense = documents.astype(F32)
    spread = jnp.sqrt(jnp.mean(dense * dense, axis=1) + 1e-06)
    return raw / (spread[:, None] * jnp.sqrt(F32(width)))


def solution(mesh):
    fits = mesh.shape["shard"] == 2 and mesh.shape["row"] == 16
    placed = (P(AXES, None), P("row", None), P(None, "row", None))
    return jax.shard_map(
        grouped if fits else general,
        mesh=mesh,
        in_specs=placed,
        out_specs=P(AXES, None),
        check_vma=False,
    )
```

time: 35.1 us -> 34.1 us (0.972)
  waiting for transfers between devices: 9.92 us -> 7.79 us
  Pallas kernels: 8.12 us -> 9.51 us
  starting transfers between devices: 16.8 us -> 15.6 us
  local copies, waits for them, and re-layouts: 0 us -> 0.85 us
    ppermute x15 -> x14, waiting for transfers between devices: 9.92 us -> 7.79 us  [moved(): return lax.ppermute(array, AXES, pairs)]
    pallas_call x4 -> x5, Pallas kernels: 8.12 us -> 9.51 us  [call(): pl.pallas_call(kernel, out_shape=outs, in_specs=specs, out_specs=out_spec...]
    ppermute x15 -> x14, starting transfers between devices: 16.8 us -> 15.6 us  [moved(): return lax.ppermute(array, AXES, pairs)]
    unnamed x0 -> x1, local copies, waits for them, and re-layouts: none -> 0.84 us
  transfers between devices with their start and end apart: 15 -> 14, of which waited for: 7 -> 7; matrix products, arithmetic and copies ran while one was open for 0% -> 3% of each run, Pallas kernels for 15% -> 20%
where the time goes in v4:
time: 34.1 us; the launch traced here: 33.9 us
  starting transfers between devices  15.6 us (46%)
  Pallas kernels  9.51 us (28%)
  waiting for transfers between devices  7.79 us (23%)
  local copies, waits for them, and re-layouts  0.85 us (2%)
    ppermute x14, starting transfers between devices, moved(): return lax.ppermute(array, AXES, pairs)  15.6 us
    pallas_call x5, Pallas kernels, call(): pl.pallas_call(kernel, out_shape=outs, in_specs=specs, out_specs=out_spec...  9.51 us
    ppermute x14, waiting for transfers between devices, moved(): return lax.ppermute(array, AXES, pairs)  7.79 us
    unnamed x1, local copies, waits for them, and re-layouts  0.84 us
  transfers between devices with their start and end apart: 14, of which 7 were waited for; matrix products, arithmetic and copies ran while one was open for 3% of the time, Pallas kernels for 20%

profile of v4, /device:TPU:0, one launch (start us, length us, event | category | flops | bytes accessed | tf_op | source)
XLA Modules:
  0.0 33.9 jit_solution(7226492204295821254)
XLA Ops:
  0.0 0.5 %collective-permute-start.1 = (bf16[8,4096]{1,0:T(8,128)(2,1)}, bf16[8,4096]{1,0:T(8,128)(2,1)S(1)}, u32[]{:S(2)}, u32[]{:S(2)}) collective-permute-start(bf16[8,4096]{1,0:T(8,128)(2,1)} %param.4), channel_id=1, source_target_pairs={{1,0},{0,1},{3,2},{2,3},{5,4},{4,5},{7,6},{6,7},{9,8},{8,9},{11,10... | collective-permute-start | bytes 196616 | tf_op jit(solution)/shard_map/ppermute | solution.py:23
  0.5 0.1 collective-permute-start
  0.5 0.8 %constant_dynamic-update-slice_fusion.1 = bf16[16,4096]{1,0:T(8,128)(2,1)S(1)} fusion(bf16[8,4096]{1,0:T(8,128)(2,1)} %param.4), kind=kLoop, calls=%fused_computation.2 | loop fusion | bytes 131072
  1.4 0.2 collective-permute-done.1
  1.6 5.9 %collective-permute-start.3 = (bf16[16,4096]{1,0:T(8,128)(2,1)S(1)}, bf16[16,4096]{1,0:T(8,128)(2,1)S(1)}, u32[]{:S(2)}, u32[]{:S(2)}) collective-permute-start(bf16[16,4096]{1,0:T(8,128)(2,1)S(1)} %constant_dynamic-update-slice_fusion), channel_id=1, source_target_pairs={{14,0},{9,1},{12,2},{11,3},{10,4},{13,5},{8,6},{15,7},{6,8},{1,9},... | collective-permute-start | bytes 393224 | tf_op jit(solution)/shard_map/ppermute | solution.py:23
  7.4 0.7 %collective-permute-start.2 = (bf16[16,4096]{1,0:T(8,128)(2,1)S(1)}, bf16[16,4096]{1,0:T(8,128)(2,1)S(1)}, u32[]{:S(2)}, u32[]{:S(2)}) collective-permute-start(bf16[16,4096]{1,0:T(8,128)(2,1)S(1)} %constant_dynamic-update-slice_fusion), channel_id=1, source_target_pairs={{0,0},{7,1},{2,2},{5,3},{4,4},{3,5},{6,6},{1,7},{8,8},{15,9},{10,1... | collective-permute-start | bytes 393224 | tf_op jit(solution)/shard_map/ppermute | solution.py:23
  8.1 0.0 collective-permute-done.after.other
  8.1 2.7 %shard_map.37 = (bf16[512,4096]{1,0:T(8,128)(2,1)S(1)}, f32[512,128]{1,0:T(8,128)S(1)}, bf16[4,64,1024]{2,1,0:T(8,128)(2,1)S(1)}) custom-call(bf16[1024,4096]{1,0:T(8,128)(2,1)} %docs.3, bf16[4,64,1024]{2,1,0:T(8,128)(2,1)} %own.1, bf16[4,64,1024]{2,1,0:T(8,128)(2,1)S(1)} %collective-permute-done.after.other), custom_call_target="tpu_custom_call" | custom-call | flops 4194304 | bytes 4194304 | tf_op jit(solution)/shard_map/pallas_call | solution.py:175
  10.8 1.0 %collective-permute-done.3.asked1 = bf16[16,4096]{1,0:T(8,128)(2,1)S(1)} collective-permute-done((bf16[16,4096]{1,0:T(8,128)(2,1)S(1)}, bf16[16,4096]{1,0:T(8,128)(2,1)S(1)}, u32[]{:S(2)}, u32[]{:S(2)}) %collective-permute-start.3) | collective-permute-done | bytes 131104 | tf_op jit(solution)/shard_map/ppermute | solution.py:23
  11.8 0.0 collective-permute-done.2.asked0
  11.8 0.5 %shard_map.38 = bf16[32,512]{1,0:T(8,128)(2,1)S(1)} custom-call(bf16[16,4096]{1,0:T(8,128)(2,1)S(1)} %collective-permute-done.2.asked0, bf16[16,4096]{1,0:T(8,128)(2,1)S(1)} %collective-permute-done.3.asked1, bf16[4,64,1024]{2,1,0:T(8,128)(2,1)S(1)} %get-tuple-element.13.own, bf16[4,64,1024]{2,1,0:T(8,128)(2,1)S(1)} %collective-permute-done.after.other), custom_call_target="tpu_custom_call" | custom-call | flops 33554432 | bytes 1048576 | tf_op jit(solution)/shard_map/pallas_call | solution.py:175
  12.3 2.6 %collective-permute-start.6 = (bf16[32,512]{1,0:T(8,128)(2,1)S(1)}, bf16[32,512]{1,0:T(8,128)(2,1)S(1)}, u32[]{:S(2)}, u32[]{:S(2)}) collective-permute-start(bf16[32,512]{1,0:T(8,128)(2,1)S(1)} %shard_map.38), channel_id=1, source_target_pairs={{12,0},{13,1},{14,2},{15,3},{8,4},{9,5},{10,6},{11,7},{4,8},{5,9},... | collective-permute-start | bytes 98312 | tf_op jit(solution)/shard_map/ppermute | solution.py:23
  14.9 1.9 %collective-permute-start.5 = (bf16[32,512]{1,0:T(8,128)(2,1)S(1)}, bf16[32,512]{1,0:T(8,128)(2,1)S(1)}, u32[]{:S(2)}, u32[]{:S(2)}) collective-permute-start(bf16[32,512]{1,0:T(8,128)(2,1)S(1)} %shard_map.38), channel_id=1, source_target_pairs={{8,0},{9,1},{10,2},{11,3},{12,4},{13,5},{14,6},{15,7},{0,8},{1,9},... | collective-permute-start | bytes 98312 | tf_op jit(solution)/shard_map/ppermute | solution.py:23
  16.7 0.0 collective-permute-start.4
  16.7 1.5 %collective-permute-done.6 = bf16[32,512]{1,0:T(8,128)(2,1)S(1)} collective-permute-done((bf16[32,512]{1,0:T(8,128)(2,1)S(1)}, bf16[32,512]{1,0:T(8,128)(2,1)S(1)}, u32[]{:S(2)}, u32[]{:S(2)}) %collective-permute-start.6) | collective-permute-done | bytes 32800 | tf_op jit(solution)/shard_map/ppermute | solution.py:23
  18.2 1.6 %collective-permute-done.5 = bf16[32,512]{1,0:T(8,128)(2,1)S(1)} collective-permute-done((bf16[32,512]{1,0:T(8,128)(2,1)S(1)}, bf16[32,512]{1,0:T(8,128)(2,1)S(1)}, u32[]{:S(2)}, u32[]{:S(2)}) %collective-permute-start.5) | collective-permute-done | bytes 32800 | tf_op jit(solution)/shard_map/ppermute | solution.py:23
  19.9 0.8 %collective-permute-done.4 = bf16[32,512]{1,0:T(8,128)(2,1)S(1)} collective-permute-done((bf16[32,512]{1,0:T(8,128)(2,1)S(1)}, bf16[32,512]{1,0:T(8,128)(2,1)S(1)}, u32[]{:S(2)}, u32[]{:S(2)}) %collective-permute-start.4) | collective-permute-done | bytes 32800 | tf_op jit(solution)/shard_map/ppermute | solution.py:23
  20.7 1.7 %collective-permute-start.7 = (bf16[4,32,512]{2,1,0:T(8,128)(2,1)S(1)}, bf16[4,32,512]{2,1,0:T(8,128)(2,1)S(1)}, u32[]{:S(2)}, u32[]{:S(2)}) collective-permute-start(bf16[4,32,512]{2,1,0:T(8,128)(2,1)S(1)} %pad_maximum_fusion.after.own), channel_id=1, source_target_pairs={{16,0},{17,1},{18,2},{19,3},{20,4},{21,5},{22,6},{23,7},{24,8},{25... | collective-permute-start | bytes 393224 | tf_op jit(solution)/shard_map/ppermute | solution.py:23
  22.4 1.5 %collective-permute-start.12 = (bf16[4,32,512]{2,1,0:T(8,128)(2,1)S(1)}, bf16[4,32,512]{2,1,0:T(8,128)(2,1)S(1)}, u32[]{:S(2)}, u32[]{:S(2)}) collective-permute-start(bf16[4,32,512]{2,1,0:T(8,128)(2,1)S(1)} %pad_maximum_fusion.after.own), channel_id=1, source_target_pairs={{2,0},{3,1},{0,2},{1,3},{6,4},{7,5},{4,6},{5,7},{10,8},{11,9},{8,1... | collective-permute-start | bytes 393224 | tf_op jit(solution)/shard_map/ppermute | solution.py:23
  23.9 0.3 collective-permute-start.10
  24.2 0.0 collective-permute-start.8
  24.2 2.5 %shard_map.39 = (bf16[512,4096]{1,0:T(8,128)(2,1)S(1)}, f32[512,128]{1,0:T(8,128)S(1)}) custom-call(bf16[1024,4096]{1,0:T(8,128)(2,1)} %docs.3, bf16[4,32,512]{2,1,0:T(8,128)(2,1)S(1)} %pad_maximum_fusion.after.own), custom_call_target="tpu_custom_call" | custom-call | flops 4194304 | bytes 4194304 | tf_op jit(solution)/shard_map/pallas_call | solution.py:175
  26.7 0.0 collective-permute-done.7.across
  26.8 0.6 %collective-permute-start.9 = (bf16[4,32,512]{2,1,0:T(8,128)(2,1)S(1)}, bf16[4,32,512]{2,1,0:T(8,128)(2,1)S(1)}, u32[]{:S(2)}, u32[]{:S(2)}) collective-permute-start(bf16[4,32,512]{2,1,0:T(8,128)(2,1)S(1)} %collective-permute-done.7.across), channel_id=1, source_target_pairs={{1,0},{0,1},{3,2},{2,3},{5,4},{4,5},{7,6},{6,7},{9,8},{8,9},{11,10... | collective-permute-start | bytes 393224 | tf_op jit(solution)/shard_map/ppermute | solution.py:23
  27.3 1.5 %collective-permute-done.12.beside = bf16[4,32,512]{2,1,0:T(8,128)(2,1)S(1)} collective-permute-done((bf16[4,32,512]{2,1,0:T(8,128)(2,1)S(1)}, bf16[4,32,512]{2,1,0:T(8,128)(2,1)S(1)}, u32[]{:S(2)}, u32[]{:S(2)}) %collective-permute-start.12) | collective-permute-done | bytes 131104 | tf_op jit(solution)/shard_map/ppermute | solution.py:23
  28.8 0.0 collective-permute-start.13
  28.8 1.2 %collective-permute-done.10.diagonal = bf16[4,32,512]{2,1,0:T(8,128)(2,1)S(1)} collective-permute-done((bf16[4,32,512]{2,1,0:T(8,128)(2,1)S(1)}, bf16[4,32,512]{2,1,0:T(8,128)(2,1)S(1)}, u32[]{:S(2)}, u32[]{:S(2)}) %collective-permute-start.10) | collective-permute-done | bytes 131104 | tf_op jit(solution)/shard_map/ppermute | solution.py:23
  30.0 0.0 collective-permute-start.11
  30.0 0.0 collective-permute-done.8.own_c
  30.0 0.0 collective-permute-done.9.across_c
  30.0 1.5 %shard_map.40.near = f32[1024,128]{1,0:T(8,128)S(1)} custom-call(bf16[512,4096]{1,0:T(8,128)(2,1)S(1)} %get-tuple-element.12.upper, bf16[512,4096]{1,0:T(8,128)(2,1)S(1)} %get-tuple-element.14.lower, bf16[4,32,512]{2,1,0:T(8,128)(2,1)S(1)} %pad_maximum_fusion.after.own, bf16[4,32,512]{2,1,0:T(8,128)(2,1)S(1)} %collective-permute-done.8.own_c, ...), custom_call_target="tpu_custom_call" | custom-call | flops 536870912 | bytes 4194304 | tf_op jit(solution)/shard_map/pallas_call | solution.py:175
  31.6 0.0 collective-permute-done.13.beside_c
  31.6 0.0 collective-permute-done.11.diagonal_c
  31.6 2.3 %shard_map.41 = f32[1024,128]{1,0:T(8,128)} custom-call(bf16[512,4096]{1,0:T(8,128)(2,1)S(1)} %get-tuple-element.12.upper, bf16[512,4096]{1,0:T(8,128)(2,1)S(1)} %get-tuple-element.14.lower, f32[512,128]{1,0:T(8,128)S(1)} %get-tuple-element.15.upper_scale, f32[512,128]{1,0:T(8,128)S(1)} %get-tuple-element.17.lower_scale, f32[1024,128]{1,0:T(8,128)S(1)} %shard_map.40.near, ...), custom_call_target="tpu_custom_call" | custom-call | flops 536870912 | bytes 4194304 | tf_op jit(solution)/shard_map/pallas_call | solution.py:175
  (2 shorter events, 0.0 us)
Async XLA Ops:
  0.0 1.6 %collective-permute-start.1 = (bf16[8,4096]{1,0:T(8,128)(2,1)}, bf16[8,4096]{1,0:T(8,128)(2,1)S(1)}, u32[]{:S(2)}, u32[]{:S(2)}) collective-permute-start(bf16[8,4096]{1,0:T(8,128)(2,1)} %param.4), channel_id=1, source_target_pairs={{1,0},{0,1},{3,2},{2,3},{5,4},{4,5},{7,6},{6,7},{9,8},{8,9},{11,10... | collective-permute-start | bytes 196616 | tf_op jit(solution)/shard_map/ppermute | solution.py:23
  0.5 7.7 %collective-permute-start = (bf16[4,64,1024]{2,1,0:T(8,128)(2,1)}, bf16[4,64,1024]{2,1,0:T(8,128)(2,1)S(1)}, u32[]{:S(2)}, u32[]{:S(2)}) collective-permute-start(bf16[4,64,1024]{2,1,0:T(8,128)(2,1)} %own.1), channel_id=1, source_target_pairs={{1,0},{0,1},{3,2},{2,3},{5,4},{4,5},{7,6},{6,7},{9,8},{8,9},{11,10... | collective-permute-start | bytes 1572872 | tf_op jit(solution)/shard_map/ppermute | solution.py:23
  1.6 10.2 %collective-permute-start.3 = (bf16[16,4096]{1,0:T(8,128)(2,1)S(1)}, bf16[16,4096]{1,0:T(8,128)(2,1)S(1)}, u32[]{:S(2)}, u32[]{:S(2)}) collective-permute-start(bf16[16,4096]{1,0:T(8,128)(2,1)S(1)} %constant_dynamic-update-slice_fusion), channel_id=1, source_target_pairs={{14,0},{9,1},{12,2},{11,3},{10,4},{13,5},{8,6},{15,7},{6,8},{1,9},... | collective-permute-start | bytes 393224 | tf_op jit(solution)/shard_map/ppermute | solution.py:23
  7.4 4.3 %collective-permute-start.2 = (bf16[16,4096]{1,0:T(8,128)(2,1)S(1)}, bf16[16,4096]{1,0:T(8,128)(2,1)S(1)}, u32[]{:S(2)}, u32[]{:S(2)}) collective-permute-start(bf16[16,4096]{1,0:T(8,128)(2,1)S(1)} %constant_dynamic-update-slice_fusion), channel_id=1, source_target_pairs={{0,0},{7,1},{2,2},{5,3},{4,4},{3,5},{6,6},{1,7},{8,8},{15,9},{10,1... | collective-permute-start | bytes 393224 | tf_op jit(solution)/shard_map/ppermute | solution.py:23
  12.3 5.9 %collective-permute-start.6 = (bf16[32,512]{1,0:T(8,128)(2,1)S(1)}, bf16[32,512]{1,0:T(8,128)(2,1)S(1)}, u32[]{:S(2)}, u32[]{:S(2)}) collective-permute-start(bf16[32,512]{1,0:T(8,128)(2,1)S(1)} %shard_map.38), channel_id=1, source_target_pairs={{12,0},{13,1},{14,2},{15,3},{8,4},{9,5},{10,6},{11,7},{4,8},{5,9},... | collective-permute-start | bytes 98312 | tf_op jit(solution)/shard_map/ppermute | solution.py:23
  14.9 5.0 %collective-permute-start.5 = (bf16[32,512]{1,0:T(8,128)(2,1)S(1)}, bf16[32,512]{1,0:T(8,128)(2,1)S(1)}, u32[]{:S(2)}, u32[]{:S(2)}) collective-permute-start(bf16[32,512]{1,0:T(8,128)(2,1)S(1)} %shard_map.38), channel_id=1, source_target_pairs={{8,0},{9,1},{10,2},{11,3},{12,4},{13,5},{14,6},{15,7},{0,8},{1,9},... | collective-permute-start | bytes 98312 | tf_op jit(solution)/shard_map/ppermute | solution.py:23
  16.7 3.9 %collective-permute-start.4 = (bf16[32,512]{1,0:T(8,128)(2,1)S(1)}, bf16[32,512]{1,0:T(8,128)(2,1)S(1)}, u32[]{:S(2)}, u32[]{:S(2)}) collective-permute-start(bf16[32,512]{1,0:T(8,128)(2,1)S(1)} %shard_map.38), channel_id=1, source_target_pairs={{4,0},{5,1},{6,2},{7,3},{0,4},{1,5},{2,6},{3,7},{12,8},{13,9},{14,... | collective-permute-start | bytes 98312 | tf_op jit(solution)/shard_map/ppermute | solution.py:23
  20.7 6.1 %collective-permute-start.7 = (bf16[4,32,512]{2,1,0:T(8,128)(2,1)S(1)}, bf16[4,32,512]{2,1,0:T(8,128)(2,1)S(1)}, u32[]{:S(2)}, u32[]{:S(2)}) collective-permute-start(bf16[4,32,512]{2,1,0:T(8,128)(2,1)S(1)} %pad_maximum_fusion.after.own), channel_id=1, source_target_pairs={{16,0},{17,1},{18,2},{19,3},{20,4},{21,5},{22,6},{23,7},{24,8},{25... | collective-permute-start | bytes 393224 | tf_op jit(solution)/shard_map/ppermute | solution.py:23
  22.4 6.4 %collective-permute-start.12 = (bf16[4,32,512]{2,1,0:T(8,128)(2,1)S(1)}, bf16[4,32,512]{2,1,0:T(8,128)(2,1)S(1)}, u32[]{:S(2)}, u32[]{:S(2)}) collective-permute-start(bf16[4,32,512]{2,1,0:T(8,128)(2,1)S(1)} %pad_maximum_fusion.after.own), channel_id=1, source_target_pairs={{2,0},{3,1},{0,2},{1,3},{6,4},{7,5},{4,6},{5,7},{10,8},{11,9},{8,1... | collective-permute-start | bytes 393224 | tf_op jit(solution)/shard_map/ppermute | solution.py:23
  23.9 6.1 %collective-permute-start.10 = (bf16[4,32,512]{2,1,0:T(8,128)(2,1)S(1)}, bf16[4,32,512]{2,1,0:T(8,128)(2,1)S(1)}, u32[]{:S(2)}, u32[]{:S(2)}) collective-permute-start(bf16[4,32,512]{2,1,0:T(8,128)(2,1)S(1)} %pad_maximum_fusion.after.own), channel_id=1, source_target_pairs={{18,0},{19,1},{16,2},{17,3},{22,4},{23,5},{20,6},{21,7},{26,8},{27... | collective-permute-start | bytes 393224 | tf_op jit(solution)/shard_map/ppermute | solution.py:23
  24.2 5.8 %collective-permute-start.8 = (bf16[4,32,512]{2,1,0:T(8,128)(2,1)S(1)}, bf16[4,32,512]{2,1,0:T(8,128)(2,1)S(1)}, u32[]{:S(2)}, u32[]{:S(2)}) collective-permute-start(bf16[4,32,512]{2,1,0:T(8,128)(2,1)S(1)} %pad_maximum_fusion.after.own), channel_id=1, source_target_pairs={{1,0},{0,1},{3,2},{2,3},{5,4},{4,5},{7,6},{6,7},{9,8},{8,9},{11,10... | collective-permute-start | bytes 393224 | tf_op jit(solution)/shard_map/ppermute | solution.py:23
  26.8 3.3 %collective-permute-start.9 = (bf16[4,32,512]{2,1,0:T(8,128)(2,1)S(1)}, bf16[4,32,512]{2,1,0:T(8,128)(2,1)S(1)}, u32[]{:S(2)}, u32[]{:S(2)}) collective-permute-start(bf16[4,32,512]{2,1,0:T(8,128)(2,1)S(1)} %collective-permute-done.7.across), channel_id=1, source_target_pairs={{1,0},{0,1},{3,2},{2,3},{5,4},{4,5},{7,6},{6,7},{9,8},{8,9},{11,10... | collective-permute-start | bytes 393224 | tf_op jit(solution)/shard_map/ppermute | solution.py:23
  28.8 2.7 %collective-permute-start.13 = (bf16[4,32,512]{2,1,0:T(8,128)(2,1)S(1)}, bf16[4,32,512]{2,1,0:T(8,128)(2,1)S(1)}, u32[]{:S(2)}, u32[]{:S(2)}) collective-permute-start(bf16[4,32,512]{2,1,0:T(8,128)(2,1)S(1)} %collective-permute-done.12.beside), channel_id=1, source_target_pairs={{1,0},{0,1},{3,2},{2,3},{5,4},{4,5},{7,6},{6,7},{9,8},{8,9},{11,10... | collective-permute-start | bytes 393224 | tf_op jit(solution)/shard_map/ppermute | solution.py:23
  30.0 1.5 %collective-permute-start.11 = (bf16[4,32,512]{2,1,0:T(8,128)(2,1)S(1)}, bf16[4,32,512]{2,1,0:T(8,128)(2,1)S(1)}, u32[]{:S(2)}, u32[]{:S(2)}) collective-permute-start(bf16[4,32,512]{2,1,0:T(8,128)(2,1)S(1)} %collective-permute-done.10.diagonal), channel_id=1, source_target_pairs={{1,0},{0,1},{3,2},{2,3},{5,4},{4,5},{7,6},{6,7},{9,8},{8,9},{11,10... | collective-permute-start | bytes 393224 | tf_op jit(solution)/shard_map/ppermute | solution.py:23

commit v5 on v4

--- a/solution.py
+++ b/solution.py
@@ -84,32 +84,39 @@
 
 
 def assemble(pieces, ready, z):
-    for x, y, core, piece in pieces:
-        for k in range(4):
-            for turn in range(2):
-                dz, dx = asked_of(turn, y, core)
-                start = (z ^ k ^ dz) * 32 + (x ^ dx) * 16
-                rows = pl.ds(pl.multiple_of(start, 16), 16)
-                for b in range(4):
-                    start = pl.multiple_of(b * 512 + (z ^ k) * 128, 128)
-                    ready[rows, pl.ds(start, 128)] = piece[
+    for b, panel in enumerate(ready):
+        for x, y, core, piece in pieces:
+            for k in range(4):
+                for turn in range(2):
+                    dz, dx = asked_of(turn, y, core)
+                    start = (z ^ k ^ dz) * 32 + (x ^ dx) * 16
+                    rows = pl.ds(pl.multiple_of(start, 16), 16)
+                    start = pl.multiple_of((z ^ k) * 128, 128)
+                    panel[rows, pl.ds(start, 128)] = piece[
                         k, turn * 16 : (turn + 1) * 16, b * 128 : (b + 1) * 128
                     ]
 
 
-def columns(docs, at, rows, side):
+def columns(docs, at, rows, side, b):
     parts = []
-    for block in range(16):
+    for block in range(b * 4, b * 4 + 4):
         start = pl.multiple_of(block * 256 + side * 128, 128)
         parts.append(docs[pl.ds(at, rows), pl.ds(start, 128)])
     return jnp.concatenate(parts, axis=1)
 
 
+def product(docs, at, rows, side, ready):
+    total = times(columns(docs, at, rows, side, 0), ready[0][...])
+    for b in range(1, len(ready)):
+        total += times(columns(docs, at, rows, side, b), ready[b][...])
+    return total
+
+
 def times(left, right):
     return lax.dot_general(left, right, (((1,), (1,)), ((), ())), preferred_element_type=F32)
 
 
-def near_kernel(upper, lower, own, own_c, across, across_c, out, ready):
+def near_kernel(upper, lower, own, own_c, across, across_c, out, *ready):
     y, z, x, c = place()
     assemble(
         ((x, y, c, own), (x, y, 1 - c, own_c), (x, 1 - y, c, across), (x, 1 - y, 1 - c, across_c)),
@@ -119,9 +126,7 @@
     count, rows = upper.shape[0], 256
     for half, docs in enumerate((upper, lower)):
         for at in range(0, count, rows):
-            out[half * count + at : half * count + at + rows] = times(
-                columns(docs, at, rows, x), ready[...]
-            )
+            out[half * count + at : half * count + at + rows] = product(docs, at, rows, x, ready)
 
 
 def far_kernel(
@@ -135,9 +140,9 @@
     beside,
     beside_c,
     out,
-    ready,
     made,
     sems,
+    *ready,
 ):
     y, z, x, c = place()
     assemble(
@@ -155,7 +160,7 @@
     for half, (docs, scale) in enumerate(((upper, upper_scale), (lower, lower_scale))):
         for at in range(0, count, rows):
             here = half * count + at
-            got = times(columns(docs, at, rows, 1 - x), ready[...])
+            got = product(docs, at, rows, 1 - x, ready)
             made[here : here + rows] = (near[here : here + rows] + got) * scale[at : at + rows]
             copies.append(
                 pltpu.make_async_copy(
@@ -241,7 +246,7 @@
     )
     across, lower_scale = lax.optimization_barrier((across, lower_scale))
     line_c, across_c, beside_c, diagonal_c = map(over_core, (line, across, beside, diagonal))
-    half = [pltpu.VMEM((128, width // 2), BF16)]
+    half = [pltpu.VMEM((128, width // 8), BF16)] * 4
     near = call(
         near_kernel,
         (upper, lower, line, line_c, across, across_c),
@@ -259,7 +264,7 @@
         [vmem] * 9,
         like((count, 128), F32),
         anywhere,
-        [*half, pltpu.VMEM((count, 128), F32), pltpu.SemaphoreType.DMA((4,))],
+        [pltpu.VMEM((count, 128), F32), pltpu.SemaphoreType.DMA((8,)), *half],
         count * width * 128,
         count * width,
         12 * mib,

time: 34.1 us -> 34 us (level)
  no operation moved by 1% of the time
where the time goes in v5:
time: 34 us; the launch traced here: 33.8 us
  starting transfers between devices  15.6 us (46%)
  Pallas kernels  9.46 us (28%)
  waiting for transfers between devices  7.79 us (23%)
  local copies, waits for them, and re-layouts  0.85 us (2%)
    ppermute x14, starting transfers between devices, moved(): return lax.ppermute(array, AXES, pairs)  15.6 us
    pallas_call x5, Pallas kernels, call(): pl.pallas_call(kernel, out_shape=outs, in_specs=specs, out_specs=out_spec...  9.46 us
    ppermute x14, waiting for transfers between devices, moved(): return lax.ppermute(array, AXES, pairs)  7.79 us
    unnamed x1, local copies, waits for them, and re-layouts  0.84 us
  transfers between devices with their start and end apart: 14, of which 7 were waited for; matrix products, arithmetic and copies ran while one was open for 3% of the time, Pallas kernels for 20%

profile of v5, /device:TPU:0, one launch (start us, length us, event | category | flops | bytes accessed | tf_op | source)
XLA Modules:
  0.0 33.8 jit_solution(3348547827312413015)
XLA Ops:
  0.0 0.5 %collective-permute-start.1 = (bf16[8,4096]{1,0:T(8,128)(2,1)}, bf16[8,4096]{1,0:T(8,128)(2,1)S(1)}, u32[]{:S(2)}, u32[]{:S(2)}) collective-permute-start(bf16[8,4096]{1,0:T(8,128)(2,1)} %param.4), channel_id=1, source_target_pairs={{1,0},{0,1},{3,2},{2,3},{5,4},{4,5},{7,6},{6,7},{9,8},{8,9},{11,10... | collective-permute-start | bytes 196616 | tf_op jit(solution)/shard_map/ppermute | solution.py:23
  0.5 0.1 collective-permute-start
  0.5 0.8 %constant_dynamic-update-slice_fusion.1 = bf16[16,4096]{1,0:T(8,128)(2,1)S(1)} fusion(bf16[8,4096]{1,0:T(8,128)(2,1)} %param.4), kind=kLoop, calls=%fused_computation.2 | loop fusion | bytes 131072
  1.4 0.2 collective-permute-done.1
  1.6 5.9 %collective-permute-start.3 = (bf16[16,4096]{1,0:T(8,128)(2,1)S(1)}, bf16[16,4096]{1,0:T(8,128)(2,1)S(1)}, u32[]{:S(2)}, u32[]{:S(2)}) collective-permute-start(bf16[16,4096]{1,0:T(8,128)(2,1)S(1)} %constant_dynamic-update-slice_fusion), channel_id=1, source_target_pairs={{14,0},{9,1},{12,2},{11,3},{10,4},{13,5},{8,6},{15,7},{6,8},{1,9},... | collective-permute-start | bytes 393224 | tf_op jit(solution)/shard_map/ppermute | solution.py:23
  7.4 0.7 %collective-permute-start.2 = (bf16[16,4096]{1,0:T(8,128)(2,1)S(1)}, bf16[16,4096]{1,0:T(8,128)(2,1)S(1)}, u32[]{:S(2)}, u32[]{:S(2)}) collective-permute-start(bf16[16,4096]{1,0:T(8,128)(2,1)S(1)} %constant_dynamic-update-slice_fusion), channel_id=1, source_target_pairs={{0,0},{7,1},{2,2},{5,3},{4,4},{3,5},{6,6},{1,7},{8,8},{15,9},{10,1... | collective-permute-start | bytes 393224 | tf_op jit(solution)/shard_map/ppermute | solution.py:23
  8.1 0.0 collective-permute-done.after.other
  8.1 2.7 %shard_map.37 = (bf16[512,4096]{1,0:T(8,128)(2,1)S(1)}, f32[512,128]{1,0:T(8,128)S(1)}, bf16[4,64,1024]{2,1,0:T(8,128)(2,1)S(1)}) custom-call(bf16[1024,4096]{1,0:T(8,128)(2,1)} %docs.3, bf16[4,64,1024]{2,1,0:T(8,128)(2,1)} %own.1, bf16[4,64,1024]{2,1,0:T(8,128)(2,1)S(1)} %collective-permute-done.after.other), custom_call_target="tpu_custom_call" | custom-call | flops 4194304 | bytes 4194304 | tf_op jit(solution)/shard_map/pallas_call | solution.py:180
  10.8 1.0 %collective-permute-done.3.asked1 = bf16[16,4096]{1,0:T(8,128)(2,1)S(1)} collective-permute-done((bf16[16,4096]{1,0:T(8,128)(2,1)S(1)}, bf16[16,4096]{1,0:T(8,128)(2,1)S(1)}, u32[]{:S(2)}, u32[]{:S(2)}) %collective-permute-start.3) | collective-permute-done | bytes 131104 | tf_op jit(solution)/shard_map/ppermute | solution.py:23
  11.8 0.0 collective-permute-done.2.asked0
  11.8 0.5 %shard_map.38 = bf16[32,512]{1,0:T(8,128)(2,1)S(1)} custom-call(bf16[16,4096]{1,0:T(8,128)(2,1)S(1)} %collective-permute-done.2.asked0, bf16[16,4096]{1,0:T(8,128)(2,1)S(1)} %collective-permute-done.3.asked1, bf16[4,64,1024]{2,1,0:T(8,128)(2,1)S(1)} %get-tuple-element.13.own, bf16[4,64,1024]{2,1,0:T(8,128)(2,1)S(1)} %collective-permute-done.after.other), custom_call_target="tpu_custom_call" | custom-call | flops 33554432 | bytes 1048576 | tf_op jit(solution)/shard_map/pallas_call | solution.py:180
  12.3 2.6 %collective-permute-start.6 = (bf16[32,512]{1,0:T(8,128)(2,1)S(1)}, bf16[32,512]{1,0:T(8,128)(2,1)S(1)}, u32[]{:S(2)}, u32[]{:S(2)}) collective-permute-start(bf16[32,512]{1,0:T(8,128)(2,1)S(1)} %shard_map.38), channel_id=1, source_target_pairs={{12,0},{13,1},{14,2},{15,3},{8,4},{9,5},{10,6},{11,7},{4,8},{5,9},... | collective-permute-start | bytes 98312 | tf_op jit(solution)/shard_map/ppermute | solution.py:23
  14.9 1.9 %collective-permute-start.5 = (bf16[32,512]{1,0:T(8,128)(2,1)S(1)}, bf16[32,512]{1,0:T(8,128)(2,1)S(1)}, u32[]{:S(2)}, u32[]{:S(2)}) collective-permute-start(bf16[32,512]{1,0:T(8,128)(2,1)S(1)} %shard_map.38), channel_id=1, source_target_pairs={{8,0},{9,1},{10,2},{11,3},{12,4},{13,5},{14,6},{15,7},{0,8},{1,9},... | collective-permute-start | bytes 98312 | tf_op jit(solution)/shard_map/ppermute | solution.py:23
  16.7 0.0 collective-permute-start.4
  16.7 1.5 %collective-permute-done.6 = bf16[32,512]{1,0:T(8,128)(2,1)S(1)} collective-permute-done((bf16[32,512]{1,0:T(8,128)(2,1)S(1)}, bf16[32,512]{1,0:T(8,128)(2,1)S(1)}, u32[]{:S(2)}, u32[]{:S(2)}) %collective-permute-start.6) | collective-permute-done | bytes 32800 | tf_op jit(solution)/shard_map/ppermute | solution.py:23
  18.2 1.6 %collective-permute-done.5 = bf16[32,512]{1,0:T(8,128)(2,1)S(1)} collective-permute-done((bf16[32,512]{1,0:T(8,128)(2,1)S(1)}, bf16[32,512]{1,0:T(8,128)(2,1)S(1)}, u32[]{:S(2)}, u32[]{:S(2)}) %collective-permute-start.5) | collective-permute-done | bytes 32800 | tf_op jit(solution)/shard_map/ppermute | solution.py:23
  19.9 0.8 %collective-permute-done.4 = bf16[32,512]{1,0:T(8,128)(2,1)S(1)} collective-permute-done((bf16[32,512]{1,0:T(8,128)(2,1)S(1)}, bf16[32,512]{1,0:T(8,128)(2,1)S(1)}, u32[]{:S(2)}, u32[]{:S(2)}) %collective-permute-start.4) | collective-permute-done | bytes 32800 | tf_op jit(solution)/shard_map/ppermute | solution.py:23
  20.7 1.7 %collective-permute-start.7 = (bf16[4,32,512]{2,1,0:T(8,128)(2,1)S(1)}, bf16[4,32,512]{2,1,0:T(8,128)(2,1)S(1)}, u32[]{:S(2)}, u32[]{:S(2)}) collective-permute-start(bf16[4,32,512]{2,1,0:T(8,128)(2,1)S(1)} %pad_maximum_fusion.after.own), channel_id=1, source_target_pairs={{16,0},{17,1},{18,2},{19,3},{20,4},{21,5},{22,6},{23,7},{24,8},{25... | collective-permute-start | bytes 393224 | tf_op jit(solution)/shard_map/ppermute | solution.py:23
  22.4 1.5 %collective-permute-start.12 = (bf16[4,32,512]{2,1,0:T(8,128)(2,1)S(1)}, bf16[4,32,512]{2,1,0:T(8,128)(2,1)S(1)}, u32[]{:S(2)}, u32[]{:S(2)}) collective-permute-start(bf16[4,32,512]{2,1,0:T(8,128)(2,1)S(1)} %pad_maximum_fusion.after.own), channel_id=1, source_target_pairs={{2,0},{3,1},{0,2},{1,3},{6,4},{7,5},{4,6},{5,7},{10,8},{11,9},{8,1... | collective-permute-start | bytes 393224 | tf_op jit(solution)/shard_map/ppermute | solution.py:23
  23.9 0.3 collective-permute-start.10
  24.2 0.0 collective-permute-start.8
  24.2 2.5 %shard_map.39 = (bf16[512,4096]{1,0:T(8,128)(2,1)S(1)}, f32[512,128]{1,0:T(8,128)S(1)}) custom-call(bf16[1024,4096]{1,0:T(8,128)(2,1)} %docs.3, bf16[4,32,512]{2,1,0:T(8,128)(2,1)S(1)} %pad_maximum_fusion.after.own), custom_call_target="tpu_custom_call" | custom-call | flops 4194304 | bytes 4194304 | tf_op jit(solution)/shard_map/pallas_call | solution.py:180
  26.7 0.0 collective-permute-done.7.across
  26.8 0.6 %collective-permute-start.9 = (bf16[4,32,512]{2,1,0:T(8,128)(2,1)S(1)}, bf16[4,32,512]{2,1,0:T(8,128)(2,1)S(1)}, u32[]{:S(2)}, u32[]{:S(2)}) collective-permute-start(bf16[4,32,512]{2,1,0:T(8,128)(2,1)S(1)} %collective-permute-done.7.across), channel_id=1, source_target_pairs={{1,0},{0,1},{3,2},{2,3},{5,4},{4,5},{7,6},{6,7},{9,8},{8,9},{11,10... | collective-permute-start | bytes 393224 | tf_op jit(solution)/shard_map/ppermute | solution.py:23
  27.3 1.5 %collective-permute-done.12.beside = bf16[4,32,512]{2,1,0:T(8,128)(2,1)S(1)} collective-permute-done((bf16[4,32,512]{2,1,0:T(8,128)(2,1)S(1)}, bf16[4,32,512]{2,1,0:T(8,128)(2,1)S(1)}, u32[]{:S(2)}, u32[]{:S(2)}) %collective-permute-start.12) | collective-permute-done | bytes 131104 | tf_op jit(solution)/shard_map/ppermute | solution.py:23
  28.8 0.0 collective-permute-start.13
  28.8 1.2 %collective-permute-done.10.diagonal = bf16[4,32,512]{2,1,0:T(8,128)(2,1)S(1)} collective-permute-done((bf16[4,32,512]{2,1,0:T(8,128)(2,1)S(1)}, bf16[4,32,512]{2,1,0:T(8,128)(2,1)S(1)}, u32[]{:S(2)}, u32[]{:S(2)}) %collective-permute-start.10) | collective-permute-done | bytes 131104 | tf_op jit(solution)/shard_map/ppermute | solution.py:23
  30.0 0.0 collective-permute-start.11
  30.0 0.0 collective-permute-done.8.own_c
  30.0 0.0 collective-permute-done.9.across_c
  30.0 1.4 %shard_map.40.near = f32[1024,128]{1,0:T(8,128)S(1)} custom-call(bf16[512,4096]{1,0:T(8,128)(2,1)S(1)} %get-tuple-element.12.upper, bf16[512,4096]{1,0:T(8,128)(2,1)S(1)} %get-tuple-element.14.lower, bf16[4,32,512]{2,1,0:T(8,128)(2,1)S(1)} %pad_maximum_fusion.after.own, bf16[4,32,512]{2,1,0:T(8,128)(2,1)S(1)} %collective-permute-done.8.own_c, ...), custom_call_target="tpu_custom_call" | custom-call | flops 536870912 | bytes 4194304 | tf_op jit(solution)/shard_map/pallas_call | solution.py:180
  31.5 0.0 collective-permute-done.13.beside_c
  31.5 0.0 collective-permute-done.11.diagonal_c
  31.5 2.3 %shard_map.41 = f32[1024,128]{1,0:T(8,128)} custom-call(bf16[512,4096]{1,0:T(8,128)(2,1)S(1)} %get-tuple-element.12.upper, bf16[512,4096]{1,0:T(8,128)(2,1)S(1)} %get-tuple-element.14.lower, f32[512,128]{1,0:T(8,128)S(1)} %get-tuple-element.15.upper_scale, f32[512,128]{1,0:T(8,128)S(1)} %get-tuple-element.17.lower_scale, f32[1024,128]{1,0:T(8,128)S(1)} %shard_map.40.near, ...), custom_call_target="tpu_custom_call" | custom-call | flops 536870912 | bytes 4194304 | tf_op jit(solution)/shard_map/pallas_call | solution.py:180
  (2 shorter events, 0.0 us)
Async XLA Ops:
  0.0 1.6 %collective-permute-start.1 = (bf16[8,4096]{1,0:T(8,128)(2,1)}, bf16[8,4096]{1,0:T(8,128)(2,1)S(1)}, u32[]{:S(2)}, u32[]{:S(2)}) collective-permute-start(bf16[8,4096]{1,0:T(8,128)(2,1)} %param.4), channel_id=1, source_target_pairs={{1,0},{0,1},{3,2},{2,3},{5,4},{4,5},{7,6},{6,7},{9,8},{8,9},{11,10... | collective-permute-start | bytes 196616 | tf_op jit(solution)/shard_map/ppermute | solution.py:23
  0.5 7.7 %collective-permute-start = (bf16[4,64,1024]{2,1,0:T(8,128)(2,1)}, bf16[4,64,1024]{2,1,0:T(8,128)(2,1)S(1)}, u32[]{:S(2)}, u32[]{:S(2)}) collective-permute-start(bf16[4,64,1024]{2,1,0:T(8,128)(2,1)} %own.1), channel_id=1, source_target_pairs={{1,0},{0,1},{3,2},{2,3},{5,4},{4,5},{7,6},{6,7},{9,8},{8,9},{11,10... | collective-permute-start | bytes 1572872 | tf_op jit(solution)/shard_map/ppermute | solution.py:23
  1.6 10.2 %collective-permute-start.3 = (bf16[16,4096]{1,0:T(8,128)(2,1)S(1)}, bf16[16,4096]{1,0:T(8,128)(2,1)S(1)}, u32[]{:S(2)}, u32[]{:S(2)}) collective-permute-start(bf16[16,4096]{1,0:T(8,128)(2,1)S(1)} %constant_dynamic-update-slice_fusion), channel_id=1, source_target_pairs={{14,0},{9,1},{12,2},{11,3},{10,4},{13,5},{8,6},{15,7},{6,8},{1,9},... | collective-permute-start | bytes 393224 | tf_op jit(solution)/shard_map/ppermute | solution.py:23
  7.4 4.3 %collective-permute-start.2 = (bf16[16,4096]{1,0:T(8,128)(2,1)S(1)}, bf16[16,4096]{1,0:T(8,128)(2,1)S(1)}, u32[]{:S(2)}, u32[]{:S(2)}) collective-permute-start(bf16[16,4096]{1,0:T(8,128)(2,1)S(1)} %constant_dynamic-update-slice_fusion), channel_id=1, source_target_pairs={{0,0},{7,1},{2,2},{5,3},{4,4},{3,5},{6,6},{1,7},{8,8},{15,9},{10,1... | collective-permute-start | bytes 393224 | tf_op jit(solution)/shard_map/ppermute | solution.py:23
  12.3 5.9 %collective-permute-start.6 = (bf16[32,512]{1,0:T(8,128)(2,1)S(1)}, bf16[32,512]{1,0:T(8,128)(2,1)S(1)}, u32[]{:S(2)}, u32[]{:S(2)}) collective-permute-start(bf16[32,512]{1,0:T(8,128)(2,1)S(1)} %shard_map.38), channel_id=1, source_target_pairs={{12,0},{13,1},{14,2},{15,3},{8,4},{9,5},{10,6},{11,7},{4,8},{5,9},... | collective-permute-start | bytes 98312 | tf_op jit(solution)/shard_map/ppermute | solution.py:23
  14.9 5.0 %collective-permute-start.5 = (bf16[32,512]{1,0:T(8,128)(2,1)S(1)}, bf16[32,512]{1,0:T(8,128)(2,1)S(1)}, u32[]{:S(2)}, u32[]{:S(2)}) collective-permute-start(bf16[32,512]{1,0:T(8,128)(2,1)S(1)} %shard_map.38), channel_id=1, source_target_pairs={{8,0},{9,1},{10,2},{11,3},{12,4},{13,5},{14,6},{15,7},{0,8},{1,9},... | collective-permute-start | bytes 98312 | tf_op jit(solution)/shard_map/ppermute | solution.py:23
  16.7 3.9 %collective-permute-start.4 = (bf16[32,512]{1,0:T(8,128)(2,1)S(1)}, bf16[32,512]{1,0:T(8,128)(2,1)S(1)}, u32[]{:S(2)}, u32[]{:S(2)}) collective-permute-start(bf16[32,512]{1,0:T(8,128)(2,1)S(1)} %shard_map.38), channel_id=1, source_target_pairs={{4,0},{5,1},{6,2},{7,3},{0,4},{1,5},{2,6},{3,7},{12,8},{13,9},{14,... | collective-permute-start | bytes 98312 | tf_op jit(solution)/shard_map/ppermute | solution.py:23
  20.7 6.1 %collective-permute-start.7 = (bf16[4,32,512]{2,1,0:T(8,128)(2,1)S(1)}, bf16[4,32,512]{2,1,0:T(8,128)(2,1)S(1)}, u32[]{:S(2)}, u32[]{:S(2)}) collective-permute-start(bf16[4,32,512]{2,1,0:T(8,128)(2,1)S(1)} %pad_maximum_fusion.after.own), channel_id=1, source_target_pairs={{16,0},{17,1},{18,2},{19,3},{20,4},{21,5},{22,6},{23,7},{24,8},{25... | collective-permute-start | bytes 393224 | tf_op jit(solution)/shard_map/ppermute | solution.py:23
  22.4 6.4 %collective-permute-start.12 = (bf16[4,32,512]{2,1,0:T(8,128)(2,1)S(1)}, bf16[4,32,512]{2,1,0:T(8,128)(2,1)S(1)}, u32[]{:S(2)}, u32[]{:S(2)}) collective-permute-start(bf16[4,32,512]{2,1,0:T(8,128)(2,1)S(1)} %pad_maximum_fusion.after.own), channel_id=1, source_target_pairs={{2,0},{3,1},{0,2},{1,3},{6,4},{7,5},{4,6},{5,7},{10,8},{11,9},{8,1... | collective-permute-start | bytes 393224 | tf_op jit(solution)/shard_map/ppermute | solution.py:23
  23.9 6.1 %collective-permute-start.10 = (bf16[4,32,512]{2,1,0:T(8,128)(2,1)S(1)}, bf16[4,32,512]{2,1,0:T(8,128)(2,1)S(1)}, u32[]{:S(2)}, u32[]{:S(2)}) collective-permute-start(bf16[4,32,512]{2,1,0:T(8,128)(2,1)S(1)} %pad_maximum_fusion.after.own), channel_id=1, source_target_pairs={{18,0},{19,1},{16,2},{17,3},{22,4},{23,5},{20,6},{21,7},{26,8},{27... | collective-permute-start | bytes 393224 | tf_op jit(solution)/shard_map/ppermute | solution.py:23
  24.2 5.8 %collective-permute-start.8 = (bf16[4,32,512]{2,1,0:T(8,128)(2,1)S(1)}, bf16[4,32,512]{2,1,0:T(8,128)(2,1)S(1)}, u32[]{:S(2)}, u32[]{:S(2)}) collective-permute-start(bf16[4,32,512]{2,1,0:T(8,128)(2,1)S(1)} %pad_maximum_fusion.after.own), channel_id=1, source_target_pairs={{1,0},{0,1},{3,2},{2,3},{5,4},{4,5},{7,6},{6,7},{9,8},{8,9},{11,10... | collective-permute-start | bytes 393224 | tf_op jit(solution)/shard_map/ppermute | solution.py:23
  26.8 3.3 %collective-permute-start.9 = (bf16[4,32,512]{2,1,0:T(8,128)(2,1)S(1)}, bf16[4,32,512]{2,1,0:T(8,128)(2,1)S(1)}, u32[]{:S(2)}, u32[]{:S(2)}) collective-permute-start(bf16[4,32,512]{2,1,0:T(8,128)(2,1)S(1)} %collective-permute-done.7.across), channel_id=1, source_target_pairs={{1,0},{0,1},{3,2},{2,3},{5,4},{4,5},{7,6},{6,7},{9,8},{8,9},{11,10... | collective-permute-start | bytes 393224 | tf_op jit(solution)/shard_map/ppermute | solution.py:23
  28.8 2.7 %collective-permute-start.13 = (bf16[4,32,512]{2,1,0:T(8,128)(2,1)S(1)}, bf16[4,32,512]{2,1,0:T(8,128)(2,1)S(1)}, u32[]{:S(2)}, u32[]{:S(2)}) collective-permute-start(bf16[4,32,512]{2,1,0:T(8,128)(2,1)S(1)} %collective-permute-done.12.beside), channel_id=1, source_target_pairs={{1,0},{0,1},{3,2},{2,3},{5,4},{4,5},{7,6},{6,7},{9,8},{8,9},{11,10... | collective-permute-start | bytes 393224 | tf_op jit(solution)/shard_map/ppermute | solution.py:23
  30.0 1.5 %collective-permute-start.11 = (bf16[4,32,512]{2,1,0:T(8,128)(2,1)S(1)}, bf16[4,32,512]{2,1,0:T(8,128)(2,1)S(1)}, u32[]{:S(2)}, u32[]{:S(2)}) collective-permute-start(bf16[4,32,512]{2,1,0:T(8,128)(2,1)S(1)} %collective-permute-done.10.diagonal), channel_id=1, source_target_pairs={{1,0},{0,1},{3,2},{2,3},{5,4},{4,5},{7,6},{6,7},{9,8},{8,9},{11,10... | collective-permute-start | bytes 393224 | tf_op jit(solution)/shard_map/ppermute | solution.py:23

commit v6 on v5

--- a/solution.py
+++ b/solution.py
@@ -155,10 +155,12 @@
         ready,
         z,
     )
-    count, rows = upper.shape[0], 256
+    count = upper.shape[0]
     copies = []
     for half, (docs, scale) in enumerate(((upper, upper_scale), (lower, lower_scale))):
-        for at in range(0, count, rows):
+        cuts = (0, 2, 4) if half == 0 else (0, 2, 3, 4)
+        for low, high in zip(cuts, cuts[1:]):
+            at, rows = low * count // 4, (high - low) * count // 4
             here = half * count + at
             got = product(docs, at, rows, 1 - x, ready)
             made[here : here + rows] = (near[here : here + rows] + got) * scale[at : at + rows]

time: 34 us -> 34 us (level)
  no operation moved by 1% of the time
where the time goes in v6:
time: 34 us; the launch traced here: 33.8 us
  starting transfers between devices  15.6 us (46%)
  Pallas kernels  9.47 us (28%)
  waiting for transfers between devices  7.79 us (23%)
  local copies, waits for them, and re-layouts  0.85 us (2%)
    ppermute x14, starting transfers between devices, moved(): return lax.ppermute(array, AXES, pairs)  15.6 us
    pallas_call x5, Pallas kernels, call(): pl.pallas_call(kernel, out_shape=outs, in_specs=specs, out_specs=out_spec...  9.47 us
    ppermute x14, waiting for transfers between devices, moved(): return lax.ppermute(array, AXES, pairs)  7.79 us
    unnamed x1, local copies, waits for them, and re-layouts  0.84 us
  transfers between devices with their start and end apart: 14, of which 7 were waited for; matrix products, arithmetic and copies ran while one was open for 3% of the time, Pallas kernels for 20%

profile of v6, /device:TPU:0, one launch (start us, length us, event | category | flops | bytes accessed | tf_op | source)
XLA Modules:
  0.0 33.8 jit_solution(10805523501944705781)
XLA Ops:
  0.0 0.5 %collective-permute-start.1 = (bf16[8,4096]{1,0:T(8,128)(2,1)}, bf16[8,4096]{1,0:T(8,128)(2,1)S(1)}, u32[]{:S(2)}, u32[]{:S(2)}) collective-permute-start(bf16[8,4096]{1,0:T(8,128)(2,1)} %param.4), channel_id=1, source_target_pairs={{1,0},{0,1},{3,2},{2,3},{5,4},{4,5},{7,6},{6,7},{9,8},{8,9},{11,10... | collective-permute-start | bytes 196616 | tf_op jit(solution)/shard_map/ppermute | solution.py:23
  0.5 0.1 collective-permute-start
  0.5 0.8 %constant_dynamic-update-slice_fusion.1 = bf16[16,4096]{1,0:T(8,128)(2,1)S(1)} fusion(bf16[8,4096]{1,0:T(8,128)(2,1)} %param.4), kind=kLoop, calls=%fused_computation.2 | loop fusion | bytes 131072
  1.4 0.2 collective-permute-done.1
  1.6 5.9 %collective-permute-start.3 = (bf16[16,4096]{1,0:T(8,128)(2,1)S(1)}, bf16[16,4096]{1,0:T(8,128)(2,1)S(1)}, u32[]{:S(2)}, u32[]{:S(2)}) collective-permute-start(bf16[16,4096]{1,0:T(8,128)(2,1)S(1)} %constant_dynamic-update-slice_fusion), channel_id=1, source_target_pairs={{14,0},{9,1},{12,2},{11,3},{10,4},{13,5},{8,6},{15,7},{6,8},{1,9},... | collective-permute-start | bytes 393224 | tf_op jit(solution)/shard_map/ppermute | solution.py:23
  7.4 0.7 %collective-permute-start.2 = (bf16[16,4096]{1,0:T(8,128)(2,1)S(1)}, bf16[16,4096]{1,0:T(8,128)(2,1)S(1)}, u32[]{:S(2)}, u32[]{:S(2)}) collective-permute-start(bf16[16,4096]{1,0:T(8,128)(2,1)S(1)} %constant_dynamic-update-slice_fusion), channel_id=1, source_target_pairs={{0,0},{7,1},{2,2},{5,3},{4,4},{3,5},{6,6},{1,7},{8,8},{15,9},{10,1... | collective-permute-start | bytes 393224 | tf_op jit(solution)/shard_map/ppermute | solution.py:23
  8.1 0.0 collective-permute-done.after.other
  8.1 2.7 %shard_map.37 = (bf16[512,4096]{1,0:T(8,128)(2,1)S(1)}, f32[512,128]{1,0:T(8,128)S(1)}, bf16[4,64,1024]{2,1,0:T(8,128)(2,1)S(1)}) custom-call(bf16[1024,4096]{1,0:T(8,128)(2,1)} %docs.3, bf16[4,64,1024]{2,1,0:T(8,128)(2,1)} %own.1, bf16[4,64,1024]{2,1,0:T(8,128)(2,1)S(1)} %collective-permute-done.after.other), custom_call_target="tpu_custom_call" | custom-call | flops 4194304 | bytes 4194304 | tf_op jit(solution)/shard_map/pallas_call | solution.py:182
  10.8 1.0 %collective-permute-done.3.asked1 = bf16[16,4096]{1,0:T(8,128)(2,1)S(1)} collective-permute-done((bf16[16,4096]{1,0:T(8,128)(2,1)S(1)}, bf16[16,4096]{1,0:T(8,128)(2,1)S(1)}, u32[]{:S(2)}, u32[]{:S(2)}) %collective-permute-start.3) | collective-permute-done | bytes 131104 | tf_op jit(solution)/shard_map/ppermute | solution.py:23
  11.8 0.0 collective-permute-done.2.asked0
  11.8 0.5 %shard_map.38 = bf16[32,512]{1,0:T(8,128)(2,1)S(1)} custom-call(bf16[16,4096]{1,0:T(8,128)(2,1)S(1)} %collective-permute-done.2.asked0, bf16[16,4096]{1,0:T(8,128)(2,1)S(1)} %collective-permute-done.3.asked1, bf16[4,64,1024]{2,1,0:T(8,128)(2,1)S(1)} %get-tuple-element.13.own, bf16[4,64,1024]{2,1,0:T(8,128)(2,1)S(1)} %collective-permute-done.after.other), custom_call_target="tpu_custom_call" | custom-call | flops 33554432 | bytes 1048576 | tf_op jit(solution)/shard_map/pallas_call | solution.py:182
  12.3 2.6 %collective-permute-start.6 = (bf16[32,512]{1,0:T(8,128)(2,1)S(1)}, bf16[32,512]{1,0:T(8,128)(2,1)S(1)}, u32[]{:S(2)}, u32[]{:S(2)}) collective-permute-start(bf16[32,512]{1,0:T(8,128)(2,1)S(1)} %shard_map.38), channel_id=1, source_target_pairs={{12,0},{13,1},{14,2},{15,3},{8,4},{9,5},{10,6},{11,7},{4,8},{5,9},... | collective-permute-start | bytes 98312 | tf_op jit(solution)/shard_map/ppermute | solution.py:23
  14.9 1.9 %collective-permute-start.5 = (bf16[32,512]{1,0:T(8,128)(2,1)S(1)}, bf16[32,512]{1,0:T(8,128)(2,1)S(1)}, u32[]{:S(2)}, u32[]{:S(2)}) collective-permute-start(bf16[32,512]{1,0:T(8,128)(2,1)S(1)} %shard_map.38), channel_id=1, source_target_pairs={{8,0},{9,1},{10,2},{11,3},{12,4},{13,5},{14,6},{15,7},{0,8},{1,9},... | collective-permute-start | bytes 98312 | tf_op jit(solution)/shard_map/ppermute | solution.py:23
  16.7 0.0 collective-permute-start.4
  16.7 1.5 %collective-permute-done.6 = bf16[32,512]{1,0:T(8,128)(2,1)S(1)} collective-permute-done((bf16[32,512]{1,0:T(8,128)(2,1)S(1)}, bf16[32,512]{1,0:T(8,128)(2,1)S(1)}, u32[]{:S(2)}, u32[]{:S(2)}) %collective-permute-start.6) | collective-permute-done | bytes 32800 | tf_op jit(solution)/shard_map/ppermute | solution.py:23
  18.2 1.6 %collective-permute-done.5 = bf16[32,512]{1,0:T(8,128)(2,1)S(1)} collective-permute-done((bf16[32,512]{1,0:T(8,128)(2,1)S(1)}, bf16[32,512]{1,0:T(8,128)(2,1)S(1)}, u32[]{:S(2)}, u32[]{:S(2)}) %collective-permute-start.5) | collective-permute-done | bytes 32800 | tf_op jit(solution)/shard_map/ppermute | solution.py:23
  19.9 0.8 %collective-permute-done.4 = bf16[32,512]{1,0:T(8,128)(2,1)S(1)} collective-permute-done((bf16[32,512]{1,0:T(8,128)(2,1)S(1)}, bf16[32,512]{1,0:T(8,128)(2,1)S(1)}, u32[]{:S(2)}, u32[]{:S(2)}) %collective-permute-start.4) | collective-permute-done | bytes 32800 | tf_op jit(solution)/shard_map/ppermute | solution.py:23
  20.7 1.7 %collective-permute-start.7 = (bf16[4,32,512]{2,1,0:T(8,128)(2,1)S(1)}, bf16[4,32,512]{2,1,0:T(8,128)(2,1)S(1)}, u32[]{:S(2)}, u32[]{:S(2)}) collective-permute-start(bf16[4,32,512]{2,1,0:T(8,128)(2,1)S(1)} %pad_maximum_fusion.after.own), channel_id=1, source_target_pairs={{16,0},{17,1},{18,2},{19,3},{20,4},{21,5},{22,6},{23,7},{24,8},{25... | collective-permute-start | bytes 393224 | tf_op jit(solution)/shard_map/ppermute | solution.py:23
  22.4 1.5 %collective-permute-start.12 = (bf16[4,32,512]{2,1,0:T(8,128)(2,1)S(1)}, bf16[4,32,512]{2,1,0:T(8,128)(2,1)S(1)}, u32[]{:S(2)}, u32[]{:S(2)}) collective-permute-start(bf16[4,32,512]{2,1,0:T(8,128)(2,1)S(1)} %pad_maximum_fusion.after.own), channel_id=1, source_target_pairs={{2,0},{3,1},{0,2},{1,3},{6,4},{7,5},{4,6},{5,7},{10,8},{11,9},{8,1... | collective-permute-start | bytes 393224 | tf_op jit(solution)/shard_map/ppermute | solution.py:23
  23.9 0.3 collective-permute-start.10
  24.2 0.0 collective-permute-start.8
  24.2 2.5 %shard_map.39 = (bf16[512,4096]{1,0:T(8,128)(2,1)S(1)}, f32[512,128]{1,0:T(8,128)S(1)}) custom-call(bf16[1024,4096]{1,0:T(8,128)(2,1)} %docs.3, bf16[4,32,512]{2,1,0:T(8,128)(2,1)S(1)} %pad_maximum_fusion.after.own), custom_call_target="tpu_custom_call" | custom-call | flops 4194304 | bytes 4194304 | tf_op jit(solution)/shard_map/pallas_call | solution.py:182
  26.7 0.0 collective-permute-done.7.across
  26.8 0.6 %collective-permute-start.9 = (bf16[4,32,512]{2,1,0:T(8,128)(2,1)S(1)}, bf16[4,32,512]{2,1,0:T(8,128)(2,1)S(1)}, u32[]{:S(2)}, u32[]{:S(2)}) collective-permute-start(bf16[4,32,512]{2,1,0:T(8,128)(2,1)S(1)} %collective-permute-done.7.across), channel_id=1, source_target_pairs={{1,0},{0,1},{3,2},{2,3},{5,4},{4,5},{7,6},{6,7},{9,8},{8,9},{11,10... | collective-permute-start | bytes 393224 | tf_op jit(solution)/shard_map/ppermute | solution.py:23
  27.3 1.5 %collective-permute-done.12.beside = bf16[4,32,512]{2,1,0:T(8,128)(2,1)S(1)} collective-permute-done((bf16[4,32,512]{2,1,0:T(8,128)(2,1)S(1)}, bf16[4,32,512]{2,1,0:T(8,128)(2,1)S(1)}, u32[]{:S(2)}, u32[]{:S(2)}) %collective-permute-start.12) | collective-permute-done | bytes 131104 | tf_op jit(solution)/shard_map/ppermute | solution.py:23
  28.8 0.0 collective-permute-start.13
  28.8 1.2 %collective-permute-done.10.diagonal = bf16[4,32,512]{2,1,0:T(8,128)(2,1)S(1)} collective-permute-done((bf16[4,32,512]{2,1,0:T(8,128)(2,1)S(1)}, bf16[4,32,512]{2,1,0:T(8,128)(2,1)S(1)}, u32[]{:S(2)}, u32[]{:S(2)}) %collective-permute-start.10) | collective-permute-done | bytes 131104 | tf_op jit(solution)/shard_map/ppermute | solution.py:23
  30.0 0.0 collective-permute-start.11
  30.0 0.0 collective-permute-done.8.own_c
  30.0 0.0 collective-permute-done.9.across_c
  30.0 1.4 %shard_map.40.near = f32[1024,128]{1,0:T(8,128)S(1)} custom-call(bf16[512,4096]{1,0:T(8,128)(2,1)S(1)} %get-tuple-element.12.upper, bf16[512,4096]{1,0:T(8,128)(2,1)S(1)} %get-tuple-element.14.lower, bf16[4,32,512]{2,1,0:T(8,128)(2,1)S(1)} %pad_maximum_fusion.after.own, bf16[4,32,512]{2,1,0:T(8,128)(2,1)S(1)} %collective-permute-done.8.own_c, ...), custom_call_target="tpu_custom_call" | custom-call | flops 536870912 | bytes 4194304 | tf_op jit(solution)/shard_map/pallas_call | solution.py:182
  31.5 0.0 collective-permute-done.13.beside_c
  31.5 0.0 collective-permute-done.11.diagonal_c
  31.5 2.3 %shard_map.41 = f32[1024,128]{1,0:T(8,128)} custom-call(bf16[512,4096]{1,0:T(8,128)(2,1)S(1)} %get-tuple-element.12.upper, bf16[512,4096]{1,0:T(8,128)(2,1)S(1)} %get-tuple-element.14.lower, f32[512,128]{1,0:T(8,128)S(1)} %get-tuple-element.15.upper_scale, f32[512,128]{1,0:T(8,128)S(1)} %get-tuple-element.17.lower_scale, f32[1024,128]{1,0:T(8,128)S(1)} %shard_map.40.near, ...), custom_call_target="tpu_custom_call" | custom-call | flops 536870912 | bytes 4194304 | tf_op jit(solution)/shard_map/pallas_call | solution.py:182
  (2 shorter events, 0.0 us)
Async XLA Ops:
  0.0 1.6 %collective-permute-start.1 = (bf16[8,4096]{1,0:T(8,128)(2,1)}, bf16[8,4096]{1,0:T(8,128)(2,1)S(1)}, u32[]{:S(2)}, u32[]{:S(2)}) collective-permute-start(bf16[8,4096]{1,0:T(8,128)(2,1)} %param.4), channel_id=1, source_target_pairs={{1,0},{0,1},{3,2},{2,3},{5,4},{4,5},{7,6},{6,7},{9,8},{8,9},{11,10... | collective-permute-start | bytes 196616 | tf_op jit(solution)/shard_map/ppermute | solution.py:23
  0.5 7.7 %collective-permute-start = (bf16[4,64,1024]{2,1,0:T(8,128)(2,1)}, bf16[4,64,1024]{2,1,0:T(8,128)(2,1)S(1)}, u32[]{:S(2)}, u32[]{:S(2)}) collective-permute-start(bf16[4,64,1024]{2,1,0:T(8,128)(2,1)} %own.1), channel_id=1, source_target_pairs={{1,0},{0,1},{3,2},{2,3},{5,4},{4,5},{7,6},{6,7},{9,8},{8,9},{11,10... | collective-permute-start | bytes 1572872 | tf_op jit(solution)/shard_map/ppermute | solution.py:23
  1.6 10.2 %collective-permute-start.3 = (bf16[16,4096]{1,0:T(8,128)(2,1)S(1)}, bf16[16,4096]{1,0:T(8,128)(2,1)S(1)}, u32[]{:S(2)}, u32[]{:S(2)}) collective-permute-start(bf16[16,4096]{1,0:T(8,128)(2,1)S(1)} %constant_dynamic-update-slice_fusion), channel_id=1, source_target_pairs={{14,0},{9,1},{12,2},{11,3},{10,4},{13,5},{8,6},{15,7},{6,8},{1,9},... | collective-permute-start | bytes 393224 | tf_op jit(solution)/shard_map/ppermute | solution.py:23
  7.4 4.3 %collective-permute-start.2 = (bf16[16,4096]{1,0:T(8,128)(2,1)S(1)}, bf16[16,4096]{1,0:T(8,128)(2,1)S(1)}, u32[]{:S(2)}, u32[]{:S(2)}) collective-permute-start(bf16[16,4096]{1,0:T(8,128)(2,1)S(1)} %constant_dynamic-update-slice_fusion), channel_id=1, source_target_pairs={{0,0},{7,1},{2,2},{5,3},{4,4},{3,5},{6,6},{1,7},{8,8},{15,9},{10,1... | collective-permute-start | bytes 393224 | tf_op jit(solution)/shard_map/ppermute | solution.py:23
  12.3 5.9 %collective-permute-start.6 = (bf16[32,512]{1,0:T(8,128)(2,1)S(1)}, bf16[32,512]{1,0:T(8,128)(2,1)S(1)}, u32[]{:S(2)}, u32[]{:S(2)}) collective-permute-start(bf16[32,512]{1,0:T(8,128)(2,1)S(1)} %shard_map.38), channel_id=1, source_target_pairs={{12,0},{13,1},{14,2},{15,3},{8,4},{9,5},{10,6},{11,7},{4,8},{5,9},... | collective-permute-start | bytes 98312 | tf_op jit(solution)/shard_map/ppermute | solution.py:23
  14.9 5.0 %collective-permute-start.5 = (bf16[32,512]{1,0:T(8,128)(2,1)S(1)}, bf16[32,512]{1,0:T(8,128)(2,1)S(1)}, u32[]{:S(2)}, u32[]{:S(2)}) collective-permute-start(bf16[32,512]{1,0:T(8,128)(2,1)S(1)} %shard_map.38), channel_id=1, source_target_pairs={{8,0},{9,1},{10,2},{11,3},{12,4},{13,5},{14,6},{15,7},{0,8},{1,9},... | collective-permute-start | bytes 98312 | tf_op jit(solution)/shard_map/ppermute | solution.py:23
  16.7 3.9 %collective-permute-start.4 = (bf16[32,512]{1,0:T(8,128)(2,1)S(1)}, bf16[32,512]{1,0:T(8,128)(2,1)S(1)}, u32[]{:S(2)}, u32[]{:S(2)}) collective-permute-start(bf16[32,512]{1,0:T(8,128)(2,1)S(1)} %shard_map.38), channel_id=1, source_target_pairs={{4,0},{5,1},{6,2},{7,3},{0,4},{1,5},{2,6},{3,7},{12,8},{13,9},{14,... | collective-permute-start | bytes 98312 | tf_op jit(solution)/shard_map/ppermute | solution.py:23
  20.7 6.1 %collective-permute-start.7 = (bf16[4,32,512]{2,1,0:T(8,128)(2,1)S(1)}, bf16[4,32,512]{2,1,0:T(8,128)(2,1)S(1)}, u32[]{:S(2)}, u32[]{:S(2)}) collective-permute-start(bf16[4,32,512]{2,1,0:T(8,128)(2,1)S(1)} %pad_maximum_fusion.after.own), channel_id=1, source_target_pairs={{16,0},{17,1},{18,2},{19,3},{20,4},{21,5},{22,6},{23,7},{24,8},{25... | collective-permute-start | bytes 393224 | tf_op jit(solution)/shard_map/ppermute | solution.py:23
  22.4 6.4 %collective-permute-start.12 = (bf16[4,32,512]{2,1,0:T(8,128)(2,1)S(1)}, bf16[4,32,512]{2,1,0:T(8,128)(2,1)S(1)}, u32[]{:S(2)}, u32[]{:S(2)}) collective-permute-start(bf16[4,32,512]{2,1,0:T(8,128)(2,1)S(1)} %pad_maximum_fusion.after.own), channel_id=1, source_target_pairs={{2,0},{3,1},{0,2},{1,3},{6,4},{7,5},{4,6},{5,7},{10,8},{11,9},{8,1... | collective-permute-start | bytes 393224 | tf_op jit(solution)/shard_map/ppermute | solution.py:23
  23.9 6.1 %collective-permute-start.10 = (bf16[4,32,512]{2,1,0:T(8,128)(2,1)S(1)}, bf16[4,32,512]{2,1,0:T(8,128)(2,1)S(1)}, u32[]{:S(2)}, u32[]{:S(2)}) collective-permute-start(bf16[4,32,512]{2,1,0:T(8,128)(2,1)S(1)} %pad_maximum_fusion.after.own), channel_id=1, source_target_pairs={{18,0},{19,1},{16,2},{17,3},{22,4},{23,5},{20,6},{21,7},{26,8},{27... | collective-permute-start | bytes 393224 | tf_op jit(solution)/shard_map/ppermute | solution.py:23
  24.2 5.8 %collective-permute-start.8 = (bf16[4,32,512]{2,1,0:T(8,128)(2,1)S(1)}, bf16[4,32,512]{2,1,0:T(8,128)(2,1)S(1)}, u32[]{:S(2)}, u32[]{:S(2)}) collective-permute-start(bf16[4,32,512]{2,1,0:T(8,128)(2,1)S(1)} %pad_maximum_fusion.after.own), channel_id=1, source_target_pairs={{1,0},{0,1},{3,2},{2,3},{5,4},{4,5},{7,6},{6,7},{9,8},{8,9},{11,10... | collective-permute-start | bytes 393224 | tf_op jit(solution)/shard_map/ppermute | solution.py:23
  26.8 3.3 %collective-permute-start.9 = (bf16[4,32,512]{2,1,0:T(8,128)(2,1)S(1)}, bf16[4,32,512]{2,1,0:T(8,128)(2,1)S(1)}, u32[]{:S(2)}, u32[]{:S(2)}) collective-permute-start(bf16[4,32,512]{2,1,0:T(8,128)(2,1)S(1)} %collective-permute-done.7.across), channel_id=1, source_target_pairs={{1,0},{0,1},{3,2},{2,3},{5,4},{4,5},{7,6},{6,7},{9,8},{8,9},{11,10... | collective-permute-start | bytes 393224 | tf_op jit(solution)/shard_map/ppermute | solution.py:23
  28.8 2.7 %collective-permute-start.13 = (bf16[4,32,512]{2,1,0:T(8,128)(2,1)S(1)}, bf16[4,32,512]{2,1,0:T(8,128)(2,1)S(1)}, u32[]{:S(2)}, u32[]{:S(2)}) collective-permute-start(bf16[4,32,512]{2,1,0:T(8,128)(2,1)S(1)} %collective-permute-done.12.beside), channel_id=1, source_target_pairs={{1,0},{0,1},{3,2},{2,3},{5,4},{4,5},{7,6},{6,7},{9,8},{8,9},{11,10... | collective-permute-start | bytes 393224 | tf_op jit(solution)/shard_map/ppermute | solution.py:23
  30.0 1.5 %collective-permute-start.11 = (bf16[4,32,512]{2,1,0:T(8,128)(2,1)S(1)}, bf16[4,32,512]{2,1,0:T(8,128)(2,1)S(1)}, u32[]{:S(2)}, u32[]{:S(2)}) collective-permute-start(bf16[4,32,512]{2,1,0:T(8,128)(2,1)S(1)} %collective-permute-done.10.diagonal), channel_id=1, source_target_pairs={{1,0},{0,1},{3,2},{2,3},{5,4},{4,5},{7,6},{6,7},{9,8},{8,9},{11,10... | collective-permute-start | bytes 393224 | tf_op jit(solution)/shard_map/ppermute | solution.py:23

commit v7 on v5

--- a/solution.py
+++ b/solution.py
@@ -123,7 +123,7 @@
         ready,
         z,
     )
-    count, rows = upper.shape[0], 256
+    count, rows = upper.shape[0], 512
     for half, docs in enumerate((upper, lower)):
         for at in range(0, count, rows):
             out[half * count + at : half * count + at + rows] = product(docs, at, rows, x, ready)

time: 34 us -> 34 us (level)
  no operation moved by 1% of the time
where the time goes in v7:
time: 34 us; the launch traced here: 33.8 us
  starting transfers between devices  15.6 us (46%)
  Pallas kernels  9.44 us (28%)
  waiting for transfers between devices  7.79 us (23%)
  local copies, waits for them, and re-layouts  0.85 us (2%)
    ppermute x14, starting transfers between devices, moved(): return lax.ppermute(array, AXES, pairs)  15.6 us
    pallas_call x5, Pallas kernels, call(): pl.pallas_call(kernel, out_shape=outs, in_specs=specs, out_specs=out_spec...  9.44 us
    ppermute x14, waiting for transfers between devices, moved(): return lax.ppermute(array, AXES, pairs)  7.79 us
    unnamed x1, local copies, waits for them, and re-layouts  0.84 us
  transfers between devices with their start and end apart: 14, of which 7 were waited for; matrix products, arithmetic and copies ran while one was open for 3% of the time, Pallas kernels for 20%

profile of v7, /device:TPU:0, one launch (start us, length us, event | category | flops | bytes accessed | tf_op | source)
XLA Modules:
  0.0 33.8 jit_solution(14508605963567344613)
XLA Ops:
  0.0 0.5 %collective-permute-start.1 = (bf16[8,4096]{1,0:T(8,128)(2,1)}, bf16[8,4096]{1,0:T(8,128)(2,1)S(1)}, u32[]{:S(2)}, u32[]{:S(2)}) collective-permute-start(bf16[8,4096]{1,0:T(8,128)(2,1)} %param.4), channel_id=1, source_target_pairs={{1,0},{0,1},{3,2},{2,3},{5,4},{4,5},{7,6},{6,7},{9,8},{8,9},{11,10... | collective-permute-start | bytes 196616 | tf_op jit(solution)/shard_map/ppermute | solution.py:23
  0.5 0.1 collective-permute-start
  0.5 0.8 %constant_dynamic-update-slice_fusion.1 = bf16[16,4096]{1,0:T(8,128)(2,1)S(1)} fusion(bf16[8,4096]{1,0:T(8,128)(2,1)} %param.4), kind=kLoop, calls=%fused_computation.2 | loop fusion | bytes 131072
  1.4 0.2 collective-permute-done.1
  1.6 5.9 %collective-permute-start.3 = (bf16[16,4096]{1,0:T(8,128)(2,1)S(1)}, bf16[16,4096]{1,0:T(8,128)(2,1)S(1)}, u32[]{:S(2)}, u32[]{:S(2)}) collective-permute-start(bf16[16,4096]{1,0:T(8,128)(2,1)S(1)} %constant_dynamic-update-slice_fusion), channel_id=1, source_target_pairs={{14,0},{9,1},{12,2},{11,3},{10,4},{13,5},{8,6},{15,7},{6,8},{1,9},... | collective-permute-start | bytes 393224 | tf_op jit(solution)/shard_map/ppermute | solution.py:23
  7.4 0.7 %collective-permute-start.2 = (bf16[16,4096]{1,0:T(8,128)(2,1)S(1)}, bf16[16,4096]{1,0:T(8,128)(2,1)S(1)}, u32[]{:S(2)}, u32[]{:S(2)}) collective-permute-start(bf16[16,4096]{1,0:T(8,128)(2,1)S(1)} %constant_dynamic-update-slice_fusion), channel_id=1, source_target_pairs={{0,0},{7,1},{2,2},{5,3},{4,4},{3,5},{6,6},{1,7},{8,8},{15,9},{10,1... | collective-permute-start | bytes 393224 | tf_op jit(solution)/shard_map/ppermute | solution.py:23
  8.1 0.0 collective-permute-done.after.other
  8.1 2.7 %shard_map.37 = (bf16[512,4096]{1,0:T(8,128)(2,1)S(1)}, f32[512,128]{1,0:T(8,128)S(1)}, bf16[4,64,1024]{2,1,0:T(8,128)(2,1)S(1)}) custom-call(bf16[1024,4096]{1,0:T(8,128)(2,1)} %docs.3, bf16[4,64,1024]{2,1,0:T(8,128)(2,1)} %own.1, bf16[4,64,1024]{2,1,0:T(8,128)(2,1)S(1)} %collective-permute-done.after.other), custom_call_target="tpu_custom_call" | custom-call | flops 4194304 | bytes 4194304 | tf_op jit(solution)/shard_map/pallas_call | solution.py:180
  10.8 1.0 %collective-permute-done.3.asked1 = bf16[16,4096]{1,0:T(8,128)(2,1)S(1)} collective-permute-done((bf16[16,4096]{1,0:T(8,128)(2,1)S(1)}, bf16[16,4096]{1,0:T(8,128)(2,1)S(1)}, u32[]{:S(2)}, u32[]{:S(2)}) %collective-permute-start.3) | collective-permute-done | bytes 131104 | tf_op jit(solution)/shard_map/ppermute | solution.py:23
  11.8 0.0 collective-permute-done.2.asked0
  11.8 0.5 %shard_map.38 = bf16[32,512]{1,0:T(8,128)(2,1)S(1)} custom-call(bf16[16,4096]{1,0:T(8,128)(2,1)S(1)} %collective-permute-done.2.asked0, bf16[16,4096]{1,0:T(8,128)(2,1)S(1)} %collective-permute-done.3.asked1, bf16[4,64,1024]{2,1,0:T(8,128)(2,1)S(1)} %get-tuple-element.13.own, bf16[4,64,1024]{2,1,0:T(8,128)(2,1)S(1)} %collective-permute-done.after.other), custom_call_target="tpu_custom_call" | custom-call | flops 33554432 | bytes 1048576 | tf_op jit(solution)/shard_map/pallas_call | solution.py:180
  12.3 2.6 %collective-permute-start.6 = (bf16[32,512]{1,0:T(8,128)(2,1)S(1)}, bf16[32,512]{1,0:T(8,128)(2,1)S(1)}, u32[]{:S(2)}, u32[]{:S(2)}) collective-permute-start(bf16[32,512]{1,0:T(8,128)(2,1)S(1)} %shard_map.38), channel_id=1, source_target_pairs={{12,0},{13,1},{14,2},{15,3},{8,4},{9,5},{10,6},{11,7},{4,8},{5,9},... | collective-permute-start | bytes 98312 | tf_op jit(solution)/shard_map/ppermute | solution.py:23
  14.9 1.9 %collective-permute-start.5 = (bf16[32,512]{1,0:T(8,128)(2,1)S(1)}, bf16[32,512]{1,0:T(8,128)(2,1)S(1)}, u32[]{:S(2)}, u32[]{:S(2)}) collective-permute-start(bf16[32,512]{1,0:T(8,128)(2,1)S(1)} %shard_map.38), channel_id=1, source_target_pairs={{8,0},{9,1},{10,2},{11,3},{12,4},{13,5},{14,6},{15,7},{0,8},{1,9},... | collective-permute-start | bytes 98312 | tf_op jit(solution)/shard_map/ppermute | solution.py:23
  16.7 0.0 collective-permute-start.4
  16.7 1.5 %collective-permute-done.6 = bf16[32,512]{1,0:T(8,128)(2,1)S(1)} collective-permute-done((bf16[32,512]{1,0:T(8,128)(2,1)S(1)}, bf16[32,512]{1,0:T(8,128)(2,1)S(1)}, u32[]{:S(2)}, u32[]{:S(2)}) %collective-permute-start.6) | collective-permute-done | bytes 32800 | tf_op jit(solution)/shard_map/ppermute | solution.py:23
  18.2 1.6 %collective-permute-done.5 = bf16[32,512]{1,0:T(8,128)(2,1)S(1)} collective-permute-done((bf16[32,512]{1,0:T(8,128)(2,1)S(1)}, bf16[32,512]{1,0:T(8,128)(2,1)S(1)}, u32[]{:S(2)}, u32[]{:S(2)}) %collective-permute-start.5) | collective-permute-done | bytes 32800 | tf_op jit(solution)/shard_map/ppermute | solution.py:23
  19.9 0.8 %collective-permute-done.4 = bf16[32,512]{1,0:T(8,128)(2,1)S(1)} collective-permute-done((bf16[32,512]{1,0:T(8,128)(2,1)S(1)}, bf16[32,512]{1,0:T(8,128)(2,1)S(1)}, u32[]{:S(2)}, u32[]{:S(2)}) %collective-permute-start.4) | collective-permute-done | bytes 32800 | tf_op jit(solution)/shard_map/ppermute | solution.py:23
  20.7 1.7 %collective-permute-start.7 = (bf16[4,32,512]{2,1,0:T(8,128)(2,1)S(1)}, bf16[4,32,512]{2,1,0:T(8,128)(2,1)S(1)}, u32[]{:S(2)}, u32[]{:S(2)}) collective-permute-start(bf16[4,32,512]{2,1,0:T(8,128)(2,1)S(1)} %pad_maximum_fusion.after.own), channel_id=1, source_target_pairs={{16,0},{17,1},{18,2},{19,3},{20,4},{21,5},{22,6},{23,7},{24,8},{25... | collective-permute-start | bytes 393224 | tf_op jit(solution)/shard_map/ppermute | solution.py:23
  22.4 1.5 %collective-permute-start.12 = (bf16[4,32,512]{2,1,0:T(8,128)(2,1)S(1)}, bf16[4,32,512]{2,1,0:T(8,128)(2,1)S(1)}, u32[]{:S(2)}, u32[]{:S(2)}) collective-permute-start(bf16[4,32,512]{2,1,0:T(8,128)(2,1)S(1)} %pad_maximum_fusion.after.own), channel_id=1, source_target_pairs={{2,0},{3,1},{0,2},{1,3},{6,4},{7,5},{4,6},{5,7},{10,8},{11,9},{8,1... | collective-permute-start | bytes 393224 | tf_op jit(solution)/shard_map/ppermute | solution.py:23
  23.9 0.3 collective-permute-start.10
  24.2 0.0 collective-permute-start.8
  24.2 2.5 %shard_map.39 = (bf16[512,4096]{1,0:T(8,128)(2,1)S(1)}, f32[512,128]{1,0:T(8,128)S(1)}) custom-call(bf16[1024,4096]{1,0:T(8,128)(2,1)} %docs.3, bf16[4,32,512]{2,1,0:T(8,128)(2,1)S(1)} %pad_maximum_fusion.after.own), custom_call_target="tpu_custom_call" | custom-call | flops 4194304 | bytes 4194304 | tf_op jit(solution)/shard_map/pallas_call | solution.py:180
  26.7 0.0 collective-permute-done.7.across
  26.8 0.6 %collective-permute-start.9 = (bf16[4,32,512]{2,1,0:T(8,128)(2,1)S(1)}, bf16[4,32,512]{2,1,0:T(8,128)(2,1)S(1)}, u32[]{:S(2)}, u32[]{:S(2)}) collective-permute-start(bf16[4,32,512]{2,1,0:T(8,128)(2,1)S(1)} %collective-permute-done.7.across), channel_id=1, source_target_pairs={{1,0},{0,1},{3,2},{2,3},{5,4},{4,5},{7,6},{6,7},{9,8},{8,9},{11,10... | collective-permute-start | bytes 393224 | tf_op jit(solution)/shard_map/ppermute | solution.py:23
  27.3 1.5 %collective-permute-done.12.beside = bf16[4,32,512]{2,1,0:T(8,128)(2,1)S(1)} collective-permute-done((bf16[4,32,512]{2,1,0:T(8,128)(2,1)S(1)}, bf16[4,32,512]{2,1,0:T(8,128)(2,1)S(1)}, u32[]{:S(2)}, u32[]{:S(2)}) %collective-permute-start.12) | collective-permute-done | bytes 131104 | tf_op jit(solution)/shard_map/ppermute | solution.py:23
  28.8 0.0 collective-permute-start.13
  28.8 1.2 %collective-permute-done.10.diagonal = bf16[4,32,512]{2,1,0:T(8,128)(2,1)S(1)} collective-permute-done((bf16[4,32,512]{2,1,0:T(8,128)(2,1)S(1)}, bf16[4,32,512]{2,1,0:T(8,128)(2,1)S(1)}, u32[]{:S(2)}, u32[]{:S(2)}) %collective-permute-start.10) | collective-permute-done | bytes 131104 | tf_op jit(solution)/shard_map/ppermute | solution.py:23
  30.0 0.0 collective-permute-start.11
  30.0 0.0 collective-permute-done.8.own_c
  30.0 0.0 collective-permute-done.9.across_c
  30.0 1.4 %shard_map.40.near = f32[1024,128]{1,0:T(8,128)S(1)} custom-call(bf16[512,4096]{1,0:T(8,128)(2,1)S(1)} %get-tuple-element.12.upper, bf16[512,4096]{1,0:T(8,128)(2,1)S(1)} %get-tuple-element.14.lower, bf16[4,32,512]{2,1,0:T(8,128)(2,1)S(1)} %pad_maximum_fusion.after.own, bf16[4,32,512]{2,1,0:T(8,128)(2,1)S(1)} %collective-permute-done.8.own_c, ...), custom_call_target="tpu_custom_call" | custom-call | flops 536870912 | bytes 4194304 | tf_op jit(solution)/shard_map/pallas_call | solution.py:180
  31.5 0.0 collective-permute-done.13.beside_c
  31.5 0.0 collective-permute-done.11.diagonal_c
  31.5 2.3 %shard_map.41 = f32[1024,128]{1,0:T(8,128)} custom-call(bf16[512,4096]{1,0:T(8,128)(2,1)S(1)} %get-tuple-element.12.upper, bf16[512,4096]{1,0:T(8,128)(2,1)S(1)} %get-tuple-element.14.lower, f32[512,128]{1,0:T(8,128)S(1)} %get-tuple-element.15.upper_scale, f32[512,128]{1,0:T(8,128)S(1)} %get-tuple-element.17.lower_scale, f32[1024,128]{1,0:T(8,128)S(1)} %shard_map.40.near, ...), custom_call_target="tpu_custom_call" | custom-call | flops 536870912 | bytes 4194304 | tf_op jit(solution)/shard_map/pallas_call | solution.py:180
  (2 shorter events, 0.0 us)
Async XLA Ops:
  0.0 1.6 %collective-permute-start.1 = (bf16[8,4096]{1,0:T(8,128)(2,1)}, bf16[8,4096]{1,0:T(8,128)(2,1)S(1)}, u32[]{:S(2)}, u32[]{:S(2)}) collective-permute-start(bf16[8,4096]{1,0:T(8,128)(2,1)} %param.4), channel_id=1, source_target_pairs={{1,0},{0,1},{3,2},{2,3},{5,4},{4,5},{7,6},{6,7},{9,8},{8,9},{11,10... | collective-permute-start | bytes 196616 | tf_op jit(solution)/shard_map/ppermute | solution.py:23
  0.5 7.7 %collective-permute-start = (bf16[4,64,1024]{2,1,0:T(8,128)(2,1)}, bf16[4,64,1024]{2,1,0:T(8,128)(2,1)S(1)}, u32[]{:S(2)}, u32[]{:S(2)}) collective-permute-start(bf16[4,64,1024]{2,1,0:T(8,128)(2,1)} %own.1), channel_id=1, source_target_pairs={{1,0},{0,1},{3,2},{2,3},{5,4},{4,5},{7,6},{6,7},{9,8},{8,9},{11,10... | collective-permute-start | bytes 1572872 | tf_op jit(solution)/shard_map/ppermute | solution.py:23
  1.6 10.2 %collective-permute-start.3 = (bf16[16,4096]{1,0:T(8,128)(2,1)S(1)}, bf16[16,4096]{1,0:T(8,128)(2,1)S(1)}, u32[]{:S(2)}, u32[]{:S(2)}) collective-permute-start(bf16[16,4096]{1,0:T(8,128)(2,1)S(1)} %constant_dynamic-update-slice_fusion), channel_id=1, source_target_pairs={{14,0},{9,1},{12,2},{11,3},{10,4},{13,5},{8,6},{15,7},{6,8},{1,9},... | collective-permute-start | bytes 393224 | tf_op jit(solution)/shard_map/ppermute | solution.py:23
  7.4 4.3 %collective-permute-start.2 = (bf16[16,4096]{1,0:T(8,128)(2,1)S(1)}, bf16[16,4096]{1,0:T(8,128)(2,1)S(1)}, u32[]{:S(2)}, u32[]{:S(2)}) collective-permute-start(bf16[16,4096]{1,0:T(8,128)(2,1)S(1)} %constant_dynamic-update-slice_fusion), channel_id=1, source_target_pairs={{0,0},{7,1},{2,2},{5,3},{4,4},{3,5},{6,6},{1,7},{8,8},{15,9},{10,1... | collective-permute-start | bytes 393224 | tf_op jit(solution)/shard_map/ppermute | solution.py:23
  12.3 5.9 %collective-permute-start.6 = (bf16[32,512]{1,0:T(8,128)(2,1)S(1)}, bf16[32,512]{1,0:T(8,128)(2,1)S(1)}, u32[]{:S(2)}, u32[]{:S(2)}) collective-permute-start(bf16[32,512]{1,0:T(8,128)(2,1)S(1)} %shard_map.38), channel_id=1, source_target_pairs={{12,0},{13,1},{14,2},{15,3},{8,4},{9,5},{10,6},{11,7},{4,8},{5,9},... | collective-permute-start | bytes 98312 | tf_op jit(solution)/shard_map/ppermute | solution.py:23
  14.9 5.0 %collective-permute-start.5 = (bf16[32,512]{1,0:T(8,128)(2,1)S(1)}, bf16[32,512]{1,0:T(8,128)(2,1)S(1)}, u32[]{:S(2)}, u32[]{:S(2)}) collective-permute-start(bf16[32,512]{1,0:T(8,128)(2,1)S(1)} %shard_map.38), channel_id=1, source_target_pairs={{8,0},{9,1},{10,2},{11,3},{12,4},{13,5},{14,6},{15,7},{0,8},{1,9},... | collective-permute-start | bytes 98312 | tf_op jit(solution)/shard_map/ppermute | solution.py:23
  16.7 3.9 %collective-permute-start.4 = (bf16[32,512]{1,0:T(8,128)(2,1)S(1)}, bf16[32,512]{1,0:T(8,128)(2,1)S(1)}, u32[]{:S(2)}, u32[]{:S(2)}) collective-permute-start(bf16[32,512]{1,0:T(8,128)(2,1)S(1)} %shard_map.38), channel_id=1, source_target_pairs={{4,0},{5,1},{6,2},{7,3},{0,4},{1,5},{2,6},{3,7},{12,8},{13,9},{14,... | collective-permute-start | bytes 98312 | tf_op jit(solution)/shard_map/ppermute | solution.py:23
  20.7 6.1 %collective-permute-start.7 = (bf16[4,32,512]{2,1,0:T(8,128)(2,1)S(1)}, bf16[4,32,512]{2,1,0:T(8,128)(2,1)S(1)}, u32[]{:S(2)}, u32[]{:S(2)}) collective-permute-start(bf16[4,32,512]{2,1,0:T(8,128)(2,1)S(1)} %pad_maximum_fusion.after.own), channel_id=1, source_target_pairs={{16,0},{17,1},{18,2},{19,3},{20,4},{21,5},{22,6},{23,7},{24,8},{25... | collective-permute-start | bytes 393224 | tf_op jit(solution)/shard_map/ppermute | solution.py:23
  22.4 6.4 %collective-permute-start.12 = (bf16[4,32,512]{2,1,0:T(8,128)(2,1)S(1)}, bf16[4,32,512]{2,1,0:T(8,128)(2,1)S(1)}, u32[]{:S(2)}, u32[]{:S(2)}) collective-permute-start(bf16[4,32,512]{2,1,0:T(8,128)(2,1)S(1)} %pad_maximum_fusion.after.own), channel_id=1, source_target_pairs={{2,0},{3,1},{0,2},{1,3},{6,4},{7,5},{4,6},{5,7},{10,8},{11,9},{8,1... | collective-permute-start | bytes 393224 | tf_op jit(solution)/shard_map/ppermute | solution.py:23
  23.9 6.1 %collective-permute-start.10 = (bf16[4,32,512]{2,1,0:T(8,128)(2,1)S(1)}, bf16[4,32,512]{2,1,0:T(8,128)(2,1)S(1)}, u32[]{:S(2)}, u32[]{:S(2)}) collective-permute-start(bf16[4,32,512]{2,1,0:T(8,128)(2,1)S(1)} %pad_maximum_fusion.after.own), channel_id=1, source_target_pairs={{18,0},{19,1},{16,2},{17,3},{22,4},{23,5},{20,6},{21,7},{26,8},{27... | collective-permute-start | bytes 393224 | tf_op jit(solution)/shard_map/ppermute | solution.py:23
  24.2 5.8 %collective-permute-start.8 = (bf16[4,32,512]{2,1,0:T(8,128)(2,1)S(1)}, bf16[4,32,512]{2,1,0:T(8,128)(2,1)S(1)}, u32[]{:S(2)}, u32[]{:S(2)}) collective-permute-start(bf16[4,32,512]{2,1,0:T(8,128)(2,1)S(1)} %pad_maximum_fusion.after.own), channel_id=1, source_target_pairs={{1,0},{0,1},{3,2},{2,3},{5,4},{4,5},{7,6},{6,7},{9,8},{8,9},{11,10... | collective-permute-start | bytes 393224 | tf_op jit(solution)/shard_map/ppermute | solution.py:23
  26.8 3.3 %collective-permute-start.9 = (bf16[4,32,512]{2,1,0:T(8,128)(2,1)S(1)}, bf16[4,32,512]{2,1,0:T(8,128)(2,1)S(1)}, u32[]{:S(2)}, u32[]{:S(2)}) collective-permute-start(bf16[4,32,512]{2,1,0:T(8,128)(2,1)S(1)} %collective-permute-done.7.across), channel_id=1, source_target_pairs={{1,0},{0,1},{3,2},{2,3},{5,4},{4,5},{7,6},{6,7},{9,8},{8,9},{11,10... | collective-permute-start | bytes 393224 | tf_op jit(solution)/shard_map/ppermute | solution.py:23
  28.8 2.7 %collective-permute-start.13 = (bf16[4,32,512]{2,1,0:T(8,128)(2,1)S(1)}, bf16[4,32,512]{2,1,0:T(8,128)(2,1)S(1)}, u32[]{:S(2)}, u32[]{:S(2)}) collective-permute-start(bf16[4,32,512]{2,1,0:T(8,128)(2,1)S(1)} %collective-permute-done.12.beside), channel_id=1, source_target_pairs={{1,0},{0,1},{3,2},{2,3},{5,4},{4,5},{7,6},{6,7},{9,8},{8,9},{11,10... | collective-permute-start | bytes 393224 | tf_op jit(solution)/shard_map/ppermute | solution.py:23
  30.0 1.5 %collective-permute-start.11 = (bf16[4,32,512]{2,1,0:T(8,128)(2,1)S(1)}, bf16[4,32,512]{2,1,0:T(8,128)(2,1)S(1)}, u32[]{:S(2)}, u32[]{:S(2)}) collective-permute-start(bf16[4,32,512]{2,1,0:T(8,128)(2,1)S(1)} %collective-permute-done.10.diagonal), channel_id=1, source_target_pairs={{1,0},{0,1},{3,2},{2,3},{5,4},{4,5},{7,6},{6,7},{9,8},{8,9},{11,10... | collective-permute-start | bytes 393224 | tf_op jit(solution)/shard_map/ppermute | solution.py:23
